TPU v7x, 32 devices: a whole 2x2x4 slice. The times are simulated.
32 devices in a mesh: dp: 8 (over z, x), tensor: 4 (over y, core).
Axes of the slice: x: 2, y: 2, z: 4, core: 2. Of those that a mesh axis runs over, the one named last changes fastest.
Arguments:
- inputs: bfloat16 [24, 1024, 512], P('dp', 'tensor'), may hold values from -6 to 6
- cotangent: bfloat16 [24, 1024, 512], P('dp', 'tensor'), may hold values from -6 to 6
- mix_weight: bfloat16 [512, 1536], P(('dp', 'tensor')), may hold values from -0.25 to 0.25
- gate_weight: bfloat16 [512, 8], P(('dp', 'tensor')), may hold values from -0.25 to 0.25
- gate_bias: float32 [8], replicated, may hold values from 2.5 to 8
- out_weight: bfloat16 [512, 512], P(('dp', 'tensor')), may hold values from -1 to 1
- gain_first: bfloat16 [512], P(('dp', 'tensor')), may hold values from 0.5 to 1.5
- shift_first: bfloat16 [512], P(('dp', 'tensor')), may hold values from -2.5 to 2.5
- gain_second: bfloat16 [512], P(('dp', 'tensor')), may hold values from 0.5 to 1.5
- shift_second: bfloat16 [512], P(('dp', 'tensor')), may hold values from -2.5 to 2.5
- up_weight: bfloat16 [512, 2048], P('dp', 'tensor'), may hold values from -0.25 to 0.25
- down_weight: bfloat16 [2048, 512], P('tensor', 'dp'), may hold values from -0.125 to 0.125
- random_maps: bfloat16 [8, 64, 64], replicated, may hold values from -0.75 to 0.75
Outputs:
- output: bfloat16 [24, 1024, 512], P('dp', 'tensor')
- input_grad: float32 [24, 1024, 512], P('dp', 'tensor')
- mix_grad: float32 [512, 1536], P(('dp', 'tensor'))
- gate_grad: float32 [512, 8], P(('dp', 'tensor'))
- bias_grad: float32 [8], replicated
- out_grad: float32 [512, 512], P(('dp', 'tensor'))
- first_gain_grad: float32 [512], P(('dp', 'tensor'))
- first_shift_grad: float32 [512], P(('dp', 'tensor'))
- second_gain_grad: float32 [512], P(('dp', 'tensor'))
- second_shift_grad: float32 [512], P(('dp', 'tensor'))
- up_grad: float32 [512, 2048], P('dp', 'tensor')
- down_grad: float32 [2048, 512], P('tensor', 'dp')
All inputs are finite; a program needn't handle non-finite values.
Results may differ from a plain program's by a relative error of at most 0.012.
Values may be sent and summed in bfloat16 or wider, within the bound.
No kernel may reach another device: no remote copies, remote signals or barrier semaphores. Data moves between devices by JAX's collectives and lax.ppermute only.
A program may use at most 192 MiB of HBM per device.

v0:
```python
import jax
import jax.numpy as jnp
from jax import lax
from jax.sharding import PartitionSpec as P

BLOCK = 128


HIGHEST = lax.Precision.HIGHEST
EPSILON = 1e-05
ROOT_HALF = 0.7071067811865476
DENSITY = 0.3989422804014327


def carried_in(array, axis, join, neutral):
    place = lax.axis_index(axis)
    gathered = jax.tree.map(
        lambda a, kind: lax.all_gather(a.astype(kind), axis),
        array,
        (jnp.bfloat16, jnp.bfloat16, jnp.bfloat16),
    )
    state = jax.tree.map(lambda a, e: jnp.zeros_like(a) + jnp.asarray(e, a.dtype), array, neutral)

    def one(turn, state):
        return join(
            state,
            jax.tree.map(
                lambda a, own: lax.dynamic_index_in_dim(a, turn, 0, False).astype(own.dtype),
                gathered,
                array,
            ),
        )

    return lax.fori_loop(0, place, one, state)


def split_up(array, dim, peers):
    before, after = (array.shape[:dim], array.shape[dim + 1 :])
    return jnp.moveaxis(array.reshape(*before, peers, -1, *after), dim, 0)


def summed_on_arrival(array, axis, dim):
    blocks = split_up(array, dim, lax.axis_size(axis))
    arrived = lax.all_to_all(blocks, axis, split_axis=0, concat_axis=0, tiled=True)
    return arrived.astype(jnp.float32).sum(axis=0)


def entering(array, axis, combine, identity):
    peers, place = (lax.axis_size(axis), lax.axis_index(axis))
    everything = jax.tree.map(
        lambda part, kind: lax.all_gather(part.astype(kind), axis),
        array,
        jax.tree.map(lambda a: jnp.bfloat16 if a.dtype == jnp.float32 else a.dtype, array),
    )
    start = jax.tree.map(
        lambda part, zero: jnp.broadcast_to(jnp.asarray(zero, part.dtype), part.shape),
        array,
        identity,
    )

    def turn(k, before):
        at = peers - 1 - k
        reached = at > place
        new = combine(
            before, jax.tree.map(lambda part, own: part[at].astype(own.dtype), everything, array)
        )
        return jax.tree.map(lambda a, b: jnp.where(reached, a, b), new, before)

    return lax.fori_loop(0, peers, turn, start)


def product(pattern, *operands):
    return jnp.einsum(pattern, *operands, precision=HIGHEST)


def norm_parts(values, gain_vec, shift_vec):
    row_mean = jnp.mean(values, axis=-1, keepdims=True)
    centered = values - row_mean
    variance = jnp.mean(centered * centered, axis=-1, keepdims=True)
    inv_scale = lax.rsqrt(variance + EPSILON)
    unit_rows = centered * inv_scale
    return (unit_rows * gain_vec + shift_vec, unit_rows, inv_scale)


def norm_back(upstream, unit_rows, inv_scale, gain_vec):
    scaled = upstream * gain_vec
    return inv_scale * (
        scaled
        - jnp.mean(scaled, axis=-1, keepdims=True)
        - unit_rows * jnp.mean(scaled * unit_rows, axis=-1, keepdims=True)
    )


def gelu_value(pre_act):
    return pre_act * 0.5 * (1.0 + lax.erf(pre_act * ROOT_HALF))


def gelu_slope(pre_act):
    return 0.5 * (1.0 + lax.erf(pre_act * ROOT_HALF)) + pre_act * DENSITY * jnp.exp(
        -0.5 * pre_act * pre_act
    )


def features(rows, random_maps):
    angles = product("blhd,hdf->bhlf", rows, random_maps)
    return jnp.concatenate([jnp.sin(angles), jnp.cos(angles)], axis=-1)


def block_step(carried, pieces):
    state_mat, state_sum, offset = carried
    query_feats, key_feats, values, log_gate, fresh_share = pieces
    cum_log = jnp.cumsum(log_gate, axis=-1)
    positions = jnp.arange(cum_log.shape[-1])
    causal = positions[:, None] >= positions[None, :]
    log_gap = jnp.minimum(cum_log[..., :, None] - cum_log[..., None, :], 0.0)
    weights = jnp.where(causal, jnp.exp(log_gap), 0.0) * fresh_share[..., None, :]
    kernel = product("bhtf,bhsf->bhts", query_feats, key_feats) * weights
    decay_in = jnp.exp(cum_log)
    numerator = product("bhts,bhsd->bhtd", kernel, values) + decay_in[..., None] * product(
        "bhtf,bhfd->bhtd", query_feats, state_mat
    )
    denominator = jnp.sum(kernel, axis=-1) + decay_in * product(
        "bhtf,bhf->bht", query_feats, state_sum
    )
    decay_out = jnp.exp(cum_log[..., -1:] - cum_log) * fresh_share
    decay_all = decay_in[..., -1]
    state_mat = decay_all[..., None, None] * state_mat + product(
        "bhs,bhsf,bhsd->bhfd", decay_out, key_feats, values
    )
    state_sum = decay_all[..., None] * state_sum + product("bhs,bhsf->bhf", decay_out, key_feats)
    return (
        (state_mat, state_sum, offset + cum_log[..., -1]),
        (numerator, denominator, offset[..., None] + cum_log),
    )


def run_blocks(query_feats, key_feats, values, log_gate, fresh_share, block_size):
    seq_count, head_count, length = log_gate.shape
    block_count = length // block_size

    def to_blocks(array):
        shaped = array.reshape((seq_count, head_count, block_count, block_size) + array.shape[3:])
        return jnp.moveaxis(shaped, 2, 0)

    def join_back(array):
        moved = jnp.moveaxis(array, 0, 2)
        return moved.reshape((seq_count, head_count, length) + moved.shape[4:])

    feat_width = query_feats.shape[-1]
    head_size = values.shape[-1]
    start = (
        jnp.zeros((seq_count, head_count, feat_width, head_size), query_feats.dtype),
        jnp.zeros((seq_count, head_count, feat_width), query_feats.dtype),
        jnp.zeros((seq_count, head_count), query_feats.dtype),
    )
    pieces = (
        to_blocks(query_feats),
        to_blocks(key_feats),
        to_blocks(values),
        to_blocks(log_gate),
        to_blocks(fresh_share),
    )
    final, outputs = lax.scan(jax.checkpoint(block_step), start, pieces)
    return (join_back(outputs[0]), join_back(outputs[1]), join_back(outputs[2]), final)


def mixer_base(query_rows, key_rows, value_rows, gate_logits, random_maps, block_size):
    query_feats = features(query_rows, random_maps)
    key_feats = features(key_rows, random_maps)
    values = jnp.transpose(value_rows, (0, 2, 1, 3))
    log_gate = jnp.transpose(jax.nn.log_sigmoid(gate_logits), (0, 2, 1))
    fresh_share = jnp.transpose(jax.nn.sigmoid(-gate_logits), (0, 2, 1))
    numerator, denominator, cumulative, final = run_blocks(
        query_feats, key_feats, values, log_gate, fresh_share, block_size
    )
    return (numerator, denominator, cumulative, query_feats, jnp.exp(final[2]), final[0], final[1])


def mixer_finish(numerator, denominator, cumulative, query_feats, state_in, sum_in):
    carry_in = jnp.exp(cumulative)
    numer_all = numerator + carry_in[..., None] * product("bhtf,bhfd->bhtd", query_feats, state_in)
    denom_all = denominator + carry_in * product("bhtf,bhf->bht", query_feats, sum_in)
    return numer_all / jnp.sqrt(denom_all * denom_all + 1.0)[..., None]


def link_states(earlier_part, later_part):
    decay_early, mat_early, sum_early = earlier_part
    decay_late, mat_late, sum_late = later_part
    return (
        decay_early * decay_late,
        decay_late[..., None, None] * mat_early + mat_late,
        decay_late[..., None] * sum_early + sum_late,
    )


def body(
    inputs,
    cotangent,
    mix_weight,
    gate_weight,
    gate_bias,
    out_weight,
    gain_first,
    shift_first,
    gain_second,
    shift_second,
    up_weight,
    down_weight,
    random_maps,
):
    gathered = (
        lax.all_gather(mix_weight, ("dp", "tensor"), axis=0, tiled=True),
        lax.all_gather(gate_weight, ("dp", "tensor"), axis=0, tiled=True),
        lax.all_gather(out_weight, ("dp", "tensor"), axis=0, tiled=True),
        lax.all_gather(gain_first, ("dp", "tensor"), axis=0, tiled=True),
        lax.all_gather(shift_first, ("dp", "tensor"), axis=0, tiled=True),
        lax.all_gather(gain_second, ("dp", "tensor"), axis=0, tiled=True),
        lax.all_gather(shift_second, ("dp", "tensor"), axis=0, tiled=True),
    )
    mix_full, gate_full, out_full = (gathered[0], gathered[1], gathered[2])
    gain_one = gathered[3].astype(jnp.float32)
    shift_one = gathered[4].astype(jnp.float32)
    gain_two = gathered[5].astype(jnp.float32)
    shift_two = gathered[6].astype(jnp.float32)
    up_local, down_local = (
        lax.all_gather(up_weight, "dp", axis=0, tiled=True),
        lax.all_gather(down_weight, "dp", axis=1, tiled=True),
    )
    seq_count, local_len, model_width = inputs.shape
    head_count = gate_bias.shape[0]
    head_size = model_width // head_count
    residual_in = inputs.astype(jnp.float32)
    normed_one, unit_one, scale_one = norm_parts(residual_in, gain_one, shift_one)
    attend_in = normed_one.astype(jnp.bfloat16)
    mixed_rows = jnp.einsum(
        "bld,de->ble", attend_in, mix_full, preferred_element_type=jnp.float32
    ).astype(jnp.bfloat16)
    gate_logits = (
        jnp.einsum("bld,dh->blh", attend_in, gate_full, preferred_element_type=jnp.float32)
        + gate_bias
    )
    split_rows = mixed_rows.astype(jnp.float32).reshape(
        seq_count, local_len, 3, head_count, head_size
    )
    maps_wide = random_maps.astype(jnp.float32)

    def base_local(query_rows, key_rows, value_rows, logit_rows):
        return mixer_base(query_rows, key_rows, value_rows, logit_rows, maps_wide, BLOCK)

    base_out, base_pull = jax.vjp(
        base_local, split_rows[:, :, 0], split_rows[:, :, 1], split_rows[:, :, 2], gate_logits
    )
    numerator, denominator, cumulative, query_feats, decay_all, state_mat, state_sum = base_out
    identity = (jnp.ones_like(decay_all), jnp.zeros_like(state_mat), jnp.zeros_like(state_sum))
    carried = carried_in((decay_all, state_mat, state_sum), "tensor", link_states, identity)
    state_in, sum_in = (carried[1], carried[2])
    attended, finish_pull = jax.vjp(
        mixer_finish, numerator, denominator, cumulative, query_feats, state_in, sum_in
    )
    attended_rows = (
        jnp.transpose(attended, (0, 2, 1, 3))
        .reshape(seq_count, local_len, model_width)
        .astype(jnp.bfloat16)
    )
    middle = residual_in + jnp.einsum(
        "bld,de->ble", attended_rows, out_full, preferred_element_type=jnp.float32
    )
    normed_two, unit_two, scale_two = norm_parts(middle, gain_two, shift_two)
    feed_in = normed_two.astype(jnp.bfloat16)
    feed_rows = lax.all_gather(feed_in, "tensor", axis=1, tiled=True)
    up_use, down_use = (up_local, down_local)
    pre_act = jnp.einsum("bld,df->blf", feed_rows, up_use, preferred_element_type=jnp.float32)
    hidden = gelu_value(pre_act).astype(jnp.bfloat16)
    partial_out = jnp.einsum("blf,fd->bld", hidden, down_use, preferred_element_type=jnp.float32)
    feed_out = lax.psum_scatter(
        partial_out.astype(jnp.bfloat16), "tensor", scatter_dimension=1, tiled=True
    ).astype(jnp.float32)
    output = (middle + feed_out).astype(jnp.bfloat16)
    upstream = cotangent.astype(jnp.float32)
    grad_rows = lax.all_gather(cotangent, "tensor", axis=1, tiled=True)
    grad_down = jnp.einsum("blf,bld->fd", hidden, grad_rows, preferred_element_type=jnp.float32)
    grad_hidden = jnp.einsum("bld,fd->blf", grad_rows, down_use, preferred_element_type=jnp.float32)
    grad_pre = (grad_hidden * gelu_slope(pre_act)).astype(jnp.bfloat16)
    grad_up = jnp.einsum("bld,blf->df", feed_rows, grad_pre, preferred_element_type=jnp.float32)
    grad_feed = jnp.einsum("blf,df->bld", grad_pre, up_use, preferred_element_type=jnp.float32)
    grad_feed = lax.psum_scatter(
        grad_feed.astype(jnp.bfloat16), "tensor", scatter_dimension=1, tiled=True
    ).astype(jnp.float32)
    grad_up, grad_down = (
        summed_on_arrival(grad_up.astype(jnp.bfloat16), "dp", 0),
        summed_on_arrival(grad_down.astype(jnp.bfloat16), "dp", 1),
    )
    gain_two_grad = jnp.sum(grad_feed * unit_two, axis=(0, 1))
    shift_two_grad = jnp.sum(grad_feed, axis=(0, 1))
    grad_middle = upstream + norm_back(grad_feed, unit_two, scale_two, gain_two)
    grad_branch = grad_middle.astype(jnp.bfloat16)
    grad_out = jnp.einsum(
        "bld,ble->de", attended_rows, grad_branch, preferred_element_type=jnp.float32
    )
    grad_attended = jnp.einsum(
        "ble,de->bld", grad_branch, out_full, preferred_element_type=jnp.float32
    )
    grad_attended = jnp.transpose(
        grad_attended.reshape(seq_count, local_len, head_count, head_size), (0, 2, 1, 3)
    )
    pulled = finish_pull(grad_attended)
    flowing = entering((decay_all, pulled[4], pulled[5]), "tensor", link_states, identity)
    out_mat, out_sum = (flowing[1], flowing[2])
    grad_decay = jnp.sum(out_mat * state_in, axis=(2, 3)) + jnp.sum(out_sum * sum_in, axis=2)
    grad_query, grad_key, grad_value, grad_logits = base_pull(
        (pulled[0], pulled[1], pulled[2], pulled[3], grad_decay, out_mat, out_sum)
    )
    grad_mix = (
        jnp.stack((grad_query, grad_key, grad_value), axis=2)
        .reshape(seq_count, local_len, 3 * model_width)
        .astype(jnp.bfloat16)
    )
    grad_logit_low = grad_logits.astype(jnp.bfloat16)
    bias_part = jnp.sum(grad_logits, axis=(0, 1))
    grad_mix_weight = jnp.einsum(
        "bld,ble->de", attend_in, grad_mix, preferred_element_type=jnp.float32
    )
    grad_gate_weight = jnp.einsum(
        "bld,blh->dh", attend_in, grad_logit_low, preferred_element_type=jnp.float32
    )
    grad_normed = jnp.einsum("ble,de->bld", grad_mix, mix_full, preferred_element_type=jnp.float32)
    grad_normed = grad_normed + jnp.einsum(
        "blh,dh->bld", grad_logit_low, gate_full, preferred_element_type=jnp.float32
    )
    gain_one_grad = jnp.sum(grad_normed * unit_one, axis=(0, 1))
    shift_one_grad = jnp.sum(grad_normed, axis=(0, 1))
    input_grad = grad_middle + norm_back(grad_normed, unit_one, scale_one, gain_one)
    reduced = (
        lax.psum_scatter(grad_mix_weight, ("dp", "tensor"), scatter_dimension=0, tiled=True),
        lax.psum_scatter(grad_gate_weight, ("dp", "tensor"), scatter_dimension=0, tiled=True),
        lax.psum_scatter(grad_out, ("dp", "tensor"), scatter_dimension=0, tiled=True),
        lax.psum_scatter(gain_one_grad, ("dp", "tensor"), scatter_dimension=0, tiled=True),
        lax.psum_scatter(shift_one_grad, ("dp", "tensor"), scatter_dimension=0, tiled=True),
        lax.psum_scatter(gain_two_grad, ("dp", "tensor"), scatter_dimension=0, tiled=True),
        lax.psum_scatter(shift_two_grad, ("dp", "tensor"), scatter_dimension=0, tiled=True),
    )
    bias_grad = lax.psum(bias_part, ("dp", "tensor"))
    return (
        output,
        input_grad,
        reduced[0],
        reduced[1],
        bias_grad,
        reduced[2],
        reduced[3],
        reduced[4],
        reduced[5],
        reduced[6],
        grad_up,
        grad_down,
    )


def solution(mesh):
    in_specs = (
        P("dp", "tensor", None),
        P("dp", "tensor", None),
        P(("dp", "tensor"), None),
        P(("dp", "tensor"), None),
        P(),
        P(("dp", "tensor"), None),
        P(("dp", "tensor")),
        P(("dp", "tensor")),
        P(("dp", "tensor")),
        P(("dp", "tensor")),
        P("dp", "tensor"),
        P("tensor", "dp"),
        P(),
    )
    out_specs = (
        P("dp", "tensor", None),
        P("dp", "tensor", None),
        P(("dp", "tensor"), None),
        P(("dp", "tensor"), None),
        P(),
        P(("dp", "tensor"), None),
        P(("dp", "tensor")),
        P(("dp", "tensor")),
        P(("dp", "tensor")),
        P(("dp", "tensor")),
        P("dp", "tensor"),
        P("tensor", "dp"),
    )
    return jax.shard_map(body, mesh=mesh, in_specs=in_specs, out_specs=out_specs, check_vma=False)
```

profile of v0, /device:TPU:0, one launch (start us, length us, event | category | flops | bytes accessed | tf_op | source)
XLA Modules:
  0.0 1023.1 jit_solution(18282705926242496672)
XLA Ops:
  11.5 42.0 %all-reduce.12 = (bf16[512]{0:T(512)(128)(2,1)S(1)}, bf16[512]{0:T(512)(128)(2,1)S(1)}, bf16[512]{0:T(512)(128)(2,1)S(1)}, bf16[512]{0:T(512)(128)(2,1)S(1)}) all-reduce(bf16[512]{0:T(512)(128)(2,1)S(1)} %dynamic-update-slice.1, bf16[512]{0:T(512)(128)(2,1)S(1)} %dynamic-update-slice, ...), channel_id=1, replica_groups=mesh['dp'=8,'tensor'=4] {'dp','tensor'}, use_global_device_ids=true, to_apply=%add.4 | all-reduce | flops 2048 | bytes 8192
  53.5 40.9 %all-gather.5 = bf16[32,16,8]{1,2,0:T(8,128)(2,1)S(1)} all-gather(bf16[1,16,8]{1,2,0:T(8,128)(2,1)} %bitcast.693), channel_id=1, replica_groups=mesh['dp'=8,'tensor'=4] {'dp','tensor'}, dimensions={0}, use_global_device_ids=true | all-gather | bytes 8448 | tf_op jit(solution)/shard_map/all_gather | solution.py:213
  126.1 5.8 copy.119
  151.9 51.8 %while.92 = (s32[]{:T(128)}, f32[3,8,128,64]{2,3,1,0:T(8,128)S(1)}, f32[3,8,128]{2,1,0:T(8,128)S(1)}, f32[3,8]{1,0:T(4,128)S(1)}, f32[2,3,8,128,64]{3,4,2,1,0:T(...) while((s32[]{:T(128)}, f32[3,8,128,64]{2,3,1,0:T(8,128)S(1)}, ...), condition=%wide.region_5.6_spmd.clone.clone, body=%wide.region_2.5_spmd.clone.sunk.clone | while | flops 1523730432 | bytes 20839652 | solution.py:163
  204.6 40.9 %all_gather.75 = bf16[512,512]{1,0:T(8,128)(2,1)} all-gather(bf16[16,512]{1,0:T(8,128)(2,1)S(1)} %copy-done.62), channel_id=1, replica_groups=mesh['dp'=8,'tensor'=4] {'dp','tensor'}, dimensions={0}, use_global_device_ids=true | all-gather | bytes 540672 | tf_op jit(solution)/shard_map/all_gather | solution.py:214
  261.2 6.2 divide_convert_fusion
  270.5 34.0 %all_gather.79 = bf16[512,512]{1,0:T(8,128)(2,1)} all-gather(bf16[64,512]{1,0:T(8,128)(2,1)} %param.31), channel_id=1, replica_groups=mesh['dp'=8,'tensor'=4] {'dp'}, dimensions={0}, use_global_device_ids=true | all-gather | bytes 589824 | tf_op jit(solution)/shard_map/all_gather | solution.py:226
  304.4 33.6 %all_gather.80 = bf16[512,512]{0,1:T(8,128)(2,1)} all-gather(bf16[512,64]{0,1:T(8,128)(2,1)} %param.32), channel_id=1, replica_groups=mesh['dp'=8,'tensor'=4] {'dp'}, dimensions={1}, use_global_device_ids=true | all-gather | bytes 589824 | tf_op jit(solution)/shard_map/all_gather | solution.py:227
  338.1 6.3 multiply_convert_fusion
  344.4 6.2 fusion.109
  361.8 33.2 %reduce-scatter.10.cloned.1.call-done = bf16[3,256,512]{2,1,0:T(8,128)(2,1)} async-done(((bf16[3,1024,512]{2,1,0:T(8,128)(2,1)}), bf16[3,256,512]{2,1,0:T(8,128)(2,1)}) %reduce-scatter.10.cloned.1.call-update) | async-done | bytes 786448 | tf_op jit(solution)/shard_map/reduce_scatter | solution.py:286
  397.5 38.0 %reduce-scatter.8.cloned.1.call-done = bf16[3,256,512]{2,1,0:T(8,128)(2,1)} async-done(((bf16[3,1024,512]{2,1,0:T(8,128)(2,1)}), bf16[3,256,512]{2,1,0:T(8,128)(2,1)}) %reduce-scatter.8.cloned.1.call-update) | async-done | bytes 786448 | tf_op jit(solution)/shard_map/reduce_scatter | solution.py:275
  461.6 6.6 all-gather.21.cloned.1.call-done
  468.2 16.0 %while.93 = (s32[]{:T(128)}, f32[3,8,128,64]{3,2,1,0:T(8,128)}, f32[3,8,128]{2,1,0:T(8,128)S(1)}, s32[]{:T(128)}, bf16[4,3,8]{2,1,0:T(4,128)(2,1)S(1)}, /*index=...) while((s32[]{:T(128)}, f32[3,8,128,64]{3,2,1,0:T(8,128)}, ...), condition=%wide.region_16.17_spmd.clone.clone, body=%wide.region_15.16_spmd.clone.sunk.clone | while | flops 998432 | bytes 3570165 | solution.py:69
  492.9 147.7 %while.91 = (s32[]{:T(128)}, f32[3,8,128,64]{2,3,1,0:T(8,128)}, f32[3,8,128]{2,1,0:T(8,128)S(1)}, f32[3,8]{1,0:T(4,128)S(1)}, f32[2,3,8,128,128]{4,3,2,1,0:T(8,1...) while((s32[]{:T(128)}, f32[3,8,128,64]{2,3,1,0:T(8,128)}, ...), condition=%wide.region_31.32_spmd.clone, body=%wide.region_20.31_spmd.sunk.clone | while | flops 3958389760 | bytes 159438128 | solution.py:163
  646.5 5.8 copy.145
  660.1 5.8 copy.144
  671.6 8.3 fusion.165
  685.0 8.6 fusion.168
  715.5 9.6 all-to-all-done.1
  729.4 14.0 %all-to-all-done = bf16[8,64,512]{2,1,0:T(8,128)(2,1)S(1)} async-done(((bf16[8,64,512]{2,1,0:T(8,128)(2,1)}), bf16[8,64,512]{2,1,0:T(8,128)(2,1)S(1)}, u32[]{:S(2)}, u32[]{:S(2)}) %all-to-all-start) | async-done | bytes 524320 | tf_op jit(solution)/shard_map/all_to_all | solution.py:44
  749.7 38.6 %all-reduce.11 = (f32[8]{0:T(128)}, f32[512]{0:T(512)S(1)}, f32[512]{0:T(512)S(1)}, f32[512]{0:T(512)S(1)}, f32[512]{0:T(512)S(1)}) all-reduce(f32[8]{0:T(128)S(1)} %copy-done.72, f32[512]{0:T(512)S(1)} %get-tuple-element.995, f32[512]{0:T(512)S(1)} %get-tuple-element.998, ...), channel_id=1, replica_groups=mesh['dp'=8,'tensor'=4] {'dp','tensor'}, use_global_device_ids=true, to_apply=%region_37.38 | all-reduce | flops 2056 | bytes 16448 | tf_op jit(solution)/shard_map/psum | solution.py:342
  795.1 117.6 %reduce-scatter.14.cloned.1.call-done = f32[16,512]{1,0:T(8,128)} async-done(((f32[512,512]{1,0:T(8,128)}), f32[16,512]{1,0:T(8,128)}) %reduce-scatter.14.cloned.1.call-update) | async-done | bytes 32784 | tf_op jit(solution)/shard_map/reduce_scatter | solution.py:336
  912.7 103.4 %reduce-scatter.12.cloned.1.call-done = f32[16,1536]{1,0:T(8,128)} async-done(((f32[512,1536]{1,0:T(8,128)}), f32[16,1536]{1,0:T(8,128)}) %reduce-scatter.12.cloned.1.call-update) | async-done | bytes 98320 | tf_op jit(solution)/shard_map/reduce_scatter | solution.py:334
  (461 shorter events, 373.2 us)
Async XLA Ops:
  7.2 98.4 %copy-start = (bf16[8,64,64]{2,1,0:T(8,128)(2,1)S(1)}, bf16[8,64,64]{2,1,0:T(8,128)(2,1)}, u32[]{:S(2)}) copy-start(bf16[8,64,64]{2,1,0:T(8,128)(2,1)} %param.33) | copy-start | bytes 196612
  7.2 88.7 %copy-start.33 = (bf16[3,256,512]{2,1,0:T(8,128)(2,1)S(1)}, bf16[3,256,512]{2,1,0:T(8,128)(2,1)}, u32[]{:S(2)}) copy-start(bf16[3,256,512]{2,1,0:T(8,128)(2,1)} %param.21) | copy-start | bytes 2359300
  7.2 89.1 %copy-start.75 = (f32[8]{0:T(128)S(1)}, f32[8]{0:T(128)}, u32[]{:S(2)}) copy-start(f32[8]{0:T(128)} %param.25) | copy-start | bytes 100
  7.2 89.7 %all-gather.13.cloned.1.call-start = ((), (), s32[]{:S(2)}) async-start(), calls=%async_computation.7 | async-start | bytes 1622016 | tf_op jit(solution)/shard_map/all_gather | solution.py:212
  7.9 247.9 %all-gather.19.cloned.1.call-start = ((), (), s32[]{:S(2)}) async-start(), calls=%async_computation.14 | async-start | bytes 1966080 | tf_op jit(solution)/shard_map/all_gather | solution.py:18
  53.5 43.4 %copy-start.73 = (f32[512]{0:T(512)}, f32[512]{0:T(512)S(1)}, u32[]{:S(2)}) copy-start(f32[512]{0:T(512)S(1)} %convert_element_type.180) | copy-start | bytes 6148
  53.5 43.4 %copy-start.65 = (f32[512]{0:T(512)}, f32[512]{0:T(512)S(1)}, u32[]{:S(2)}) copy-start(f32[512]{0:T(512)S(1)} %convert_element_type.179) | copy-start | bytes 6148
  106.0 25.9 %copy-start.25 = (f32[8,3,256,64]{2,3,1,0:T(8,128)}, f32[8,3,256,64]{2,3,1,0:T(8,128)S(1)}, u32[]{:S(2)}) copy-start(f32[8,3,256,64]{2,3,1,0:T(8,128)S(1)} %fusion.174) | copy-start | bytes 4718596
  204.6 133.5 %all-gather.15.cloned.1.call-start = ((), (), s32[]{:S(2)}) async-start(), calls=%async_computation.8 | async-start | bytes 3932160 | tf_op jit(solution)/shard_map/all_gather | solution.py:270
  256.3 227.9 %copy-start.11 = (f32[3,8,128,64]{3,2,1,0:T(8,128)}, f32[3,8,128,64]{3,2,1,0:T(8,128)S(1)}, u32[]{:S(2)}) copy-start(f32[3,8,128,64]{3,2,1,0:T(8,128)S(1)} %get-tuple-element.773) | copy-start | bytes 2359300
  269.9 74.5 %all-gather.17.cloned.1.call-start = ((), (), s32[]{:S(2)}) async-start(), calls=%async_computation.10 | async-start | bytes 3932160 | tf_op jit(solution)/shard_map/all_gather | solution.py:280
  270.4 124.5 %reduce-scatter.10.cloned.1.call-start = ((), (), s32[]{:S(2)}) async-start(), calls=%async_computation.11 | async-start | bytes 3932160 | tf_op jit(solution)/shard_map/reduce_scatter | solution.py:286
  355.8 79.7 %reduce-scatter.8.cloned.1.call-start = ((), (), s32[]{:S(2)}) async-start(), calls=%async_computation.9 | async-start | bytes 3932160 | tf_op jit(solution)/shard_map/reduce_scatter | solution.py:275
  361.7 106.4 %all-gather.21.cloned.1.call-start = ((), (), s32[]{:S(2)}) async-start(), calls=%async_computation.15 | async-start | bytes 1966080 | tf_op jit(solution)/shard_map/all_gather | solution.py:51
  448.2 345.6 %reduce-scatter.16.cloned.1.call-start = ((), (), s32[]{:S(2)}) async-start(), calls=%async_computation.16 | async-start | bytes 270336
  492.9 149.3 %copy-start.59 = (f32[3,256]{1,0:T(4,128)S(1)}, f32[3,256]{1,0:T(4,128)}, u32[]{:S(2)}) copy-start(f32[3,256]{1,0:T(4,128)} %copy-done.58) | copy-start | bytes 9220
  644.8 267.9 %reduce-scatter.14.cloned.1.call-start = ((), (), s32[]{:S(2)}) async-start(), calls=%async_computation.13 | async-start | bytes 1081344 | tf_op jit(solution)/shard_map/reduce_scatter | solution.py:336
  646.4 369.6 %reduce-scatter.12.cloned.1.call-start = ((), (), s32[]{:S(2)}) async-start(), calls=%async_computation.12 | async-start | bytes 3244032 | tf_op jit(solution)/shard_map/reduce_scatter | solution.py:334
  671.6 8.4 copy-start.12
  671.6 8.4 copy-start.24
  685.0 8.6 copy-start.39
  704.6 20.6 %all-to-all-start.1 = ((bf16[8,512,64]{1,2,0:T(8,128)(2,1)}), bf16[8,512,64]{1,2,0:T(8,128)(2,1)S(1)}, u32[]{:S(2)}, u32[]{:S(2)}) async-start(bf16[8,512,64]{1,2,0:T(8,128)(2,1)} %bitcast.115), calls=%async_computation.5 | async-start | bytes 1048576 | tf_op jit(solution)/shard_map/all_to_all | solution.py:44
  725.1 18.2 %all-to-all-start = ((bf16[8,64,512]{2,1,0:T(8,128)(2,1)}), bf16[8,64,512]{2,1,0:T(8,128)(2,1)S(1)}, u32[]{:S(2)}, u32[]{:S(2)}) async-start(bf16[8,64,512]{2,1,0:T(8,128)(2,1)} %bitcast.686), calls=%async_computation.4 | async-start | bytes 1048576 | tf_op jit(solution)/shard_map/all_to_all | solution.py:44
  747.7 42.9 %copy-start.67 = (f32[512]{0:T(512)S(1)}, f32[512]{0:T(512)}, u32[]{:S(2)}) copy-start(f32[512]{0:T(512)} %copy-done.65) | copy-start | bytes 6148
  (86 other events, 277.5 us)
Sparse Core Ops, SparseCore 0:
  10.9 57.8 all-gather.12
  204.7 17.3 all-gather.18
  270.0 31.4 all-gather.14
  302.9 28.5 all-gather.16
  355.9 39.0 reduce-scatter.9
  397.5 37.9 reduce-scatter.7
  448.3 19.8 all-gather.20
  644.9 134.0 reduce-scatter.15
  782.0 130.6 reduce-scatter.13
  918.5 97.4 reduce-scatter.11
where the time goes:
time: 1030 us; the launch traced here: 1020 us
  waiting for transfers between devices  324 us (31%)
  blocking collectives  246 us (24%)
  matrix products  220 us (21%)
  local copies, waits for them, and re-layouts  122 us (12%)
  other arithmetic  56.9 us (6%)
  loops' own time  29.8 us (3%)
  between operations  15.2 us (1%)
    dot_general x47, matrix products, product(): return jnp.einsum(pattern, *operands, precision=HIGHEST)  169 us
    reduce_scatter x1, waiting for transfers between devices, body(): lax.psum_scatter(grad_out, ('dp', 'tensor'), scatter_dimension=0, tiled=T...  118 us
    reduce_scatter x1, waiting for transfers between devices, body(): lax.psum_scatter(grad_mix_weight, ('dp', 'tensor'), scatter_dimension=0,...  103 us
    unnamed x1, blocking collectives  42 us
    all_gather x1, blocking collectives, body(): lax.all_gather(out_weight, ('dp', 'tensor'), axis=0, tiled=True)  40.9 us
    all_gather x1, blocking collectives, body(): lax.all_gather(gate_weight, ('dp', 'tensor'), axis=0, tiled=True)  40.9 us
    psum x1, blocking collectives, body(): bias_grad = lax.psum(bias_part, ('dp', 'tensor'))  38.6 us
    reduce_scatter x1, waiting for transfers between devices, body(): lax.psum_scatter(partial_out.astype(jnp.bfloat16), 'tensor', scatter_dime...  38 us
  transfers between devices with their start and end apart: 12, of which 7 were waited for; matrix products, arithmetic and copies ran while one was open for 10% of the time, Pallas kernels for 0%

commit v1 on v0

v1 whole, which is shorter than its diff:
```python
import functools

import jax
import jax.numpy as jnp
from jax import lax
from jax.experimental import pallas as pl
from jax.experimental.pallas import tpu as pltpu
from jax.sharding import PartitionSpec as P

BOTH = ("dp", "tensor")
F32 = jnp.float32
BF16 = jnp.bfloat16
EPSILON = 1e-05
ROOT_HALF = 0.7071067811865476
DENSITY = 0.3989422804014327
SIN = (9.9999999998e-01, -1.6666666617e-01, 8.3333309689e-03, -1.9840860382e-04, 2.7525224003e-06, -2.3888330913e-08)
COS = (9.9999999978e-01, -4.9999999354e-01, 4.1666636104e-02, -1.3888359409e-03, 2.4760057595e-05, -2.6049626765e-07)

NN = (((1,), (0,)), ((), ()))
NT = (((1,), (1,)), ((), ()))
TN = (((0,), (0,)), ((), ()))


def mm(a, b, dims=NN):
    return lax.dot_general(a, b, dims, preferred_element_type=F32)


def low(a):
    return a.astype(BF16)


def lanes_of(shape):
    return lax.broadcasted_iota(jnp.int32, shape, len(shape) - 1)


def swap_halves(a):
    return pltpu.roll(a, 64, 1)


def sincos(a):
    turns = jnp.floor(a * 0.3183098861837907 + 0.5)
    r = (a - turns * 3.140625) - turns * 9.676535897932e-4
    half = turns * 0.5
    sign = 1.0 - 4.0 * (half - jnp.floor(half))
    r2 = r * r
    s = r * (SIN[0] + r2 * (SIN[1] + r2 * (SIN[2] + r2 * (SIN[3] + r2 * (SIN[4] + r2 * SIN[5])))))
    c = COS[0] + r2 * (COS[1] + r2 * (COS[2] + r2 * (COS[3] + r2 * (COS[4] + r2 * COS[5]))))
    return sign * s, sign * c


def normal_parts(v):
    x = jnp.abs(v) * ROOT_HALF
    base = 1.0 + 0.3275911 * x
    t = pl.reciprocal(base, approx=True)
    t = t * (2.0 - base * t)
    bell = jnp.exp(-0.5 * v * v)
    poly = t * (0.254829592 + t * (-0.284496736 + t * (1.421413741 + t * (-1.453152027 + t * 1.061405429))))
    tail = 0.5 * poly * bell
    return jnp.where(v >= 0.0, 1.0 - tail, tail), DENSITY * bell


def three_parts(a):
    high = a.astype(BF16)
    rest = a - high.astype(F32)
    mid = rest.astype(BF16)
    return high, mid, (rest - mid.astype(F32)).astype(BF16)


def tri_sum(tri, a):
    high, mid, rest = three_parts(a)
    return mm(tri, high) + (mm(tri, mid) + mm(tri, rest))


def norm_of(x):
    mean = jnp.mean(x, axis=-1, keepdims=True)
    centered = x - mean
    inv = lax.rsqrt(jnp.mean(centered * centered, axis=-1, keepdims=True) + EPSILON)
    return centered * inv, inv


def norm_back(s, unit, inv):
    return inv * (
        s
        - jnp.mean(s, axis=-1, keepdims=True)
        - unit * jnp.mean(s * unit, axis=-1, keepdims=True)
    )


def chip_row(pos, mz, mx, my):
    return (((pos[0] ^ mz) * 2 + (pos[1] ^ mx)) * 2 + (pos[2] ^ my)) * 32


def lower_tri(n):
    row = lax.broadcasted_iota(jnp.int32, (n, n), 0)
    col = lax.broadcasted_iota(jnp.int32, (n, n), 1)
    return row, col


def unpack_states(pack, b, zcols, last=65):
    lane = lanes_of((128, 128))
    out = []
    for p in range(2):
        both = pack[2 * b + p].astype(F32)
        for h, mat in ((2 * p, both), (2 * p + 1, swap_halves(both))):
            z = jnp.sum(jnp.where(lane == 4 * b + h, zcols, 0.0), axis=1, keepdims=True)
            out.append(jnp.where(lane < 64, mat, jnp.where(lane <= last, z, 0.0)))
    return out


def pack_states(states, pack_o, b, last, split=False):
    lane = lanes_of((128, 128))
    zcols = jnp.where(b == 0, 0.0, pack_o[last].astype(F32))

    def sum_of(s):
        return s[:, 64:65] + s[:, 65:66] if split else s[:, 64:65]

    for p in range(2):
        s0, s1 = states[2 * p], states[2 * p + 1]
        pack_o[2 * b + p] = jnp.where(lane < 64, s0, swap_halves(s1)).astype(BF16)
        zcols = jnp.where(lane == 4 * b + 2 * p, sum_of(s0), zcols)
        zcols = jnp.where(lane == 4 * b + 2 * p + 1, sum_of(s1), zcols)
    pack_o[last] = zcols.astype(BF16)


def project_kernel(
    b, pos, own, oth, w0, w1, w2, w3, bias, maps,
    a_o, fq_o, fk_o, fql_o, fkl_o, va_o, ccol_o, ucol_o, crow_o, urow_o, smid_o, pack_o, wmix_o, vec_o, vbar_o,
):
    chunk = own.shape[1]
    nz = w0.shape[0]

    @pl.when(b == 0)
    def _():
        for piece, (my, mx) in ((w0, (0, 0)), (w1, (0, 1)), (w2, (1, 0)), (w3, (1, 1))):
            for mz in range(nz):
                base = chip_row(pos, mz, mx, my)
                for mc in range(2):
                    row = pl.multiple_of(base + (pos[3] ^ mc) * 16, 16)
                    wmix_o[pl.ds(row, 16), :] = piece[mz, mc]
        vec_o[...] = wmix_o[:, 768:896].astype(F32).T[0:8]
        vbar_o[...] = mm(jnp.broadcast_to(vec_o[5:6], vec_o.shape).astype(BF16), wmix_o[:, 512:768])

    gain, shift = vec_o[4:5], vec_o[5:6]
    first = pos[3] == 0
    row, col = lower_tri(chunk)
    tri = jnp.where(row >= col, 1.0, 0.0).astype(BF16)
    lane = lanes_of((chunk, 128))
    states = [None] * 4
    for j in range(2):
        rows = slice(j * chunk, (j + 1) * chunk)
        mine, theirs = own[0], oth[0]
        x = jnp.where(first == (j == 0), mine, theirs).astype(F32)
        unit, _ = norm_of(x)
        a = (unit * gain + shift).astype(BF16)
        a_o[0, rows] = a
        mixed = mm(a, wmix_o[:, 0:768]).astype(BF16)
        logits = jnp.where(lane < 4, mm(a, wmix_o[:, 768:896]) + bias[...], 0.0)
        e = jnp.exp(-jnp.abs(logits))
        w = 1.0 + e
        log1 = jnp.where(w == 1.0, e, jnp.log(w) * (e / jnp.where(w == 1.0, 1.0, w - 1.0)))
        log_gate = jnp.minimum(logits, 0.0) - log1
        fresh = jnp.where(logits >= 0.0, e, 1.0) / w
        cum = tri_sum(tri, log_gate)
        ccol_o[0, rows] = cum
        ucol_o[0, rows] = fresh
        crow_o[0, j] = cum.T[0:8]
        urow_o[0, j] = fresh.T[0:8]
        dout = jnp.exp(cum[chunk - 1 : chunk] - cum) * fresh
        for p in range(2):
            for base, target, rest in ((0, fq_o, fql_o), (256, fk_o, fkl_o)):
                angles = mm(mixed[:, base + 128 * p : base + 128 * p + 128], maps[p])
                s, c = sincos(angles)
                for h, f in (
                    (2 * p, jnp.where(lane < 64, s, swap_halves(c))),
                    (2 * p + 1, jnp.where(lane < 64, swap_halves(s), c)),
                ):
                    high = low(f)
                    target[0, h, rows] = high
                    rest[0, h, rows] = low(f - high.astype(F32))
            v = mixed[:, 512 + 128 * p : 640 + 128 * p].astype(F32) - vbar_o[0:1, 128 * p : 128 * p + 128]
            one = jnp.where((lane == 64) | (lane == 65), 1.0, 0.0)
            for h, vh in ((2 * p, v), (2 * p + 1, swap_halves(v))):
                aug = jnp.where(lane < 64, vh, one)
                va_o[0, h, rows] = aug.astype(BF16)
                local = mm(fk_o[0, h, rows], low(aug * dout[:, h : h + 1]), TN)
                if j == 0:
                    states[h] = local
                    smid_o[0, h] = local
                else:
                    states[h] = states[h] * jnp.exp(cum[chunk - 1 : chunk, h : h + 1]) + local
    pack_states(states, pack_o, b, pack_o.shape[0] - 1)


def weights_of(ccol, ucol_row, crow, row, col):
    gap = jnp.minimum(ccol - crow, 0.0)
    return jnp.where(row >= col, jnp.exp(gap), 0.0) * ucol_row


def scores(fq, fk, fql, fkl, h, rows):
    q, k = fq[0, h, rows], fk[0, h, rows]
    return mm(
        jnp.concatenate([q, fql[0, h, rows], q], axis=1), jnp.concatenate([k, k, fkl[0, h, rows]], axis=1), NT
    )


def local_kernel(b, fq, fk, fql, fkl, va, ccol, crow, urow, o_o):
    chunk = crow.shape[3]
    row, col = lower_tri(chunk)
    for j in range(2):
        rows = slice(j * chunk, (j + 1) * chunk)
        for h in range(4):
            w = weights_of(ccol[0, rows, h : h + 1], urow[0, j, h : h + 1], crow[0, j, h : h + 1], row, col)
            qk = scores(fq, fk, fql, fkl, h, rows)
            o_o[0, h, rows] = mm(low(qk * w), va[0, h, rows])


def mean_of(vbar, h):
    pair = vbar[:, 128 * (h // 2) : 128 * (h // 2) + 128]
    return (pair if h % 2 == 0 else swap_halves(pair))[0:1]


def finish_kernel(b, pos, o_loc, fq, ccol, pack, smid, vbar, o_o, st_o, keep_o, send_o):
    chunk = ccol.shape[1] // 2
    zcols = pack[pack.shape[0] - 1].astype(F32)
    states = unpack_states(pack, b, zcols)
    lane = lanes_of((chunk, 128))
    cend = ccol[0, chunk - 1 : chunk]
    att = [[None] * 4, [None] * 4]
    for h in range(4):
        s0 = states[h]
        s1 = jnp.exp(cend[:, h : h + 1]) * s0 + smid[0, h]
        for j, s in ((0, s0), (1, s1)):
            rows = slice(j * chunk, (j + 1) * chunk)
            near = low(s)
            st_o[0, h, j] = near
            o = o_loc[0, h, rows] + jnp.exp(ccol[0, rows, h : h + 1]) * mm(fq[0, h, rows], near)
            o_o[0, h, rows] = o
            den = o[:, 64:65]
            att[j][h] = (o + den * mean_of(vbar, h)) * lax.rsqrt(den * den + 1.0)
    first = pos[3] == 0
    for p in range(2):
        both = [
            jnp.where(lane < 64, att[j][2 * p], swap_halves(att[j][2 * p + 1])) for j in range(2)
        ]
        keep_o[0, :, 128 * p : 128 * p + 128] = jnp.where(first, both[0], both[1]).astype(BF16)
        send_o[0, :, 128 * p : 128 * p + 128] = jnp.where(first, both[1], both[0]).astype(BF16)


def feed_kernel(
    pos, akeep, arecv, x, cot, vec, q0, q1, q2, q3, q4, q5, q6, q7,
    out_o, gm_o, gak_o, gas_o, gsend_o, gkeep_o, gv_o,
    up_s, dn_s, ow_s, feed_s, feedt_s, cott_s, att_s, hid_s, gp_s, gb_s, mid_s, unit_s, acc_s, gf_s, big_s,
):
    seqs, chunk, width = x.shape
    nz = q0.shape[0]
    pieces = (q0, q1, q2, q3, q4, q5, q6, q7)
    z, xbit, y, c = pos[0], pos[1], pos[2], pos[3]
    rows_up = up_s.shape[1] // (2 * nz)

    def dp_of(mz, mx):
        return (z ^ mz) * 2 + (xbit ^ mx)

    for mc in range(2):
        for my in range(2):
            t = (y ^ my) * 2 + (c ^ mc)
            for mx in range(2):
                piece = pieces[(mc * 2 + my) * 2 + mx]
                for mz in range(nz):
                    d = dp_of(mz, mx)
                    at = pl.multiple_of(d * rows_up, rows_up)
                    up_s[mc * 2 + my, pl.ds(at, rows_up), :] = piece[mz, 0:rows_up]
                    dn_s[mc * 2 + my, pl.ds(at, rows_up), :] = piece[mz, rows_up : 2 * rows_up]
                    ow_s[pl.ds(pl.multiple_of((d * 4 + t) * 16, 16), 16), :] = piece[mz, 2 * rows_up :]
    first = c == 0
    gain, shift = vec[6:7], vec[7:8]
    for r in range(seqs):
        rows = slice(r * chunk, (r + 1) * chunk)
        mine, theirs = akeep[r], arecv[r]
        att = jnp.concatenate(
            [jnp.where(first, mine, theirs), jnp.where(first, theirs, mine)], axis=1
        )
        att_s[rows] = att
        mid = x[r].astype(F32) + mm(att, ow_s[...])
        mid_s[rows] = mid
        unit, inv = norm_of(mid)
        unit_s[rows] = unit
        feed_s[rows] = (unit * gain + shift).astype(BF16)
        cott_s[:, rows] = cot[r].astype(F32).T.astype(BF16)
        feedt_s[:, rows] = (unit * gain + shift).T.astype(BF16)
    acc_s[...] = jnp.zeros_like(acc_s)
    gf_s[...] = jnp.zeros_like(gf_s)

    def scatter(source, target, my, offset, nrows):
        for mx in range(2):
            for mz in range(nz):
                at = pl.multiple_of(dp_of(mz, mx) * nrows, nrows)
                target[my, mx, mz, offset : offset + nrows, :] = source[pl.ds(at, nrows), :]

    for mc, target in ((1, gsend_o), (0, gkeep_o)):

        def one(my, carry, mc=mc, target=target):
            k = mc * 2 + my
            up, dn = up_s[k], dn_s[k]
            for r in range(seqs):
                rows = slice(r * chunk, (r + 1) * chunk)
                pre = mm(feed_s[rows], up)
                cdf, pdf = normal_parts(pre)
                hid = (pre * cdf).astype(BF16)
                gp = (mm(cot[r], dn) * (cdf + pre * pdf)).astype(BF16)
                hid_s[rows] = hid
                gp_s[rows] = gp
                acc_s[rows] += mm(hid, dn, NT)
                gf_s[rows] += mm(gp, up, NT)
            big_s[...] = mm(feedt_s[...], gp_s[...]).astype(BF16)
            scatter(big_s, target, my, 0, rows_up)
            big_s[...] = mm(cott_s[...], hid_s[...]).astype(BF16)
            scatter(big_s, target, my, rows_up, rows_up)
            return carry

        lax.fori_loop(0, 2, one, 0)

    gain_sum = jnp.zeros((1, width), F32)
    shift_sum = jnp.zeros((1, width), F32)
    for r in range(seqs):
        rows = slice(r * chunk, (r + 1) * chunk)
        mid = mid_s[rows]
        out_o[r] = (mid + acc_s[rows]).astype(BF16)
        unit = unit_s[rows]
        _, inv = norm_of(mid)
        gf = gf_s[rows]
        gain_sum += jnp.sum(gf * unit, axis=0, keepdims=True)
        shift_sum += jnp.sum(gf, axis=0, keepdims=True)
        gm = cot[r].astype(F32) + norm_back(gf * gain, unit, inv)
        gm_o[r] = gm
        gb = gm.astype(BF16)
        gb_s[rows] = gb
        ga = mm(gb, ow_s[...], NT).astype(BF16)
        half = width // 2
        gak_o[r] = jnp.where(first, ga[:, :half], ga[:, half:])
        gas_o[r] = jnp.where(first, ga[:, half:], ga[:, :half])
    gv_o[...] = jnp.concatenate([gain_sum, shift_sum, jnp.zeros((6, width), F32)], axis=0)
    big_s[...] = mm(att_s[...], gb_s[...], TN).astype(BF16)
    for mc, target in ((0, gkeep_o), (1, gsend_o)):
        for my in range(2):
            t = (y ^ my) * 2 + (c ^ mc)
            for mx in range(2):
                for mz in range(nz):
                    at = pl.multiple_of((dp_of(mz, mx) * 4 + t) * 16, 16)
                    target[my, mx, mz, 2 * rows_up :, :] = big_s[pl.ds(at, 16), :]


def adjoint_kernel(b, pos, gak, gar, o_all, fq, ccol, vbar, g_o, l1_o, pack_o):
    chunk = ccol.shape[1] // 2
    lane = lanes_of((chunk, 128))
    first = pos[3] == 0
    states = [None] * 4
    for j in range(2):
        rows = slice(j * chunk, (j + 1) * chunk)
        for p in range(2):
            cols = slice(128 * p, 128 * p + 128)
            pair = jnp.where(first == (j == 0), gak[0, :, cols], gar[0, :, cols]).astype(F32)
            for h, ga in ((2 * p, pair), (2 * p + 1, swap_halves(pair))):
                o = o_all[0, h, rows]
                den = o[:, 64:65]
                inv = lax.rsqrt(den * den + 1.0)
                gn = jnp.where(lane < 64, ga * inv, 0.0).astype(BF16).astype(F32)
                mean = mean_of(vbar, h)
                share = den * inv * inv
                gd = jnp.sum(gn * (mean - share * (o + den * mean)), axis=1, keepdims=True)
                high = gd.astype(BF16).astype(F32)
                g = jnp.where(lane == 64, high, jnp.where(lane == 65, gd - high, gn))
                g_o[0, h, rows] = low(g)
                decay = jnp.exp(ccol[0, rows, h : h + 1])
                local = mm(fq[0, h, rows], low(g * decay), TN)
                if j == 0:
                    states[h] = local
                else:
                    l1_o[0, h] = local
                    states[h] = states[h] + jnp.exp(ccol[0, chunk - 1 : chunk, h : h + 1]) * local
    pack_states(states, pack_o, b, pack_o.shape[0] - 1, split=True)


def local_back_kernel(b, fq, fk, fql, fkl, va, g, st, ccol, crow, urow, dfq_o, dfk_o, dva_o):
    chunk = crow.shape[3]
    row, col = lower_tri(chunk)
    for j in range(2):
        rows = slice(j * chunk, (j + 1) * chunk)
        for h in range(4):
            w = weights_of(ccol[0, rows, h : h + 1], urow[0, j, h : h + 1], crow[0, j, h : h + 1], row, col)
            q, k, v, gh = fq[0, h, rows], fk[0, h, rows], va[0, h, rows], g[0, h, rows]
            attn = low(scores(fq, fk, fql, fkl, h, rows) * w)
            dp = low(mm(gh, v, NT) * w)
            decay = jnp.exp(ccol[0, rows, h : h + 1])
            dfq_o[0, h, rows] = mm(dp, k) + decay * mm(gh, st[0, h, j], NT)
            dfk_o[0, h, rows] = mm(dp, q, TN)
            dva_o[0, h, rows] = mm(attn, gh, TN)


def close_kernel(
    b, pos, own, oth, a, fq, fk, va, dfq, dfk, dva, ccol, ucol, pack, l1, st, wmix, vec, gv, back,
    m00_o, m01_o, m10_o, m11_o, gnk_o, gns_o,
    acc_s, gate_s, vsum_s, big_s,
    *, seqs_total,
):
    seqs = seqs_total
    chunk = own.shape[1]
    nz = m00_o.shape[0]
    lane = lanes_of((chunk, 128))
    row, col = lower_tri(chunk)
    upper = jnp.where(row <= col, 1.0, 0.0).astype(BF16)
    zcols = pack[pack.shape[0] - 1].astype(F32)
    arrived = unpack_states(pack, b, zcols, last=64)
    wide = lanes_of((128, 128))
    first = pos[3] == 0

    @pl.when(b == 0)
    def _():
        acc_s[...] = jnp.zeros_like(acc_s)
        gate_s[...] = jnp.zeros_like(gate_s)
        vsum_s[...] = jnp.zeros_like(vsum_s)

    gain_sum = jnp.zeros((1, own.shape[2]), F32)
    shift_sum = jnp.zeros((1, own.shape[2]), F32)
    bias_sum = jnp.zeros((1, 128), F32)
    normed = [None, None]
    for j in range(2):
        rows = slice(j * chunk, (j + 1) * chunk)
        cum, fresh = ccol[0, rows], ucol[0, rows]
        dout = jnp.exp(cum[chunk - 1 : chunk] - cum) * fresh
        kd = jnp.zeros((chunk, 128), F32)
        qd = jnp.zeros((chunk, 128), F32)
        level = jnp.zeros((1, 128), F32)
        grads = [None] * 6
        for p in range(2):
            dvs, pq, pk = [None, None], [None, None], [None, None]
            for i in range(2):
                h = 2 * p + i
                adj = arrived[h]
                if j == 0:
                    adj = l1[0, h] + jnp.exp(ccol[0, 2 * chunk - 1 : 2 * chunk, h : h + 1]) * adj
                zs = adj[:, 64:65] + adj[:, 65:66]
                high = zs.astype(BF16).astype(F32)
                near = low(jnp.where(wide == 64, high, jnp.where(wide == 65, zs - high, adj)))
                d = dout[:, h : h + 1]
                keys = fk[0, h, rows]
                keys32 = keys.astype(F32)
                dk_far = d * mm(va[0, h, rows], near, NT)
                dk_near = dfk[0, h, rows]
                dvs[i] = dva[0, h, rows] + d * mm(keys, near)
                kd_far = jnp.sum(keys32 * dk_far, axis=1, keepdims=True)
                kd_near = jnp.sum(keys32 * dk_near, axis=1, keepdims=True)
                kd = jnp.where(lane == h, kd_far + kd_near, kd)
                passed = st[0, h, j].astype(F32) * near.astype(F32)
                passed = jnp.sum(jnp.sum(passed, axis=1, keepdims=True), axis=0, keepdims=True)
                total = jnp.sum(kd_far, axis=0, keepdims=True) + jnp.exp(cum[chunk - 1 : chunk, h : h + 1]) * passed
                level = jnp.where(lanes_of((1, 128)) == h, total, level)
                dk = dk_far + dk_near
                pk[i] = low(dk * swap_halves(keys32))
                dq, queries32 = dfq[0, h, rows], fq[0, h, rows].astype(F32)
                qd = jnp.where(lane == h, jnp.sum(queries32 * dq, axis=1, keepdims=True), qd)
                pq[i] = low(dq * swap_halves(queries32))
            grads[p] = mm(jnp.concatenate(pq, axis=1), back[p])
            grads[2 + p] = mm(jnp.concatenate(pk, axis=1), back[p])
            grads[4 + p] = jnp.where(lane < 64, dvs[0], swap_halves(dvs[1]))
        flow = qd - kd
        dlog = tri_sum(upper, flow) + level
        dlogit = jnp.where(lane < 4, fresh * dlog - (1.0 - fresh) * kd, 0.0)
        bias_sum += jnp.sum(dlogit, axis=0, keepdims=True)
        gm = jnp.concatenate([g.astype(BF16) for g in grads] + [dlogit.astype(BF16)], axis=1)
        acc_s[...] += mm(a[0, rows], gm, TN)
        back_in = mm(gm, wmix[...], NT)
        x = jnp.where(first == (j == 0), own[0], oth[0]).astype(F32)
        unit, _ = norm_of(x)
        gain_sum += jnp.sum(back_in * unit, axis=0, keepdims=True)
        shift_sum += jnp.sum(back_in, axis=0, keepdims=True)
        normed[j] = back_in
    gnk_o[0] = jnp.where(first, normed[0], normed[1])
    gns_o[0] = jnp.where(first, normed[1], normed[0]).astype(BF16)
    vsum_s[0:1] += gain_sum
    vsum_s[1:2] += shift_sum
    gate_s[0:1] += bias_sum

    @pl.when(b == seqs - 1)
    def _():
        width = vsum_s.shape[1]
        table = jnp.concatenate(
            [jnp.zeros((4, width), F32), vsum_s[0:2], gv[0:2], jnp.zeros((120, width), F32)], axis=0
        ).T
        total = gate_s[0:1]
        high = low(total).astype(F32)
        rest = jnp.broadcast_to(total - high, (8, 128))
        both = pltpu.roll(jnp.broadcast_to(high, (8, 128)), 8, 1) + pltpu.roll(rest, 12, 1)
        biases = jnp.broadcast_to(both[0:1], (width, 128))
        side = jnp.where(lanes_of((width, 128)) < 4, acc_s[:, 768:896], table) + biases
        big_s[:, 0:768] = acc_s[:, 0:768].astype(BF16)
        big_s[:, 768:896] = side.astype(BF16)
        for my in range(2):
            for mx in range(2):
                for mz in range(nz):
                    at = pl.multiple_of(chip_row(pos, mz, mx, my), 32)
                    (m00_o, m01_o, m10_o, m11_o)[2 * my + mx][mz] = big_s[pl.ds(at, 32), :]


def input_kernel(b, x, gm, keep, recv, vec, o):
    unit, inv = norm_of(x[0].astype(F32))
    grad = keep[0] + recv[0].astype(F32)
    o[0] = gm[0] + norm_back(grad * vec[4:5], unit, inv)


def join_kernel(*refs):
    for i, ref in enumerate(refs[:-1]):
        refs[-1][i] = ref[...]


def pair_sum_kernel(keep, recv, *outs):
    for i, out in enumerate(outs):
        out[...] = (keep[i // 2, i % 2].astype(F32) + recv[i // 2, i % 2].astype(F32)).astype(out.dtype)


def four_sum_kernel(a, b, c, d, out, *, carry):
    total = (a[...].astype(F32) + b[...].astype(F32)) + (c[...].astype(F32) + d[...].astype(F32))
    if carry:
        side = total[..., 768:896]
        rest = side - low(side).astype(F32)
        lane = lanes_of(side.shape)
        moved = jnp.where((lane >= 12) & (lane < 16), side + pltpu.roll(rest, 4, side.ndim - 1), side)
        out[..., 0:768] = low(total[..., 0:768])
        out[..., 768:896] = low(moved)
    else:
        out[...] = total.astype(out.dtype)


def call(kernel, steps, ins, outs, scratch=(), flops=0, name=None, limit=14):
    def spec(kind):
        if kind == "d":
            return pl.BlockSpec(memory_space=pl.ANY)
        return pl.BlockSpec(memory_space=pltpu.SMEM if kind == "m" else pltpu.VMEM)

    kinds = [kind for kind, _ in ins]
    out_kinds = [kind for kind, _, _ in outs]
    all_kinds = kinds + out_kinds + ["w"] * len(scratch)

    def run(*refs):
        used = [(kind, ref) for kind, ref in zip(all_kinds, refs) if kind != "d"]
        if not steps:
            kernel(*[ref for _, ref in used])
            return

        def one(b, carry):
            kernel(b, *[ref.at[pl.ds(b, 1)] if kind == "s" else ref for kind, ref in used])
            return carry

        lax.fori_loop(0, steps, one, 0)

    return pl.pallas_call(
        run,
        in_specs=[spec(kind) for kind in kinds],
        out_specs=[spec(kind) for kind in out_kinds],
        out_shape=[jax.ShapeDtypeStruct(shape, dtype) for _, shape, dtype in outs],
        scratch_shapes=list(scratch),
        compiler_params=pltpu.CompilerParams(vmem_limit_bytes=limit * 1024 * 1024),
        cost_estimate=pl.CostEstimate(flops=flops, bytes_accessed=1000000, transcendentals=0),
        name=name,
    )(*[a for _, a in ins])


def xor_with(a, mask, count):
    return lax.ppermute(a, BOTH, [(i, i ^ mask) for i in range(count)])


def body(
    inputs, cotangent, mix_weight, gate_weight, gate_bias, out_weight, gain_first, shift_first, gain_second,
    shift_second, up_weight, down_weight, random_maps,
):
    dp, tensor = lax.axis_size("dp"), lax.axis_size("tensor")
    count = dp * tensor
    place_dp, place_t = lax.axis_index("dp"), lax.axis_index("tensor")
    seqs, chunk, width = inputs.shape
    heads, head = random_maps.shape[0], random_maps.shape[1]
    hidden = up_weight.shape[1]
    core = place_t % 2
    first = core == 0
    direct = dp == 8
    nz = 4
    if direct:
        pos = jnp.stack([place_dp // 2, place_dp % 2, place_t // 2, core]).astype(jnp.int32)
    else:
        pos = jnp.stack([jnp.zeros_like(core)] * 3 + [core]).astype(jnp.int32)
    swap_core = functools.partial(xor_with, mask=1, count=count)

    def mix_pack(mix_w, gate_w, vecs):
        rows = mix_w.shape[0]
        split = mix_w.reshape(rows, 3, 2, width // 2)
        sides = [v[:, None] for v in vecs]
        pad = jnp.zeros((rows, 120), BF16)
        return [
            jnp.concatenate(
                [split[:, 0, s], split[:, 1, s], split[:, 2, s], gate_w[:, 4 * s : 4 * s + 4]] + sides + [pad], axis=1
            )
            for s in range(2)
        ]

    def join(parts, after=()):
        (out,) = call(
            join_kernel, 0, [("w", a) for a in parts] + [("d", a) for a in after],
            [("w", (len(parts), *parts[0].shape), parts[0].dtype)], name="join",
        )
        return out

    def sum_four(parts, dtype, after=(), carry=False):
        shape = parts[0].shape
        (out,) = call(
            functools.partial(four_sum_kernel, carry=carry), 0,
            [("w", a) for a in parts] + [("d", a) for a in after], [("w", shape, dtype)], name="sum_four",
        )
        return out

    other_in = swap_core(inputs)
    vectors = (gain_first, shift_first, gain_second, shift_second)
    if direct:
        rows = mix_weight.shape[0]

        def half(which):
            def placed(a, at):
                return lax.pad(a, jnp.zeros((), BF16), [(0, 0, 0), (at, 896 - at - a.shape[1], 0)])

            parts = [
                placed(lax.dynamic_slice(mix_weight, (0, width * i + (width // 2) * which), (rows, width // 2)), 256 * i)
                for i in range(3)
            ]
            parts.append(placed(lax.dynamic_slice(gate_weight, (0, 4 * which), (rows, 4)), 768))
            parts += [placed(v[:, None], 772 + i) for i, v in enumerate(vectors)]
            return functools.reduce(jnp.add, parts)

        keep, send = half(core), half(1 - core)
        pair = join([keep, swap_core(send)])
        line = join([pair] + [xor_with(pair, 8 * m, count) for m in range(1, nz)])
        w_pieces = [line] + [xor_with(line, m, count) for m in (4, 2, 6)]
        block = jnp.concatenate([up_weight, down_weight.T, out_weight], axis=0)
        (block,) = call(
            lambda a, out: out.__setitem__(..., a[...]), 0, [("w", block), ("d", line)],
            [("w", block.shape, BF16)], name="hold",
        )
        ff_line = join([block] + [xor_with(block, 8 * m, count) for m in range(1, nz)], after=w_pieces)
        ff_pieces = [ff_line] + [xor_with(ff_line, m, count) for m in (4, 2, 6)]
        ff_pieces = ff_pieces + [swap_core(piece) for piece in ff_pieces]
    else:
        whole = [
            lax.all_gather(a, BOTH, axis=0, tiled=True) for a in (mix_weight, gate_weight, out_weight) + vectors
        ]
        p0, p1 = mix_pack(whole[0], whole[1], whole[3:])
        blocks = jnp.where(first, p0, p1).reshape(nz, 2, 2, 2, 16, 896)
        blocks = jnp.where(first, blocks, blocks[:, :, :, ::-1])
        w_pieces = [blocks[:, mx, my] for my, mx in ((0, 0), (0, 1), (1, 0), (1, 1))]
        up_all = lax.all_gather(up_weight, BOTH, axis=0, tiled=False).reshape(dp, tensor, -1, hidden)
        dn_all = lax.all_gather(down_weight.T, BOTH, axis=0, tiled=False).reshape(dp, tensor, -1, hidden)
        up_all = jnp.moveaxis(up_all, 1, 0).reshape(2, 2, nz, 2, -1, hidden)
        dn_all = jnp.moveaxis(dn_all, 1, 0).reshape(2, 2, nz, 2, -1, hidden)
        out_all = whole[2].reshape(nz, 2, 2, 2, 16, width).transpose(2, 3, 0, 1, 4, 5)
        ff_all = jnp.concatenate([up_all, dn_all, out_all], axis=4)
        ff_all = jnp.where(first, ff_all, ff_all[:, ::-1])
        ff_pieces = [ff_all[my, mc, :, mx] for mc in range(2) for my in range(2) for mx in range(2)]

    maps = lax.dynamic_slice_in_dim(random_maps, core * 4, 4, 0)
    zero = jnp.zeros((head, head), BF16)
    maps_pair = jnp.stack(
        [
            jnp.concatenate(
                [jnp.concatenate([maps[2 * p], zero], 1), jnp.concatenate([zero, maps[2 * p + 1]], 1)], 0
            )
            for p in range(2)
        ]
    )
    flip = jnp.swapaxes(maps, 1, 2)
    maps_back = jnp.stack(
        [
            jnp.concatenate(
                [
                    jnp.concatenate([flip[2 * p], zero], 1),
                    jnp.concatenate([-flip[2 * p], zero], 1),
                    jnp.concatenate([zero, flip[2 * p + 1]], 1),
                    jnp.concatenate([zero, -flip[2 * p + 1]], 1),
                ],
                0,
            )
            for p in range(2)
        ]
    )
    bias = jnp.pad(lax.dynamic_slice_in_dim(gate_bias, core * 4, 4, 0), (0, 124))[None]

    long = 2 * chunk
    tokens = seqs * long
    feats = (seqs, 4, long, 128)
    npack = 2 * seqs + 1
    attend, fq, fk, fql, fkl, va, ccol, ucol, crow, urow, smid, pack, wmix, vec, vbar = call(
        project_kernel, seqs,
        [("m", pos), ("s", inputs), ("s", other_in)] + [("w", w) for w in w_pieces] + [("w", bias), ("w", maps_pair)],
        [
            ("s", (seqs, long, width), BF16), ("s", feats, BF16), ("s", feats, BF16), ("s", feats, BF16), ("s", feats, BF16), ("s", feats, BF16),
            ("s", (seqs, long, 128), F32), ("s", (seqs, long, 128), F32),
            ("s", (seqs, 2, 8, chunk), F32), ("s", (seqs, 2, 8, chunk), F32),
            ("s", (seqs, 4, 128, 128), F32),
            ("w", (npack, 128, 128), BF16), ("w", (width, 896), BF16), ("w", (8, width), F32),
            ("w", (8, width // 2), F32),
        ],
        flops=2 * tokens * width * 896, name="project",
    )
    ahead = [(i, i + 2) for i in range(count) if (i % tensor) < 2]
    arrived = lax.ppermute(pack, BOTH, ahead)
    (o_loc,) = call(
        local_kernel, seqs,
        [("s", fq), ("s", fk), ("s", fql), ("s", fkl), ("s", va), ("s", ccol), ("s", crow), ("s", urow)],
        [("s", feats, F32)], flops=2 * 2 * 24 * chunk * chunk * 128, name="local",
    )
    o_all, st, att_keep, att_send = call(
        finish_kernel, seqs,
        [("m", pos), ("s", o_loc), ("s", fq), ("s", ccol), ("w", arrived), ("s", smid), ("w", vbar)],
        [
            ("s", feats, F32), ("s", (seqs, 4, 2, 128, 128), BF16),
            ("s", (seqs, chunk, width // 2), BF16), ("s", (seqs, chunk, width // 2), BF16),
        ],
        flops=2 * 24 * chunk * 128 * 128, name="finish",
    )
    att_recv = swap_core(att_send)

    own = seqs * chunk
    nrows = ff_pieces[0].shape[1]
    payload = (2, 2, nz, nrows, hidden)
    output, grad_middle, ga_keep, ga_send, g_send, g_keep, grad_vec = call(
        feed_kernel, 0,
        [("m", pos)] + [("w", a) for a in (att_keep, att_recv, inputs, cotangent, vec, *ff_pieces)],
        [
            ("w", (seqs, chunk, width), BF16), ("w", (seqs, chunk, width), F32),
            ("w", (seqs, chunk, width // 2), BF16), ("w", (seqs, chunk, width // 2), BF16),
            ("w", payload, BF16), ("w", payload, BF16), ("w", (8, width), F32),
        ],
        scratch=[
            pltpu.VMEM((4, width, hidden), BF16), pltpu.VMEM((4, width, hidden), BF16),
            pltpu.VMEM((width, width), BF16),
            pltpu.VMEM((own, width), BF16), pltpu.VMEM((width, own), BF16), pltpu.VMEM((width, own), BF16),
            pltpu.VMEM((own, width), BF16), pltpu.VMEM((own, hidden), BF16), pltpu.VMEM((own, hidden), BF16),
            pltpu.VMEM((own, width), BF16), pltpu.VMEM((own, width), F32), pltpu.VMEM((own, width), F32),
            pltpu.VMEM((own, width), F32), pltpu.VMEM((own, width), F32), pltpu.VMEM((width, hidden), BF16),
        ],
        flops=12 * own * width * 4 * hidden, name="feed", limit=30,
    )
    ga_recv = swap_core(ga_send)

    if direct:
        g_recv = swap_core(g_send)
        s00, s01, s10, s11 = call(
            pair_sum_kernel, 0, [("w", g_keep), ("w", g_recv)], [("w", (nz, nrows, hidden), BF16)] * 4, name="pair_sum",
        )
        g_plane = [s00, xor_with(s01, 4, count), xor_with(s10, 2, count), xor_with(s11, 6, count)]
        before_adjoint = [s00]
    else:
        before_adjoint = []
        by_core = jnp.where(first, jnp.stack([g_keep, g_send]), jnp.stack([g_send, g_keep]))
        ordered = by_core.transpose(3, 2, 1, 0, 4, 5)
        rows_up = (nrows - 16) // 2
        ups = ordered[..., :rows_up, :].reshape(nz * 2, 4, rows_up, hidden).transpose(1, 0, 2, 3)
        dns = ordered[..., rows_up : 2 * rows_up, :].reshape(nz * 2, 4, rows_up, hidden).transpose(1, 0, 2, 3)
        ups = ups.reshape(4, dp, -1, hidden).transpose(1, 0, 2, 3)
        dns = dns.reshape(4, dp, -1, hidden).transpose(1, 0, 2, 3)
        outs = ordered[..., 2 * rows_up :, :].reshape(width, width)

        def reduced(a):
            return lax.psum_scatter(a.astype(F32).reshape(count, -1, a.shape[-1]), BOTH, scatter_dimension=0)

        up_grad, down_grad, out_grad = reduced(ups), reduced(dns).T, reduced(outs)

    g, l1, pack_b = call(
        adjoint_kernel, seqs,
        [("m", pos), ("s", ga_keep), ("s", ga_recv), ("s", o_all), ("s", fq), ("s", ccol), ("w", vbar)]
        + [("d", a) for a in before_adjoint],
        [
            ("s", feats, BF16), ("s", (seqs, 4, 128, 128), F32), ("w", (npack, 128, 128), BF16),
        ],
        flops=2 * 24 * chunk * 128 * 128, name="adjoint",
    )
    behind = [(i, i - 2) for i in range(count) if (i % tensor) >= 2]
    arrived_b = lax.ppermute(pack_b, BOTH, behind)
    dfq, dfk, dva = call(
        local_back_kernel, seqs,
        [("s", fq), ("s", fk), ("s", fql), ("s", fkl), ("s", va), ("s", g), ("s", st), ("s", ccol), ("s", crow), ("s", urow)],
        [("s", feats, F32), ("s", feats, F32), ("s", feats, F32)],
        flops=2 * 6 * 24 * chunk * chunk * 128, name="local_back",
    )
    before_close = []
    if direct:
        g_line = sum_four(g_plane, BF16, after=[dfq])
        before_close = [g_line]
    m00, m01, m10, m11, gn_keep, gn_send = call(
        functools.partial(close_kernel, seqs_total=seqs), seqs,
        [("m", pos), ("s", inputs), ("s", other_in), ("s", attend), ("s", fq), ("s", fk), ("s", va), ("s", dfq),
         ("s", dfk), ("s", dva), ("s", ccol), ("s", ucol), ("w", arrived_b), ("s", l1), ("s", st),
         ("w", wmix), ("w", vec), ("w", grad_vec), ("w", maps_back)]
        + [("d", a) for a in before_close],
        [
            *[("w", (nz, 32, 896), BF16)] * 4, ("s", (seqs, chunk, width), F32), ("s", (seqs, chunk, width), BF16),
        ],
        scratch=[
            pltpu.VMEM((width, 896), F32), pltpu.VMEM((8, 128), F32), pltpu.VMEM((8, width), F32),
            pltpu.VMEM((width, 896), BF16),
        ],
        flops=4 * tokens * width * 896, name="close",
    )
    gn_recv = swap_core(gn_send)
    (input_grad,) = call(
        input_kernel, seqs,
        [("s", inputs), ("s", grad_middle), ("s", gn_keep), ("s", gn_recv), ("w", vec)],
        [("s", (seqs, chunk, width), F32)], name="input_grad",
    )
    if direct:
        m_plane = sum_four(
            [m00, xor_with(m01, 4, count), xor_with(m10, 2, count), xor_with(m11, 6, count)], BF16, carry=True,
            after=[input_grad],
        )
        g_fin = sum_four([g_line[0]] + [xor_with(g_line[m], 8 * m, count) for m in range(1, nz)], F32)
        up_rows = up_weight.shape[0]
        up_grad, down_grad, out_grad = g_fin[:up_rows], g_fin[up_rows : 2 * up_rows].T, g_fin[2 * up_rows :]
        m_mine = sum_four(
            [m_plane[0]] + [xor_with(m_plane[m], 8 * m, count) for m in range(1, nz)], F32, after=[g_fin]
        )
        m_mine = m_mine.reshape(2, 16, 896)
        m_keep = jnp.where(first, m_mine[0], m_mine[1])
        m_recv = swap_core(jnp.where(first, m_mine[1], m_mine[0]))
    else:
        m_all = jnp.stack([jnp.stack([m00, m01]), jnp.stack([m10, m11])])
        mine_rows = m_all.transpose(2, 1, 0, 3, 4).reshape(count, -1, 896).astype(F32)
        keep_part = lax.psum_scatter(mine_rows * jnp.where(first, 1.0, 0.0), BOTH, scatter_dimension=0)
        far_part = lax.psum_scatter(mine_rows * jnp.where(first, 0.0, 1.0), BOTH, scatter_dimension=0)
        m_keep = jnp.where(first, keep_part, far_part)
        m_recv = jnp.where(first, far_part, keep_part)
    m_low = jnp.where(first, m_keep, m_recv)
    m_high = jnp.where(first, m_recv, m_keep)
    mix_grad = jnp.concatenate(
        [part[:, 256 * i : 256 * i + 256] for i in range(3) for part in (m_low, m_high)], axis=1
    )
    gate_grad = jnp.concatenate([m_low[:, 768:772], m_high[:, 768:772]], axis=1)
    bias_grad = jnp.concatenate([m[0, 776:780] + m[0, 780:784] for m in (m_low, m_high)])
    sides = m_keep[:, 772:776] + m_recv[:, 772:776]

    return (
        output, input_grad, mix_grad, gate_grad, bias_grad, out_grad,
        sides[:, 0], sides[:, 1], sides[:, 2], sides[:, 3], up_grad, down_grad,
    )


def solution(mesh):
    rows, spread = P(("dp", "tensor"), None), P(("dp", "tensor"))
    tokens = P("dp", "tensor", None)
    in_specs = (
        tokens, tokens, rows, rows, P(), rows, spread, spread, spread, spread, P("dp", "tensor"), P("tensor", "dp"), P(),
    )
    out_specs = (
        tokens, tokens, rows, rows, P(), rows, spread, spread, spread, spread, P("dp", "tensor"), P("tensor", "dp"),
    )
    return jax.shard_map(body, mesh=mesh, in_specs=in_specs, out_specs=out_specs, check_vma=False)
```

time: 1030 us -> 188 us (0.18)
  waiting for transfers between devices: 324 us -> 39.7 us
  blocking collectives: 246 us -> 0 us
  matrix products: 220 us -> 0 us
  local copies, waits for them, and re-layouts: 122 us -> 15.5 us
  Pallas kernels: 0 us -> 89.3 us
  other arithmetic: 56.9 us -> 2.18 us
  loops' own time: 29.8 us -> 0 us
  starting transfers between devices: 9.77 us -> 39.5 us
  between operations: 15.2 us -> 1.17 us
    reduce_scatter x4 -> x0, waiting for transfers between devices: 292 us -> none  [the longest x1 118 us: body(): lax.psum_scatter(grad_out, ('dp', 'tensor'), scatter_dimension=0, tiled=T...]
    dot_general x62 -> x0, matrix products: 220 us -> none  [the longest x47 169 us: product(): return jnp.einsum(pattern, *operands, precision=HIGHEST)]
    all_gather x7 -> x0, blocking collectives: 165 us -> none  [the longest x1 40.9 us: body(): lax.all_gather(out_weight, ('dp', 'tensor'), axis=0, tiled=True)]
    pallas_call x0 -> x17, Pallas kernels: none -> 89.3 us  [call(): pl.pallas_call(run, in_specs=[spec(kind) for kind in kinds], out_specs=[s...]
    unnamed x1 -> x0, blocking collectives: 42 us -> none
    ppermute x0 -> x37, waiting for transfers between devices: none -> 39.7 us  [the longest x35 35.2 us: xor_with(): return lax.ppermute(a, BOTH, [(i, i ^ mask) for i in range(count)])]
    ppermute x0 -> x37, starting transfers between devices: none -> 39.5 us  [the longest x35 35.6 us: xor_with(): return lax.ppermute(a, BOTH, [(i, i ^ mask) for i in range(count)])]
    psum x1 -> x0, blocking collectives: 38.6 us -> none  [body(): bias_grad = lax.psum(bias_part, ('dp', 'tensor'))]
  transfers between devices with their start and end apart: 12 -> 37, of which waited for: 7 -> 14; matrix products, arithmetic and copies ran while one was open for 10% -> 2% of each run, Pallas kernels for 0% -> 26%
where the time goes in v1:
time: 188 us; the launch traced here: 187 us
  Pallas kernels  89.3 us (48%)
  waiting for transfers between devices  39.7 us (21%)
  starting transfers between devices  39.5 us (21%)
  local copies, waits for them, and re-layouts  15.5 us (8%)
  other arithmetic  2.18 us (1%)
    pallas_call x17, Pallas kernels, call(): pl.pallas_call(run, in_specs=[spec(kind) for kind in kinds], out_specs=[s...  89.3 us
    ppermute x35, starting transfers between devices, xor_with(): return lax.ppermute(a, BOTH, [(i, i ^ mask) for i in range(count)])  35.6 us
    ppermute x35, waiting for transfers between devices, xor_with(): return lax.ppermute(a, BOTH, [(i, i ^ mask) for i in range(count)])  35.2 us
    unnamed x51, local copies, waits for them, and re-layouts  8.57 us
    ppermute x1, waiting for transfers between devices, body(): arrived_b = lax.ppermute(pack_b, BOTH, behind)  4.5 us
  transfers between devices with their start and end apart: 37, of which 14 were waited for; matrix products, arithmetic and copies ran while one was open for 2% of the time, Pallas kernels for 26%

profile of v1, /device:TPU:0, one launch (start us, length us, event | category | flops | bytes accessed | tf_op | source)
XLA Modules:
  0.0 187.3 jit_solution(8590718432684169622)
XLA Ops:
  6.9 2.9 %collective-permute-start.2 = (bf16[2,16,896]{2,1,0:T(8,128)(2,1)S(1)}, bf16[2,16,896]{2,1,0:T(8,128)(2,1)S(1)}, u32[]{:S(2)}, u32[]{:S(2)}) collective-permute-start(bf16[2,16,896]{2,1,0:T(8,128)(2,1)S(1)} %join.3.refs_0_), channel_id=1, source_target_pairs={{0,8},{1,9},{2,10},{3,11},{4,12},{5,13},{6,14},{7,15},{8,0},{9,1},... | collective-permute-start | bytes 172040 | tf_op jit(solution)/shard_map/ppermute | solution.py:568
  9.8 2.6 %collective-permute-start.3 = (bf16[2,16,896]{2,1,0:T(8,128)(2,1)S(1)}, bf16[2,16,896]{2,1,0:T(8,128)(2,1)S(1)}, u32[]{:S(2)}, u32[]{:S(2)}) collective-permute-start(bf16[2,16,896]{2,1,0:T(8,128)(2,1)S(1)} %join.3.refs_0_), channel_id=1, source_target_pairs={{0,16},{1,17},{2,18},{3,19},{4,20},{5,21},{6,22},{7,23},{8,24},{9,... | collective-permute-start | bytes 172040 | tf_op jit(solution)/shard_map/ppermute | solution.py:568
  13.3 2.9 %collective-permute-done.3.refs_2_ = bf16[2,16,896]{2,1,0:T(8,128)(2,1)S(1)} collective-permute-done((bf16[2,16,896]{2,1,0:T(8,128)(2,1)S(1)}, bf16[2,16,896]{2,1,0:T(8,128)(2,1)S(1)}, u32[]{:S(2)}, u32[]{:S(2)}) %collective-permute-start.3) | collective-permute-done | bytes 57376 | tf_op jit(solution)/shard_map/ppermute | solution.py:568
  23.6 2.3 %collective-permute-done.10.refs_1_ = bf16[144,512]{1,0:T(8,128)(2,1)S(1)} collective-permute-done((bf16[144,512]{1,0:T(8,128)(2,1)S(1)}, bf16[144,512]{1,0:T(8,128)(2,1)S(1)}, u32[]{:S(2)}, u32[]{:S(2)}) %collective-permute-start.10) | collective-permute-done | bytes 147488 | tf_op jit(solution)/shard_map/ppermute | solution.py:568
  26.6 2.4 %collective-permute-start.7 = (bf16[4,2,16,896]{3,2,1,0:T(8,128)(2,1)S(1)}, bf16[4,2,16,896]{3,2,1,0:T(8,128)(2,1)S(1)}, u32[]{:S(2)}, u32[]{:S(2)}) collective-permute-start(bf16[4,2,16,896]{3,2,1,0:T(8,128)(2,1)S(1)} %join.4.refs_3_.refs_1_.refs_4_), channel_id=1, source_target_pairs={{0,6},{1,7},{2,4},{3,5},{4,2},{5,3},{6,0},{7,1},{8,14},{9,15},{10,... | collective-permute-start | bytes 688136 | tf_op jit(solution)/shard_map/ppermute | solution.py:568
  30.7 6.1 %collective-permute-done.12.refs_3_ = bf16[144,512]{1,0:T(8,128)(2,1)S(1)} collective-permute-done((bf16[144,512]{1,0:T(8,128)(2,1)S(1)}, bf16[144,512]{1,0:T(8,128)(2,1)S(1)}, u32[]{:S(2)}, u32[]{:S(2)}) %collective-permute-start.12) | collective-permute-done | bytes 147488 | tf_op jit(solution)/shard_map/ppermute | solution.py:568
  39.9 2.4 %collective-permute-start.15 = (bf16[4,144,512]{2,1,0:T(8,128)(2,1)S(1)}, bf16[4,144,512]{2,1,0:T(8,128)(2,1)}, u32[]{:S(2)}, u32[]{:S(2)}) collective-permute-start(bf16[4,144,512]{2,1,0:T(8,128)(2,1)S(1)} %join.5.refs_6_), channel_id=1, source_target_pairs={{0,6},{1,7},{2,4},{3,5},{4,2},{5,3},{6,0},{7,1},{8,14},{9,15},{10,... | collective-permute-start | bytes 1769480 | tf_op jit(solution)/shard_map/ppermute | solution.py:568
  45.6 14.4 %project.1 = (bf16[3,512,512]{2,1,0:T(8,128)(2,1)S(1)}, bf16[3,4,512,128]{3,2,1,0:T(8,128)(2,1)S(1)}, bf16[3,4,512,128]{3,2,1,0:T(8,128)(2,1)S(1)}, bf16[3,4,512...) custom-call(s32[4]{0:T(128)S(1)} %pad_add_fusion.8.refs_0_, ...), custom_call_target="tpu_custom_call" | custom-call | flops 1409286144 | bytes 1000000 | tf_op jit(solution)/shard_map/project/pallas_call | solution.py:555
  60.0 2.6 %collective-permute-start.8 = (bf16[7,128,128]{2,1,0:T(8,128)(2,1)S(1)}, bf16[7,128,128]{2,1,0:T(8,128)(2,1)S(1)}, u32[]{:S(2)}, u32[]{:S(2)}) collective-permute-start(bf16[7,128,128]{2,1,0:T(8,128)(2,1)S(1)} %get-tuple-element.62), channel_id=1, source_target_pairs={{0,2},{1,3},{4,6},{5,7},{8,10},{9,11},{12,14},{13,15},{16,18},{17,... | collective-permute-start | bytes 688136 | tf_op jit(solution)/shard_map/ppermute | solution.py:709
  65.1 6.3 %local.1.refs_1_ = f32[3,4,512,128]{3,2,1,0:T(8,128)S(1)} custom-call(bf16[3,4,512,128]{3,2,1,0:T(8,128)(2,1)S(1)} %get-tuple-element.54.refs_0_.refs_2_.refs_4_, bf16[3,4,512,128]{3,2,1,0:T(8,128)(2,1)S(1)} %get-tuple-element.55.refs_1_.refs_5_, bf16[3,4,512,128]{3,2,1,0:T(8,128)(2,1)S(1)} %get-tuple-element.56.refs_2_, ...), custom_call_target="tpu_custom_call" | custom-call | flops 805306368 | bytes 1000000 | tf_op jit(solution)/shard_map/local/pallas_call | solution.py:555
  71.5 5.2 %finish.1 = (f32[3,4,512,128]{3,2,1,0:T(8,128)S(1)}, bf16[3,4,2,128,128]{4,3,2,1,0:T(8,128)(2,1)S(1)}, bf16[3,256,256]{2,1,0:T(8,128)(2,1)S(1)}, bf16[3,256,256]{2,1,0:T(8,128)(2,1)S(1)}) custom-call(s32[4]{0:T(128)S(1)} %pad_add_fusion.8.refs_0_, f32[3,4,512,128]{3,2,1,0:T(8,128)S(1)} %local.1.refs_1_, ...), custom_call_target="tpu_custom_call" | custom-call | flops 201326592 | bytes 1000000 | tf_op jit(solution)/shard_map/finish/pallas_call | solution.py:555
  78.7 21.5 %feed.1 = (bf16[3,256,512]{2,1,0:T(8,128)(2,1)}, f32[3,256,512]{2,1,0:T(8,128)S(1)}, bf16[3,256,256]{2,1,0:T(8,128)(2,1)S(1)}, bf16[3,256,256]{2,1,0:T(8,128)(2,...) custom-call(s32[4]{0:T(128)S(1)} %pad_add_fusion.8.refs_0_, ...), custom_call_target="tpu_custom_call" | custom-call | flops 9663676416 | bytes 1000000 | tf_op jit(solution)/shard_map/feed/pallas_call | solution.py:555
  100.7 4.0 %collective-permute-done.21.refs_1_ = bf16[2,2,4,144,512]{4,3,2,1,0:T(8,128)(2,1)S(1)} collective-permute-done((bf16[2,2,4,144,512]{4,3,2,1,0:T(8,128)(2,1)S(1)}, bf16[2,2,4,144,512]{4,3,2,1,0:T(8,128)(2,1)S(1)}, u32[]{:S(2)}, u32[]{:S(2)}) %collective-permute-start.21) | collective-permute-done | bytes 2359328 | tf_op jit(solution)/shard_map/ppermute | solution.py:568
  106.7 2.6 %collective-permute-start.24 = (bf16[4,144,512]{2,1,0:T(8,128)(2,1)S(1)}, bf16[4,144,512]{2,1,0:T(8,128)(2,1)S(1)}, u32[]{:S(2)}, u32[]{:S(2)}) collective-permute-start(bf16[4,144,512]{2,1,0:T(8,128)(2,1)S(1)} %get-tuple-element.88), channel_id=1, source_target_pairs={{0,2},{1,3},{2,0},{3,1},{4,6},{5,7},{6,4},{7,5},{8,10},{9,11},{10,... | collective-permute-start | bytes 1769480 | tf_op jit(solution)/shard_map/ppermute | solution.py:568
  109.4 9.6 %adjoint.1 = (bf16[3,4,512,128]{3,2,1,0:T(8,128)(2,1)S(1)}, f32[3,4,128,128]{3,2,1,0:T(8,128)S(1)}, bf16[7,128,128]{2,1,0:T(8,128)(2,1)S(1)}) custom-call(s32[4]{0:T(128)S(1)} %pad_add_fusion.8.refs_0_, bf16[3,256,256]{2,1,0:T(8,128)(2,1)S(1)} %get-tuple-element.71.refs_1_, bf16[3,256,256]{2,1,0:T(8,128)(2,1)S(1)} %collective-permute-done.20.refs_2_, ...), custom_call_target="tpu_custom_call" | custom-call | flops 201326592 | bytes 1000000 | tf_op jit(solution)/shard_map/adjoint/pallas_call | solution.py:555
  120.4 9.4 %local_back.1 = (f32[3,4,512,128]{3,2,1,0:T(8,128)S(1)}, f32[3,4,512,128]{3,2,1,0:T(8,128)S(1)}, f32[3,4,512,128]{3,2,1,0:T(8,128)S(1)}) custom-call(bf16[3,4,512,128]{3,2,1,0:T(8,128)(2,1)S(1)} %get-tuple-element.54.refs_0_.refs_2_.refs_4_, bf16[3,4,512,128]{3,2,1,0:T(8,128)(2,1)S(1)} %get-tuple-element.55.refs_1_.refs_5_, ...), custom_call_target="tpu_custom_call" | custom-call | flops 2415919104 | bytes 1000000 | tf_op jit(solution)/shard_map/local_back/pallas_call | solution.py:555
  129.8 5.6 %collective-permute-done.24.refs_2_ = bf16[4,144,512]{2,1,0:T(8,128)(2,1)S(1)} collective-permute-done((bf16[4,144,512]{2,1,0:T(8,128)(2,1)S(1)}, bf16[4,144,512]{2,1,0:T(8,128)(2,1)S(1)}, u32[]{:S(2)}, u32[]{:S(2)}) %collective-permute-start.24) | collective-permute-done | bytes 589856 | tf_op jit(solution)/shard_map/ppermute | solution.py:568
  135.7 4.5 %collective-permute-done.22.refs_12_ = bf16[7,128,128]{2,1,0:T(8,128)(2,1)S(1)} collective-permute-done((bf16[7,128,128]{2,1,0:T(8,128)(2,1)S(1)}, bf16[7,128,128]{2,1,0:T(8,128)(2,1)S(1)}, u32[]{:S(2)}, u32[]{:S(2)}) %collective-permute-start.22) | collective-permute-done | bytes 229408 | tf_op jit(solution)/shard_map/ppermute | solution.py:782
  140.2 19.3 %close.1 = (bf16[4,32,896]{2,1,0:T(8,128)(2,1)S(1)}, bf16[4,32,896]{2,1,0:T(8,128)(2,1)S(1)}, bf16[4,32,896]{2,1,0:T(8,128)(2,1)S(1)}, bf16[4,32,896]{2,1,0:T(8,...) custom-call(s32[4]{0:T(128)S(1)} %pad_add_fusion.8.refs_0_, ...), custom_call_target="tpu_custom_call" | custom-call | flops 2818572288 | bytes 1000000 | tf_op jit(solution)/shard_map/close/pallas_call | solution.py:555
  160.9 2.2 %collective-permute-start.29 = (bf16[4,32,896]{2,1,0:T(8,128)(2,1)S(1)}, bf16[4,32,896]{2,1,0:T(8,128)(2,1)S(1)}, u32[]{:S(2)}, u32[]{:S(2)}) collective-permute-start(bf16[4,32,896]{2,1,0:T(8,128)(2,1)S(1)} %get-tuple-element.95), channel_id=1, source_target_pairs={{0,6},{1,7},{2,4},{3,5},{4,2},{5,3},{6,0},{7,1},{8,14},{9,15},{10,... | collective-permute-start | bytes 688136 | tf_op jit(solution)/shard_map/ppermute | solution.py:568
  164.9 2.3 %input_grad.1.refs_4_ = f32[3,256,512]{2,1,0:T(8,128)} custom-call(bf16[3,256,512]{2,1,0:T(8,128)(2,1)S(1)} %copy-done.3, f32[3,256,512]{2,1,0:T(8,128)S(1)} %get-tuple-element.69.refs_1_, f32[3,256,512]{2,1,0:T(8,128)S(1)} %get-tuple-element.90.refs_2_, bf16[3,256,512]{2,1,0:T(8,128)(2,1)S(1)} %collective-permute-done.26.refs_3_, ...), custom_call_target="tpu_custom_call" | custom-call | bytes 1000000 | tf_op jit(solution)/shard_map/input_grad/pallas_call | solution.py:555
  169.9 3.6 %collective-permute-done.28.refs_2_ = bf16[4,32,896]{2,1,0:T(8,128)(2,1)S(1)} collective-permute-done((bf16[4,32,896]{2,1,0:T(8,128)(2,1)S(1)}, bf16[4,32,896]{2,1,0:T(8,128)(2,1)S(1)}, u32[]{:S(2)}, u32[]{:S(2)}) %collective-permute-start.28) | collective-permute-done | bytes 229408 | tf_op jit(solution)/shard_map/ppermute | solution.py:568
  177.2 2.5 %collective-permute-start.32 = (bf16[32,896]{1,0:T(8,128)(2,1)S(1)}, bf16[32,896]{1,0:T(8,128)(2,1)S(1)}, u32[]{:S(2)}, u32[]{:S(2)}) collective-permute-start(bf16[32,896]{1,0:T(8,128)(2,1)S(1)} %get-tuple-element.132), channel_id=1, source_target_pairs={{0,24},{1,25},{2,26},{3,27},{4,28},{5,29},{6,30},{7,31},{8,16},{9,... | collective-permute-start | bytes 172040 | tf_op jit(solution)/shard_map/ppermute | solution.py:568
  179.8 3.6 %collective-permute-done.31.refs_2_ = bf16[32,896]{1,0:T(8,128)(2,1)S(1)} collective-permute-done((bf16[32,896]{1,0:T(8,128)(2,1)S(1)}, bf16[32,896]{1,0:T(8,128)(2,1)S(1)}, u32[]{:S(2)}, u32[]{:S(2)}) %collective-permute-start.31) | collective-permute-done | bytes 57376 | tf_op jit(solution)/shard_map/ppermute | solution.py:568
  (154 shorter events, 45.2 us)
Async XLA Ops:
  18.5 10.7 %collective-permute-start.11 = (bf16[144,512]{1,0:T(8,128)(2,1)S(1)}, bf16[144,512]{1,0:T(8,128)(2,1)S(1)}, u32[]{:S(2)}, u32[]{:S(2)}) collective-permute-start(bf16[144,512]{1,0:T(8,128)(2,1)S(1)} %hold.1.refs_0_), channel_id=1, source_target_pairs={{0,16},{1,17},{2,18},{3,19},{4,20},{5,21},{6,22},{7,23},{8,24},{9,... | collective-permute-start | bytes 442376 | tf_op jit(solution)/shard_map/ppermute | solution.py:568
  20.6 22.2 %collective-permute-start = (bf16[3,256,512]{2,1,0:T(8,128)(2,1)S(1)}, bf16[3,256,512]{2,1,0:T(8,128)(2,1)S(1)}, u32[]{:S(2)}, u32[]{:S(2)}) collective-permute-start(bf16[3,256,512]{2,1,0:T(8,128)(2,1)S(1)} %copy-done.3), channel_id=1, source_target_pairs={{0,1},{1,0},{2,3},{3,2},{4,5},{5,4},{6,7},{7,6},{8,9},{9,8},{10,11... | collective-permute-start | bytes 2359304 | tf_op jit(solution)/shard_map/ppermute | solution.py:568
  20.6 16.2 %collective-permute-start.5 = (bf16[4,2,16,896]{3,2,1,0:T(8,128)(2,1)S(1)}, bf16[4,2,16,896]{3,2,1,0:T(8,128)(2,1)S(1)}, u32[]{:S(2)}, u32[]{:S(2)}) collective-permute-start(bf16[4,2,16,896]{3,2,1,0:T(8,128)(2,1)S(1)} %join.4.refs_3_.refs_1_.refs_4_), channel_id=1, source_target_pairs={{0,4},{1,5},{2,6},{3,7},{4,0},{5,1},{6,2},{7,3},{8,12},{9,13},{10,... | collective-permute-start | bytes 688136 | tf_op jit(solution)/shard_map/ppermute | solution.py:568
  22.1 14.7 %collective-permute-start.6 = (bf16[4,2,16,896]{3,2,1,0:T(8,128)(2,1)S(1)}, bf16[4,2,16,896]{3,2,1,0:T(8,128)(2,1)S(1)}, u32[]{:S(2)}, u32[]{:S(2)}) collective-permute-start(bf16[4,2,16,896]{3,2,1,0:T(8,128)(2,1)S(1)} %join.4.refs_3_.refs_1_.refs_4_), channel_id=1, source_target_pairs={{0,2},{1,3},{2,0},{3,1},{4,6},{5,7},{6,4},{7,5},{8,10},{9,11},{10,... | collective-permute-start | bytes 688136 | tf_op jit(solution)/shard_map/ppermute | solution.py:568
  26.6 10.2 %collective-permute-start.7 = (bf16[4,2,16,896]{3,2,1,0:T(8,128)(2,1)S(1)}, bf16[4,2,16,896]{3,2,1,0:T(8,128)(2,1)S(1)}, u32[]{:S(2)}, u32[]{:S(2)}) collective-permute-start(bf16[4,2,16,896]{3,2,1,0:T(8,128)(2,1)S(1)} %join.4.refs_3_.refs_1_.refs_4_), channel_id=1, source_target_pairs={{0,6},{1,7},{2,4},{3,5},{4,2},{5,3},{6,0},{7,1},{8,14},{9,15},{10,... | collective-permute-start | bytes 688136 | tf_op jit(solution)/shard_map/ppermute | solution.py:568
  38.8 23.9 %collective-permute-start.13 = (bf16[4,144,512]{2,1,0:T(8,128)(2,1)S(1)}, bf16[4,144,512]{2,1,0:T(8,128)(2,1)}, u32[]{:S(2)}, u32[]{:S(2)}) collective-permute-start(bf16[4,144,512]{2,1,0:T(8,128)(2,1)S(1)} %join.5.refs_6_), channel_id=1, source_target_pairs={{0,4},{1,5},{2,6},{3,7},{4,0},{5,1},{6,2},{7,3},{8,12},{9,13},{10,... | collective-permute-start | bytes 1769480 | tf_op jit(solution)/shard_map/ppermute | solution.py:568
  39.4 24.8 %collective-permute-start.14 = (bf16[4,144,512]{2,1,0:T(8,128)(2,1)S(1)}, bf16[4,144,512]{2,1,0:T(8,128)(2,1)}, u32[]{:S(2)}, u32[]{:S(2)}) collective-permute-start(bf16[4,144,512]{2,1,0:T(8,128)(2,1)S(1)} %join.5.refs_6_), channel_id=1, source_target_pairs={{0,2},{1,3},{2,0},{3,1},{4,6},{5,7},{6,4},{7,5},{8,10},{9,11},{10,... | collective-permute-start | bytes 1769480 | tf_op jit(solution)/shard_map/ppermute | solution.py:568
  39.9 25.2 %collective-permute-start.15 = (bf16[4,144,512]{2,1,0:T(8,128)(2,1)S(1)}, bf16[4,144,512]{2,1,0:T(8,128)(2,1)}, u32[]{:S(2)}, u32[]{:S(2)}) collective-permute-start(bf16[4,144,512]{2,1,0:T(8,128)(2,1)S(1)} %join.5.refs_6_), channel_id=1, source_target_pairs={{0,6},{1,7},{2,4},{3,5},{4,2},{5,3},{6,0},{7,1},{8,14},{9,15},{10,... | collective-permute-start | bytes 1769480 | tf_op jit(solution)/shard_map/ppermute | solution.py:568
  60.0 11.4 %collective-permute-start.8 = (bf16[7,128,128]{2,1,0:T(8,128)(2,1)S(1)}, bf16[7,128,128]{2,1,0:T(8,128)(2,1)S(1)}, u32[]{:S(2)}, u32[]{:S(2)}) collective-permute-start(bf16[7,128,128]{2,1,0:T(8,128)(2,1)S(1)} %get-tuple-element.62), channel_id=1, source_target_pairs={{0,2},{1,3},{4,6},{5,7},{8,10},{9,11},{12,14},{13,15},{16,18},{17,... | collective-permute-start | bytes 688136 | tf_op jit(solution)/shard_map/ppermute | solution.py:709
  62.6 14.7 %collective-permute-start.16 = (bf16[4,144,512]{2,1,0:T(8,128)(2,1)S(1)}, bf16[4,144,512]{2,1,0:T(8,128)(2,1)S(1)}, u32[]{:S(2)}, u32[]{:S(2)}) collective-permute-start(bf16[4,144,512]{2,1,0:T(8,128)(2,1)S(1)} %join.5.refs_6_), channel_id=1, source_target_pairs={{0,1},{1,0},{2,3},{3,2},{4,5},{5,4},{6,7},{7,6},{8,9},{9,8},{10,11... | collective-permute-start | bytes 1769480 | tf_op jit(solution)/shard_map/ppermute | solution.py:568
  62.7 15.9 %collective-permute-start.17 = (bf16[4,144,512]{2,1,0:T(8,128)(2,1)}, bf16[4,144,512]{2,1,0:T(8,128)(2,1)S(1)}, u32[]{:S(2)}, u32[]{:S(2)}) collective-permute-start(bf16[4,144,512]{2,1,0:T(8,128)(2,1)} %collective-permute-done.13.refs_7_), channel_id=1, source_target_pairs={{0,1},{1,0},{2,3},{3,2},{4,5},{5,4},{6,7},{7,6},{8,9},{9,8},{10,11... | collective-permute-start | bytes 1769480 | tf_op jit(solution)/shard_map/ppermute | solution.py:568
  64.2 14.5 %collective-permute-start.18 = (bf16[4,144,512]{2,1,0:T(8,128)(2,1)}, bf16[4,144,512]{2,1,0:T(8,128)(2,1)S(1)}, u32[]{:S(2)}, u32[]{:S(2)}) collective-permute-start(bf16[4,144,512]{2,1,0:T(8,128)(2,1)} %collective-permute-done.14.refs_8_), channel_id=1, source_target_pairs={{0,1},{1,0},{2,3},{3,2},{4,5},{5,4},{6,7},{7,6},{8,9},{9,8},{10,11... | collective-permute-start | bytes 1769480 | tf_op jit(solution)/shard_map/ppermute | solution.py:568
  65.1 13.5 %collective-permute-start.19 = (bf16[4,144,512]{2,1,0:T(8,128)(2,1)}, bf16[4,144,512]{2,1,0:T(8,128)(2,1)S(1)}, u32[]{:S(2)}, u32[]{:S(2)}) collective-permute-start(bf16[4,144,512]{2,1,0:T(8,128)(2,1)} %collective-permute-done.15.refs_9_), channel_id=1, source_target_pairs={{0,1},{1,0},{2,3},{3,2},{4,5},{5,4},{6,7},{7,6},{8,9},{9,8},{10,11... | collective-permute-start | bytes 1769480 | tf_op jit(solution)/shard_map/ppermute | solution.py:568
  100.6 8.9 %collective-permute-start.20 = (bf16[3,256,256]{2,1,0:T(8,128)(2,1)S(1)}, bf16[3,256,256]{2,1,0:T(8,128)(2,1)S(1)}, u32[]{:S(2)}, u32[]{:S(2)}) collective-permute-start(bf16[3,256,256]{2,1,0:T(8,128)(2,1)S(1)} %get-tuple-element.72), channel_id=1, source_target_pairs={{0,1},{1,0},{2,3},{3,2},{4,5},{5,4},{6,7},{7,6},{8,9},{9,8},{10,11... | collective-permute-start | bytes 1179656 | tf_op jit(solution)/shard_map/ppermute | solution.py:568
  105.3 24.6 %collective-permute-start.23 = (bf16[4,144,512]{2,1,0:T(8,128)(2,1)S(1)}, bf16[4,144,512]{2,1,0:T(8,128)(2,1)S(1)}, u32[]{:S(2)}, u32[]{:S(2)}) collective-permute-start(bf16[4,144,512]{2,1,0:T(8,128)(2,1)S(1)} %get-tuple-element.87), channel_id=1, source_target_pairs={{0,4},{1,5},{2,6},{3,7},{4,0},{5,1},{6,2},{7,3},{8,12},{9,13},{10,... | collective-permute-start | bytes 1769480 | tf_op jit(solution)/shard_map/ppermute | solution.py:568
  106.7 28.7 %collective-permute-start.24 = (bf16[4,144,512]{2,1,0:T(8,128)(2,1)S(1)}, bf16[4,144,512]{2,1,0:T(8,128)(2,1)S(1)}, u32[]{:S(2)}, u32[]{:S(2)}) collective-permute-start(bf16[4,144,512]{2,1,0:T(8,128)(2,1)S(1)} %get-tuple-element.88), channel_id=1, source_target_pairs={{0,2},{1,3},{2,0},{3,1},{4,6},{5,7},{6,4},{7,5},{8,10},{9,11},{10,... | collective-permute-start | bytes 1769480 | tf_op jit(solution)/shard_map/ppermute | solution.py:568
  109.3 26.1 %collective-permute-start.25 = (bf16[4,144,512]{2,1,0:T(8,128)(2,1)S(1)}, bf16[4,144,512]{2,1,0:T(8,128)(2,1)S(1)}, u32[]{:S(2)}, u32[]{:S(2)}) collective-permute-start(bf16[4,144,512]{2,1,0:T(8,128)(2,1)S(1)} %get-tuple-element.89), channel_id=1, source_target_pairs={{0,6},{1,7},{2,4},{3,5},{4,2},{5,3},{6,0},{7,1},{8,14},{9,15},{10,... | collective-permute-start | bytes 1769480 | tf_op jit(solution)/shard_map/ppermute | solution.py:568
  119.1 21.2 %collective-permute-start.22 = (bf16[7,128,128]{2,1,0:T(8,128)(2,1)S(1)}, bf16[7,128,128]{2,1,0:T(8,128)(2,1)S(1)}, u32[]{:S(2)}, u32[]{:S(2)}) collective-permute-start(bf16[7,128,128]{2,1,0:T(8,128)(2,1)S(1)} %get-tuple-element.83), channel_id=1, source_target_pairs={{2,0},{3,1},{6,4},{7,5},{10,8},{11,9},{14,12},{15,13},{18,16},{19,... | collective-permute-start | bytes 688136 | tf_op jit(solution)/shard_map/ppermute | solution.py:782
  159.6 8.5 %collective-permute-start.27 = (bf16[4,32,896]{2,1,0:T(8,128)(2,1)S(1)}, bf16[4,32,896]{2,1,0:T(8,128)(2,1)S(1)}, u32[]{:S(2)}, u32[]{:S(2)}) collective-permute-start(bf16[4,32,896]{2,1,0:T(8,128)(2,1)S(1)} %get-tuple-element.93), channel_id=1, source_target_pairs={{0,4},{1,5},{2,6},{3,7},{4,0},{5,1},{6,2},{7,3},{8,12},{9,13},{10,... | collective-permute-start | bytes 688136 | tf_op jit(solution)/shard_map/ppermute | solution.py:568
  160.9 12.6 %collective-permute-start.28 = (bf16[4,32,896]{2,1,0:T(8,128)(2,1)S(1)}, bf16[4,32,896]{2,1,0:T(8,128)(2,1)S(1)}, u32[]{:S(2)}, u32[]{:S(2)}) collective-permute-start(bf16[4,32,896]{2,1,0:T(8,128)(2,1)S(1)} %get-tuple-element.94), channel_id=1, source_target_pairs={{0,2},{1,3},{2,0},{3,1},{4,6},{5,7},{6,4},{7,5},{8,10},{9,11},{10,... | collective-permute-start | bytes 688136 | tf_op jit(solution)/shard_map/ppermute | solution.py:568
  160.9 12.6 %collective-permute-start.29 = (bf16[4,32,896]{2,1,0:T(8,128)(2,1)S(1)}, bf16[4,32,896]{2,1,0:T(8,128)(2,1)S(1)}, u32[]{:S(2)}, u32[]{:S(2)}) collective-permute-start(bf16[4,32,896]{2,1,0:T(8,128)(2,1)S(1)} %get-tuple-element.95), channel_id=1, source_target_pairs={{0,6},{1,7},{2,4},{3,5},{4,2},{5,3},{6,0},{7,1},{8,14},{9,15},{10,... | collective-permute-start | bytes 688136 | tf_op jit(solution)/shard_map/ppermute | solution.py:568
  163.2 14.0 %collective-permute-start.33 = (bf16[144,512]{1,0:T(8,128)(2,1)S(1)}, bf16[144,512]{1,0:T(8,128)(2,1)S(1)}, u32[]{:S(2)}, u32[]{:S(2)}) collective-permute-start(bf16[144,512]{1,0:T(8,128)(2,1)S(1)} %get-tuple-element.128), channel_id=1, source_target_pairs={{0,8},{1,9},{2,10},{3,11},{4,12},{5,13},{6,14},{7,15},{8,0},{9,1},... | collective-permute-start | bytes 442376 | tf_op jit(solution)/shard_map/ppermute | solution.py:568
  163.4 16.3 %collective-permute-start.34 = (bf16[144,512]{1,0:T(8,128)(2,1)S(1)}, bf16[144,512]{1,0:T(8,128)(2,1)S(1)}, u32[]{:S(2)}, u32[]{:S(2)}) collective-permute-start(bf16[144,512]{1,0:T(8,128)(2,1)S(1)} %get-tuple-element.127), channel_id=1, source_target_pairs={{0,16},{1,17},{2,18},{3,19},{4,20},{5,21},{6,22},{7,23},{8,24},{9,... | collective-permute-start | bytes 442376 | tf_op jit(solution)/shard_map/ppermute | solution.py:568
  168.0 11.6 %collective-permute-start.35 = (bf16[144,512]{1,0:T(8,128)(2,1)S(1)}, bf16[144,512]{1,0:T(8,128)(2,1)S(1)}, u32[]{:S(2)}, u32[]{:S(2)}) collective-permute-start(bf16[144,512]{1,0:T(8,128)(2,1)S(1)} %get-tuple-element.126), channel_id=1, source_target_pairs={{0,24},{1,25},{2,26},{3,27},{4,28},{5,29},{6,30},{7,31},{8,16},{9,... | collective-permute-start | bytes 442376 | tf_op jit(solution)/shard_map/ppermute | solution.py:568
  (34 other events, 232.9 us)

commit v2 on v1

v2 whole, which is shorter than its diff:
```python
import functools

import jax
import jax.numpy as jnp
from jax import lax
from jax.experimental import pallas as pl
from jax.experimental.pallas import tpu as pltpu
from jax.sharding import PartitionSpec as P

BOTH = ("dp", "tensor")
F32 = jnp.float32
BF16 = jnp.bfloat16
EPSILON = 1e-05
DENSITY = 0.3989422804014327
SIN = (9.9999999998e-01, -1.6666666617e-01, 8.3333309689e-03, -1.9840860382e-04, 2.7525224003e-06, -2.3888330913e-08)
COS = (9.9999999978e-01, -4.9999999354e-01, 4.1666636104e-02, -1.3888359409e-03, 2.4760057595e-05, -2.6049626765e-07)

NN = (((1,), (0,)), ((), ()))
NT = (((1,), (1,)), ((), ()))
TN = (((0,), (0,)), ((), ()))


def mm(a, b, dims=NN):
    return lax.dot_general(a, b, dims, preferred_element_type=F32)


def low(a):
    return a.astype(BF16)


def lanes_of(shape):
    return lax.broadcasted_iota(jnp.int32, shape, len(shape) - 1)


def swap_halves(a):
    return pltpu.roll(a, 64, 1)


def sincos(a):
    turns = jnp.floor(a * 0.3183098861837907 + 0.5)
    r = (a - turns * 3.140625) - turns * 9.676535897932e-4
    half = turns * 0.5
    sign = 1.0 - 4.0 * (half - jnp.floor(half))
    r2 = r * r
    s = r * (SIN[0] + r2 * (SIN[1] + r2 * (SIN[2] + r2 * (SIN[3] + r2 * (SIN[4] + r2 * SIN[5])))))
    c = COS[0] + r2 * (COS[1] + r2 * (COS[2] + r2 * (COS[3] + r2 * (COS[4] + r2 * COS[5]))))
    return sign * s, sign * c


def normal_parts(v):
    t = pl.reciprocal(1.0 + 0.23164189 * jnp.abs(v), approx=True)
    bell = jnp.exp(-0.5 * (v * v))
    poly = t * (0.127414796 + t * (-0.142248368 + t * (0.7107068705 + t * (-0.7265760135 + t * 0.5307027145))))
    tail = poly * bell
    return jnp.where(v >= 0.0, 1.0 - tail, tail), DENSITY * bell


def three_parts(a):
    high = a.astype(BF16)
    rest = a - high.astype(F32)
    mid = rest.astype(BF16)
    return high, mid, (rest - mid.astype(F32)).astype(BF16)


def tri_sum(tri, a):
    high, mid, rest = (part.astype(F32) for part in three_parts(a))
    packed = mm(tri, low(high + pltpu.roll(mid, 4, 1) + pltpu.roll(rest, 8, 1)))
    return packed + pltpu.roll(packed, 124, 1) + pltpu.roll(packed, 120, 1)


def norm_of(x):
    mean = jnp.mean(x, axis=-1, keepdims=True)
    centered = x - mean
    inv = lax.rsqrt(jnp.mean(centered * centered, axis=-1, keepdims=True) + EPSILON)
    return centered * inv, inv


def norm_back(s, unit, inv):
    return inv * (
        s
        - jnp.mean(s, axis=-1, keepdims=True)
        - unit * jnp.mean(s * unit, axis=-1, keepdims=True)
    )


def chip_row(pos, mz, mx, my):
    return (((pos[0] ^ mz) * 2 + (pos[1] ^ mx)) * 2 + (pos[2] ^ my)) * 32


def lower_tri(n):
    row = lax.broadcasted_iota(jnp.int32, (n, n), 0)
    col = lax.broadcasted_iota(jnp.int32, (n, n), 1)
    return row, col


def unpack_states(pack, b, zcols, last=65):
    lane = lanes_of((128, 128))
    out = []
    for p in range(2):
        both = pack[2 * b + p].astype(F32)
        for h, mat in ((2 * p, both), (2 * p + 1, swap_halves(both))):
            z = jnp.sum(jnp.where(lane == 4 * b + h, zcols, 0.0), axis=1, keepdims=True)
            out.append(jnp.where(lane < 64, mat, jnp.where(lane <= last, z, 0.0)))
    return out


def pack_states(states, pack_o, b, last, split=False):
    lane = lanes_of((128, 128))
    zcols = jnp.where(b == 0, 0.0, pack_o[last].astype(F32))

    def sum_of(s):
        return s[:, 64:65] + s[:, 65:66] if split else s[:, 64:65]

    for p in range(2):
        s0, s1 = states[2 * p], states[2 * p + 1]
        pack_o[2 * b + p] = jnp.where(lane < 64, s0, swap_halves(s1)).astype(BF16)
        zcols = jnp.where(lane == 4 * b + 2 * p, sum_of(s0), zcols)
        zcols = jnp.where(lane == 4 * b + 2 * p + 1, sum_of(s1), zcols)
    pack_o[last] = zcols.astype(BF16)


def pack_kernel(pos, mix, side, keep_o, send_o):
    width = mix.shape[1] // 6
    lane = lanes_of(side.shape)
    sides = side[...].astype(F32)
    moved = pltpu.roll(sides, 124, 1)
    halves = []
    for s, block in ((0, jnp.where(lane < 4, sides, moved)), (1, moved)):
        parts = [mix[:, (2 * i + s) * width : (2 * i + s + 1) * width] for i in range(3)]
        halves.append(jnp.concatenate(parts + [low(jnp.where(lane < 8, block, 0.0))], axis=1))
    first = pos[3] == 0
    keep_o[...] = jnp.where(first, halves[0], halves[1])
    send_o[...] = jnp.where(first, halves[1], halves[0])


def prepare_kernel(b, pos, own, oth, cot, unit_o, cott_o):
    chunk = own.shape[1]
    first = pos[3] == 0
    mine, theirs = own[0], oth[0]
    for j in range(2):
        unit, _ = norm_of(jnp.where(first == (j == 0), mine, theirs).astype(F32))
        unit_o[0, j * chunk : (j + 1) * chunk] = unit
    cott_o[0] = low(cot[0].astype(F32).T)


def project_kernel(
    b, pos, units, w0, w1, w2, w3, bias, maps,
    a_o, fq_o, fk_o, fql_o, fkl_o, va_o, ccol_o, ucol_o, crow_o, smid_o, pack_o, wmix_o, vec_o, vbar_o,
    w_s, sems,
):
    chunk = units.shape[1] // 2

    @pl.when(b == 0)
    def _():
        copies = [
            pltpu.make_async_copy(piece, w_s.at[:, pos[1] ^ mx, pos[2] ^ my], sems.at[2 * my + mx])
            for piece, (my, mx) in ((w0, (0, 0)), (w1, (0, 1)), (w2, (1, 0)), (w3, (1, 1)))
        ]
        for copy in copies:
            copy.start()
        for copy in copies:
            copy.wait()
        wmix_o[...] = w_s[...].reshape(wmix_o.shape)
        vec_o[...] = wmix_o[:, 768:896].astype(F32).T[0:8]
        vbar_o[...] = mm(jnp.broadcast_to(vec_o[5:6], vec_o.shape).astype(BF16), wmix_o[:, 512:768])

    gain, shift = vec_o[4:5], vec_o[5:6]
    row, col = lower_tri(chunk)
    tri = jnp.where(row >= col, 1.0, 0.0).astype(BF16)
    lane = lanes_of((chunk, 128))
    spans = [slice(j * chunk, (j + 1) * chunk) for j in range(2)]
    attends = [low(units[0, rows] * gain + shift) for rows in spans]
    for a, rows in zip(attends, spans):
        a_o[0, rows] = a
    wide = [mm(a, wmix_o[...]) for a in attends]
    mixed = [low(m[:, 0:768]) for m in wide]
    angles = [
        [mm(m[:, base : base + 128], maps[p]) for base, p in ((0, 0), (128, 1), (256, 0), (384, 1))] for m in mixed
    ]
    douts, ends = [], []
    for j, rows in enumerate(spans):
        logits = wide[j][:, 768:896] + bias[...]
        e = jnp.exp(-jnp.abs(logits))
        w = 1.0 + e
        log1 = jnp.where(w == 1.0, e, jnp.log(w) * (e / jnp.where(w == 1.0, 1.0, w - 1.0)))
        log_gate = jnp.where(lane < 4, jnp.minimum(logits, 0.0) - log1, 0.0)
        fresh = jnp.where(lane < 4, jnp.where(logits >= 0.0, e, 1.0) / w, 0.0)
        cum = jnp.where(lane < 4, tri_sum(tri, log_gate), 0.0)
        ccol_o[0, rows] = cum
        ucol_o[0, rows] = fresh
        crow_o[0, j] = (cum + pltpu.roll(fresh, 4, 1)).T[0:8]
        ends.append(cum[chunk - 1 : chunk])
        douts.append(jnp.exp(ends[j] - cum) * fresh)
    one = jnp.where((lane == 64) | (lane == 65), 1.0, 0.0)
    shares = [[None] * 4, [None] * 4]
    for j, rows in enumerate(spans):
        for p in range(2):
            v = mixed[j][:, 512 + 128 * p : 640 + 128 * p].astype(F32) - vbar_o[0:1, 128 * p : 128 * p + 128]
            for h, vh in ((2 * p, v), (2 * p + 1, swap_halves(v))):
                aug = jnp.where(lane < 64, vh, one)
                va_o[0, h, rows] = low(aug)
                shares[j][h] = low(aug * douts[j][:, h : h + 1])
    locals_ = [[None] * 4, [None] * 4]
    for base, target, rest in ((2, fk_o, fkl_o), (0, fq_o, fql_o)):
        for j, rows in enumerate(spans):
            for p in range(2):
                s, c = sincos(angles[j][base + p])
                for h, f in (
                    (2 * p, jnp.where(lane < 64, s, swap_halves(c))),
                    (2 * p + 1, jnp.where(lane < 64, swap_halves(s), c)),
                ):
                    high = low(f)
                    target[0, h, rows] = high
                    rest[0, h, rows] = low(f - high.astype(F32))
                    if base == 2:
                        locals_[j][h] = mm(high, shares[j][h], TN)
    states = []
    for h in range(4):
        smid_o[0, h] = locals_[0][h]
        states.append(locals_[0][h] * jnp.exp(ends[1][:, h : h + 1]) + locals_[1][h])
    pack_states(states, pack_o, b, pack_o.shape[0] - 1)


def weights_of(ccol, ucol_row, crow, row, col):
    gap = jnp.minimum(ccol - crow, 0.0)
    return jnp.where(row >= col, jnp.exp(gap), 0.0) * ucol_row


def pairs_of(chunk):
    return [(j, h, slice(j * chunk, (j + 1) * chunk)) for j in range(2) for h in range(4)]


def scores(fq, fk, fql, fkl, h, rows):
    q, k = fq[0, h, rows], fk[0, h, rows]
    return mm(
        jnp.concatenate([q, fql[0, h, rows], q], axis=1), jnp.concatenate([k, k, fkl[0, h, rows]], axis=1), NT
    )


def local_kernel(b, fq, fk, fql, fkl, va, ccol, crow, o_o):
    chunk = crow.shape[3]
    row, col = lower_tri(chunk)
    pairs = pairs_of(chunk)
    qk = [scores(fq, fk, fql, fkl, h, rows) for j, h, rows in pairs]
    attn = [
        low(q * weights_of(ccol[0, rows, h : h + 1], crow[0, j, 4 + h : 5 + h], crow[0, j, h : h + 1], row, col))
        for q, (j, h, rows) in zip(qk, pairs)
    ]
    outs = [mm(a, va[0, h, rows]) for a, (j, h, rows) in zip(attn, pairs)]
    for out, (j, h, rows) in zip(outs, pairs):
        o_o[0, h, rows] = out


def mean_of(vbar, h):
    pair = vbar[:, 128 * (h // 2) : 128 * (h // 2) + 128]
    return (pair if h % 2 == 0 else swap_halves(pair))[0:1]


def finish_kernel(b, pos, o_loc, fq, ccol, pack, smid, vbar, inv_o, turn_o, st_o, keep_o, send_o):
    chunk = ccol.shape[1] // 2
    zcols = pack[pack.shape[0] - 1].astype(F32)
    states = unpack_states(pack, b, zcols)
    lane = lanes_of((chunk, 128))
    cend = ccol[0, chunk - 1 : chunk]
    pairs = pairs_of(chunk)
    near = []
    for h in range(4):
        near.append(low(states[h]))
        near.append(low(jnp.exp(cend[:, h : h + 1]) * states[h] + smid[0, h]))
        for j in range(2):
            st_o[0, h, j] = near[2 * h + j]
    inter = [mm(fq[0, h, rows], near[2 * h + j]) for j, h, rows in pairs]
    outs = [
        o_loc[0, h, rows] + jnp.exp(ccol[0, rows, h : h + 1]) * part for part, (j, h, rows) in zip(inter, pairs)
    ]
    dens = [jnp.broadcast_to(o[:, 64:65], o.shape) for o in outs]
    invs = [lax.rsqrt(den * den + 1.0) for den in dens]
    att = [[None] * 4, [None] * 4]
    for o, den, inv, (j, h, rows) in zip(outs, dens, invs, pairs):
        mean = mean_of(vbar, h)
        att[j][h] = (o + den * mean) * inv
        inv_o[0, h, rows] = jnp.where(lane < 64, inv, 0.0)
        turn_o[0, h, rows] = mean - den * inv * att[j][h]
    first = pos[3] == 0
    for p in range(2):
        both = [
            jnp.where(lane < 64, att[j][2 * p], swap_halves(att[j][2 * p + 1])) for j in range(2)
        ]
        keep_o[0, :, 128 * p : 128 * p + 128] = jnp.where(first, both[0], both[1]).astype(BF16)
        send_o[0, :, 128 * p : 128 * p + 128] = jnp.where(first, both[1], both[0]).astype(BF16)


def dp_of(pos, mz, mx):
    return (pos[0] ^ mz) * 2 + (pos[1] ^ mx)


def feed_chunks(pos, near, far, cot, cott, feed, feedt, target, up_s, dn_s, hid_s, gp_s, big_s):
    seqs, chunk, _ = cot.shape
    nz = far.shape[0]
    width, both = up_s.shape
    hidden = both // 2
    rows_up = width // (2 * nz)
    for my in range(2):
        cols = slice(my * hidden, (my + 1) * hidden)
        for mx in range(2):
            k = 2 * my + mx
            piece = far if k == 3 else near.at[pl.ds(k * nz, nz)]
            for z in range(nz):
                at = pl.multiple_of((2 * z + (pos[1] ^ mx)) * rows_up, rows_up)
                up_s[pl.ds(at, rows_up), cols] = piece[z, 0:rows_up]
                dn_s[pl.ds(at, rows_up), cols] = piece[z, rows_up : 2 * rows_up]

    def scatter(offset):
        for my in range(2):
            cols = slice(my * hidden, (my + 1) * hidden)
            for mx in range(2):
                for mz in range(nz):
                    at = pl.multiple_of(dp_of(pos, mz, mx) * rows_up, rows_up)
                    target[my, mx, mz, offset : offset + rows_up, :] = big_s[pl.ds(at, rows_up), cols]

    spans = [slice(r * chunk, (r + 1) * chunk) for r in range(seqs)]
    outs, grads = [], []
    for r, rows in enumerate(spans):
        pre = mm(feed[rows], up_s[...])
        gh = mm(cot[r], dn_s[...])
        cdf, pdf = normal_parts(pre)
        hid_s[rows] = low(pre * cdf)
        gp_s[rows] = low(gh * (cdf + pre * pdf))
    for rows in spans:
        outs.append(mm(hid_s[rows], dn_s[...], NT))
        grads.append(mm(gp_s[rows], up_s[...], NT))
    big_s[...] = low(mm(feedt[...], gp_s[...]))
    scatter(0)
    big_s[...] = low(mm(jnp.concatenate([cott[r] for r in range(seqs)], axis=1), hid_s[...]))
    scatter(rows_up)
    return outs, grads


def feed_first_kernel(
    pos, akeep, arecv, x, cot, cott, vec, near_own, far_own, near, far,
    gsend_o, acc_o, gf_o, mid_o, feed_o, feedt_o, att_o, ow_o,
    up_s, dn_s, hid_s, gp_s, big_s,
):
    seqs, chunk, _ = x.shape
    nz = far.shape[0]
    rows_up = up_s.shape[0] // (2 * nz)
    first = pos[3] == 0
    for mc, (some, rest) in enumerate(((near_own, far_own), (near, far))):
        for my in range(2):
            t = (pos[2] ^ my) * 2 + (pos[3] ^ mc)
            for mx in range(2):
                k = 2 * my + mx
                for z in range(nz):
                    at = pl.multiple_of(((2 * z + (pos[1] ^ mx)) * 4 + t) * 16, 16)
                    source = rest if k == 3 else some.at[pl.ds(k * nz, nz)]
                    ow_o[pl.ds(at, 16), :] = source[z, 2 * rows_up :]
    gain, shift = vec[6:7], vec[7:8]
    for r in range(seqs):
        rows = slice(r * chunk, (r + 1) * chunk)
        mine, theirs = akeep[r], arecv[r]
        att = jnp.concatenate([jnp.where(first, mine, theirs), jnp.where(first, theirs, mine)], axis=1)
        att_o[rows] = att
        mid = x[r].astype(F32) + mm(att, ow_o[...])
        mid_o[rows] = mid
        unit, _ = norm_of(mid)
        feed = unit * gain + shift
        feed_o[rows] = low(feed)
        feedt_o[:, rows] = low(feed.T)
    outs, grads = feed_chunks(pos, near, far, cot, cott, feed_o, feedt_o, gsend_o, up_s, dn_s, hid_s, gp_s, big_s)
    for r, (out, grad) in enumerate(zip(outs, grads)):
        acc_o[r * chunk : (r + 1) * chunk] = out
        gf_o[r * chunk : (r + 1) * chunk] = grad


def feed_second_kernel(
    pos, cot, cott, vec, near, far, acc, gf_in, mid_in, feed, feedt, att, ow,
    out_o, gm_o, gak_o, gas_o, gkeep_o, okeep_o, osend_o, gv_o,
    up_s, dn_s, hid_s, gp_s, gb_s, big_s,
):
    seqs, chunk, width = cot.shape
    nz = far.shape[0]
    first = pos[3] == 0
    outs, grads = feed_chunks(pos, near, far, cot, cott, feed, feedt, gkeep_o, up_s, dn_s, hid_s, gp_s, big_s)
    gain = vec[6:7]
    gain_sum = jnp.zeros((1, width), F32)
    shift_sum = jnp.zeros((1, width), F32)
    for r in range(seqs):
        rows = slice(r * chunk, (r + 1) * chunk)
        mid = mid_in[rows]
        out_o[r] = low(mid + (acc[rows] + outs[r]))
        unit, inv = norm_of(mid)
        gf = gf_in[rows] + grads[r]
        gain_sum += jnp.sum(gf * unit, axis=0, keepdims=True)
        shift_sum += jnp.sum(gf, axis=0, keepdims=True)
        gm = cot[r].astype(F32) + norm_back(gf * gain, unit, inv)
        gm_o[r] = gm
        gb = low(gm)
        gb_s[rows] = gb
        ga = low(mm(gb, ow[...], NT))
        half = width // 2
        gak_o[r] = jnp.where(first, ga[:, :half], ga[:, half:])
        gas_o[r] = jnp.where(first, ga[:, half:], ga[:, :half])
    gv_o[...] = jnp.concatenate([gain_sum, shift_sum, jnp.zeros((6, width), F32)], axis=0)
    big_s[:, 0:width] = low(mm(att[...], gb_s[...], TN))
    for mc, target in ((0, okeep_o), (1, osend_o)):
        for my in range(2):
            t = (pos[2] ^ my) * 2 + (pos[3] ^ mc)
            for mx in range(2):
                for mz in range(nz):
                    at = pl.multiple_of((dp_of(pos, mz, mx) * 4 + t) * 16, 16)
                    target[my, mx, mz] = big_s[pl.ds(at, 16), 0:width]


def adjoint_kernel(b, pos, gak, gar, inv_root, turn, fq, ccol, g_o, scaled_o, l1_o, pack_o):
    chunk = ccol.shape[1] // 2
    lane = lanes_of((chunk, 128))
    first = pos[3] == 0
    pairs = pairs_of(chunk)
    gas = []
    for j in range(2):
        for p in range(2):
            cols = slice(128 * p, 128 * p + 128)
            pair = jnp.where(first == (j == 0), gak[0, :, cols], gar[0, :, cols]).astype(F32)
            gas += [pair, swap_halves(pair)]
    gns = [low(ga * inv_root[0, h, rows]).astype(F32) for ga, (j, h, rows) in zip(gas, pairs)]
    gds = [
        jnp.sum(gn * turn[0, h, rows], axis=1, keepdims=True) for gn, (j, h, rows) in zip(gns, pairs)
    ]
    scaled = []
    for gn, gd, (j, h, rows) in zip(gns, gds, pairs):
        gd = jnp.broadcast_to(gd, gn.shape)
        high = low(gd).astype(F32)
        g = jnp.where(lane == 64, high, jnp.where(lane == 65, gd - high, gn))
        g_o[0, h, rows] = low(g)
        scaled.append(low(g * jnp.exp(ccol[0, rows, h : h + 1])))
        scaled_o[0, h, rows] = scaled[-1]
    parts = [mm(fq[0, h, rows], g, TN) for g, (j, h, rows) in zip(scaled, pairs)]
    states = []
    for h in range(4):
        l1_o[0, h] = parts[4 + h]
        states.append(parts[h] + jnp.exp(ccol[0, chunk - 1 : chunk, h : h + 1]) * parts[4 + h])
    pack_states(states, pack_o, b, pack_o.shape[0] - 1, split=True)


def local_back_kernel(b, fq, fk, va, g, scaled, st, ccol, crow, dfq_o, dfk_o, dva_o):
    chunk = crow.shape[3]
    row, col = lower_tri(chunk)
    pairs = pairs_of(chunk)
    for half in (pairs[:4], pairs[4:]):
        qk = [mm(fq[0, h, rows], fk[0, h, rows], NT) for j, h, rows in half]
        da = [mm(g[0, h, rows], va[0, h, rows], NT) for j, h, rows in half]
        inter = [mm(scaled[0, h, rows], st[0, h, j], NT) for j, h, rows in half]
        attn, dp = [], []
        for q, d, (j, h, rows) in zip(qk, da, half):
            w = weights_of(ccol[0, rows, h : h + 1], crow[0, j, 4 + h : 5 + h], crow[0, j, h : h + 1], row, col)
            attn.append(low(q * w))
            dp.append(low(d * w))
        dva = [mm(a, g[0, h, rows], TN) for a, (j, h, rows) in zip(attn, half)]
        dfk = [mm(d, fq[0, h, rows], TN) for d, (j, h, rows) in zip(dp, half)]
        dfq = [mm(d, fk[0, h, rows]) for d, (j, h, rows) in zip(dp, half)]
        for i, (j, h, rows) in enumerate(half):
            dfq_o[0, h, rows] = dfq[i] + inter[i]
            dfk_o[0, h, rows] = dfk[i]
            dva_o[0, h, rows] = dva[i]


def close_kernel(
    b, pos, units, attend, fq, fk, va, dfq, dfk, dva, ccol, ucol, pack, l1, st, wmix, gv, back,
    m00_o, m01_o, m10_o, m11_o, gnk_o, gns_o,
    acc_s, gm_s, gate_s, vsum_s, big_s,
    *, seqs_total,
):
    seqs = seqs_total
    chunk = units.shape[1] // 2
    nz = m00_o.shape[0]
    lane = lanes_of((chunk, 128))
    row, col = lower_tri(chunk)
    upper = jnp.where(row <= col, 1.0, 0.0).astype(BF16)
    zcols = pack[pack.shape[0] - 1].astype(F32)
    arrived = unpack_states(pack, b, zcols, last=64)
    wide = lanes_of((128, 128))

    @pl.when(b == 0)
    def _():
        gate_s[...] = jnp.zeros_like(gate_s)
        vsum_s[...] = jnp.zeros_like(vsum_s)

    pairs = pairs_of(chunk)
    spans = [slice(j * chunk, (j + 1) * chunk) for j in range(2)]
    cums = [ccol[0, rows] for rows in spans]
    freshs = [ucol[0, rows] for rows in spans]
    douts = [jnp.exp(cum[chunk - 1 : chunk] - cum) * fresh for cum, fresh in zip(cums, freshs)]
    nears = []
    for j, h, rows in pairs:
        adj = arrived[h]
        if j == 0:
            adj = l1[0, h] + jnp.exp(ccol[0, 2 * chunk - 1 : 2 * chunk, h : h + 1]) * adj
        zs = adj[:, 64:65] + adj[:, 65:66]
        high = low(zs).astype(F32)
        nears.append(low(jnp.where(wide == 64, high, jnp.where(wide == 65, zs - high, adj))))
    dk_fars = [mm(va[0, h, rows], near, NT) for near, (j, h, rows) in zip(nears, pairs)]
    dv_fars = [mm(fk[0, h, rows], near) for near, (j, h, rows) in zip(nears, pairs)]
    kds, qds, levels = [], [], []
    pqs, pks, dvs = [], [], []
    for i, (j, h, rows) in enumerate(pairs):
        d = douts[j][:, h : h + 1]
        keys, queries = fk[0, h, rows].astype(F32), fq[0, h, rows].astype(F32)
        dk_far = d * dk_fars[i]
        kd_far = jnp.sum(keys * dk_far, axis=1, keepdims=True)
        dk = dk_far + dfk[0, h, rows]
        dq = dfq[0, h, rows]
        kds.append(jnp.sum(keys * dk, axis=1, keepdims=True))
        qds.append(jnp.sum(queries * dq, axis=1, keepdims=True))
        passed = st[0, h, j].astype(F32) * nears[i].astype(F32)
        passed = jnp.sum(jnp.sum(passed, axis=0, keepdims=True), axis=1, keepdims=True)
        total = jnp.sum(kd_far, axis=0, keepdims=True)
        levels.append(total + jnp.exp(cums[j][chunk - 1 : chunk, h : h + 1]) * passed)
        dvs.append(dva[0, h, rows] + d * dv_fars[i])
        pks.append(low(dk * swap_halves(keys)))
        pqs.append(low(dq * swap_halves(queries)))
    grads = [
        [mm(jnp.concatenate(ps[4 * j + 2 * p : 4 * j + 2 * p + 2], axis=1), back[p]) for ps in (pqs, pks) for p in range(2)]
        for j in range(2)
    ]
    bias_sum = jnp.zeros((1, 128), F32)
    gms = []
    for j in range(2):
        kd = qd = jnp.zeros((chunk, 128), F32)
        level = jnp.zeros((1, 128), F32)
        for h in range(4):
            kd = jnp.where(lane == h, kds[4 * j + h], kd)
            qd = jnp.where(lane == h, qds[4 * j + h], qd)
            level = jnp.where(lanes_of((1, 128)) == h, levels[4 * j + h], level)
        dlog = tri_sum(upper, qd - kd) + level
        dlogit = jnp.where(lane < 4, freshs[j] * dlog - (1.0 - freshs[j]) * kd, 0.0)
        bias_sum += jnp.sum(dlogit, axis=0, keepdims=True)
        values = [jnp.where(lane < 64, dvs[4 * j + 2 * p], swap_halves(dvs[4 * j + 2 * p + 1])) for p in range(2)]
        gm = jnp.concatenate([low(x) for x in (*grads[j], *values, dlogit)], axis=1)
        gm_s[pl.ds(pl.multiple_of((2 * b + j) * chunk, chunk), chunk), :] = gm
        gms.append(gm)
    normed = [mm(gm, wmix[...], NT) for gm in gms]
    vsum_s[0:1] += sum(jnp.sum(n * units[0, rows], axis=0, keepdims=True) for n, rows in zip(normed, spans))
    vsum_s[1:2] += sum(jnp.sum(n, axis=0, keepdims=True) for n in normed)
    first = pos[3] == 0
    gnk_o[0] = jnp.where(first, normed[0], normed[1])
    gns_o[0] = low(jnp.where(first, normed[1], normed[0]))
    gate_s[0:1] += bias_sum

    @pl.when(b == seqs - 1)
    def _():
        width = acc_s.shape[0]
        acc_s[...] = mm(attend[...].reshape(gm_s.shape[0], width), gm_s[...], TN)
        table = jnp.concatenate(
            [jnp.zeros((4, width), F32), vsum_s[0:2], gv[0:2], jnp.zeros((120, width), F32)], axis=0
        ).T
        total = gate_s[0:1]
        high = low(total).astype(F32)
        rest = jnp.broadcast_to(total - high, (8, 128))
        both = pltpu.roll(jnp.broadcast_to(high, (8, 128)), 8, 1) + pltpu.roll(rest, 12, 1)
        biases = jnp.broadcast_to(both[0:1], (width, 128))
        side = jnp.where(lanes_of((width, 128)) < 4, acc_s[:, 768:896], table) + biases
        big_s[:, 0:768] = acc_s[:, 0:768].astype(BF16)
        big_s[:, 768:896] = side.astype(BF16)
        for my in range(2):
            for mx in range(2):
                for mz in range(nz):
                    at = pl.multiple_of(chip_row(pos, mz, mx, my), 32)
                    (m00_o, m01_o, m10_o, m11_o)[2 * my + mx][mz] = big_s[pl.ds(at, 32), :]


def final_kernel(pos, keep, recv, mix_o, gate_o, bias_o, *vec_o):
    first = pos[3] == 0
    mine, theirs = keep[...], recv[...]
    halves = (jnp.where(first, mine, theirs), jnp.where(first, theirs, mine))
    width = mix_o.shape[1] // 6
    for i in range(3):
        for s in range(2):
            mix_o[:, (2 * i + s) * width : (2 * i + s + 1) * width] = halves[s][:, i * width : (i + 1) * width]
    sides = [half[:, 3 * width :] for half in halves]
    lane = lanes_of(sides[0].shape)
    gate_o[...] = jnp.where(lane < 4, sides[0], pltpu.roll(sides[1], 4, 1))[:, 0 : gate_o.shape[1]]
    both = jnp.concatenate([sides[0] + sides[1], jnp.zeros((112, 128), F32)], axis=0).T
    for i, out in enumerate(vec_o):
        out[...] = both[4 + i, 0:16]
    sums = [side[0:8] + pltpu.roll(side[0:8], 124, 1) for side in sides]
    row = jnp.where(lane[0:8] < 4, pltpu.roll(sums[0], 120, 1), pltpu.roll(sums[1], 124, 1))
    bias_o[...] = row[0, 0:8]


def input_kernel(b, x, gm, keep, recv, vec, o):
    unit, inv = norm_of(x[0].astype(F32))
    grad = keep[0] + recv[0].astype(F32)
    o[0] = gm[0] + norm_back(grad * vec[4:5], unit, inv)


def hold_kernel(*refs):
    sems = refs[-1]
    count = (len(refs) - 1) // 2
    copies = [
        pltpu.make_async_copy(refs[i], refs[count + i], sems.at[i]) for i in range(count)
    ]
    for copy in copies:
        copy.start()
    for copy in copies:
        copy.wait()


def near_kernel(line, by_x, by_y, near, x_half, y_half, sems):
    nz = line.shape[0]
    half = nz // 2
    copies = [
        pltpu.make_async_copy(source, target, sems.at[i])
        for i, (source, target) in enumerate(
            (
                (line, near.at[pl.ds(0, nz)]),
                (by_x, near.at[pl.ds(nz, nz)]),
                (by_y, near.at[pl.ds(2 * nz, nz)]),
                (by_x.at[pl.ds(0, half)], x_half),
                (by_y.at[pl.ds(half, half)], y_half),
            )
        )
    ]
    for copy in copies:
        copy.start()
    for copy in copies:
        copy.wait()


def gather_kernel(*refs):
    parts, out, sems = refs[:-2], refs[-2], refs[-1]
    copies, at = [], 0
    for i, part in enumerate(parts):
        copies.append(pltpu.make_async_copy(part, out.at[pl.ds(at, part.shape[0])], sems.at[i]))
        at += part.shape[0]
    for copy in copies:
        copy.start()
    for copy in copies:
        copy.wait()


def pause_kernel(out):
    out[...] = jnp.zeros_like(out)


def join_kernel(pos, *refs, axis):
    parts, out, sems = refs[:-2], refs[-2], refs[-1]
    copies = [
        pltpu.make_async_copy(part, out.at[pos[axis] ^ i], sems.at[i]) for i, part in enumerate(parts)
    ]
    for copy in copies:
        copy.start()
    for copy in copies:
        copy.wait()


def pair_sum_kernel(keep, recv, okeep, orecv, x_keep, x_send, y_keep, y_send):
    half = x_keep.shape[1]
    rows = keep.shape[3]
    first, second = slice(0, half), slice(half, 2 * half)
    for i in range(2):
        for my, mx, zs, out in ((i, 0, first, x_keep), (i, 1, first, x_send), (0, i, second, y_keep), (1, i, second, y_send)):
            out[i, :, 0:rows] = low(keep[my, mx, zs].astype(F32) + recv[my, mx, zs].astype(F32))
            out[i, :, rows:] = low(okeep[my, mx, zs].astype(F32) + orecv[my, mx, zs].astype(F32))


def half_sum_kernel(x_keep, x_recv, y_keep, y_recv, x_own, x_far, y_own, y_far):
    for keep, recv, own, far in ((x_keep, x_recv, x_own, x_far), (y_keep, y_recv, y_own, y_far)):
        for i, out in ((0, own), (1, far)):
            out[...] = low(keep[i].astype(F32) + recv[i].astype(F32))


def line_sum_kernel(x_own, x_recv, y_own, y_recv, *outs):
    half = x_own.shape[0]
    for i in range(half):
        outs[i][...] = low(x_own[i].astype(F32) + x_recv[i].astype(F32))
        outs[half + i][...] = low(y_own[i].astype(F32) + y_recv[i].astype(F32))


def sum_of_four(refs):
    a, b, c, d = (ref[...].astype(F32) for ref in refs)
    return (a + b) + (c + d)


def mix_sum_kernel(m0, m1, m2, m3, *outs):
    total = sum_of_four((m0, m1, m2, m3))
    side = total[..., 768:896]
    rest = side - low(side).astype(F32)
    lane = lanes_of(side.shape)
    moved = jnp.where((lane >= 12) & (lane < 16), side + pltpu.roll(rest, 4, side.ndim - 1), side)
    for i, out in enumerate(outs):
        out[:, 0:768] = low(total[i, :, 0:768])
        out[:, 768:896] = low(moved[i])


def feed_last_kernel(a, b, c, d, up_o, down_o, out_o):
    total = sum_of_four((a, b, c, d))
    rows = up_o.shape[0]
    up_o[...] = total[0:rows]
    down_o[...] = total[rows : 2 * rows].T
    out_o[...] = total[2 * rows :]


def mix_last_kernel(pos, a, b, c, d, keep_o, send_o):
    total = sum_of_four((a, b, c, d))
    rows = keep_o.shape[0]
    first = pos[3] == 0
    keep_o[...] = jnp.where(first, total[:rows], total[rows:])
    send_o[...] = jnp.where(first, total[rows:], total[:rows])


def call(kernel, steps, ins, outs, scratch=(), us=1.0, name=None, limit=14):
    def spec(kind):
        if kind in "da":
            return pl.BlockSpec(memory_space=pl.ANY)
        return pl.BlockSpec(memory_space=pltpu.SMEM if kind == "m" else pltpu.VMEM)

    kinds = [kind for kind, _ in ins]
    out_kinds = [kind for kind, _, _ in outs]
    all_kinds = kinds + out_kinds + ["w"] * len(scratch)

    def run(*refs):
        used = [(kind, ref) for kind, ref in zip(all_kinds, refs) if kind != "d"]
        if not steps:
            kernel(*[ref for _, ref in used])
            return

        def one(b, carry):
            kernel(b, *[ref.at[pl.ds(b, 1)] if kind == "s" else ref for kind, ref in used])
            return carry

        lax.fori_loop(0, steps, one, 0)

    return pl.pallas_call(
        run,
        in_specs=[spec(kind) for kind in kinds],
        out_specs=[spec(kind) for kind in out_kinds],
        out_shape=[jax.ShapeDtypeStruct(shape, dtype) for _, shape, dtype in outs],
        scratch_shapes=list(scratch),
        compiler_params=pltpu.CompilerParams(vmem_limit_bytes=limit * 1024 * 1024),
        cost_estimate=pl.CostEstimate(flops=int(us * 1.15e9), bytes_accessed=0, transcendentals=0),
        name=name,
    )(*[a for _, a in ins])


def xor_with(a, mask, count):
    return lax.ppermute(a, BOTH, [(i, i ^ mask) for i in range(count)])


def body(
    inputs, cotangent, mix_weight, gate_weight, gate_bias, out_weight, gain_first, shift_first, gain_second,
    shift_second, up_weight, down_weight, random_maps,
):
    dp, tensor = lax.axis_size("dp"), lax.axis_size("tensor")
    count = dp * tensor
    place_dp, place_t = lax.axis_index("dp"), lax.axis_index("tensor")
    seqs, chunk, width = inputs.shape
    heads, head = random_maps.shape[0], random_maps.shape[1]
    hidden = up_weight.shape[1]
    core = place_t % 2
    first = core == 0
    direct = dp == 8
    nz = 4
    if direct:
        pos = jnp.stack([place_dp // 2, place_dp % 2, place_t // 2, core]).astype(jnp.int32)
    else:
        pos = jnp.stack([jnp.zeros_like(core)] * 3 + [core]).astype(jnp.int32)
    swap_core = functools.partial(xor_with, mask=1, count=count)

    def mix_pack(mix_w, gate_w, vecs):
        rows = mix_w.shape[0]
        split = mix_w.reshape(rows, 3, 2, width // 2)
        sides = [v[:, None] for v in vecs]
        pad = jnp.zeros((rows, 120), BF16)
        return [
            jnp.concatenate(
                [split[:, 0, s], split[:, 1, s], split[:, 2, s], gate_w[:, 4 * s : 4 * s + 4]] + sides + [pad], axis=1
            )
            for s in range(2)
        ]

    def join(parts, axis, after=()):
        (out,) = call(
            functools.partial(join_kernel, axis=axis), 0, [("m", pos)] + [("a", a) for a in parts] + [("d", a) for a in after],
            [("w", (len(parts), *parts[0].shape), parts[0].dtype)],
            scratch=[pltpu.SemaphoreType.DMA((len(parts),))], name="join",
        )
        return out

    def pause(after, us):
        (out,) = call(
            pause_kernel, 0, [("d", a) for a in after], [("w", (8, 128), F32)], us=us, name="pause",
        )
        return out

    def from_plane(pieces):
        return [pieces[0], xor_with(pieces[1], 4, count), xor_with(pieces[2], 2, count), xor_with(pieces[3], 6, count)]

    other_in = swap_core(inputs)
    vectors = (gain_first, shift_first, gain_second, shift_second)
    long = 2 * chunk
    unit, cot_t = call(
        prepare_kernel, seqs, [("m", pos), ("s", inputs), ("s", other_in), ("s", cotangent)],
        [("s", (seqs, long, width), F32), ("s", (seqs, width, chunk), BF16)], us=2.5, name="prepare",
    )
    if direct:
        side_lane = lanes_of((mix_weight.shape[0], 128))
        side = jnp.pad(gate_weight, ((0, 0), (0, 128 - heads)))
        for i, v in enumerate(vectors):
            side = jnp.where(side_lane == heads + i, lax.broadcast_in_dim(v, side_lane.shape, (0,)), side)
        rows = mix_weight.shape[0]
        keep, send = call(
            pack_kernel, 0, [("m", pos), ("w", mix_weight), ("w", side)], [("w", (rows, 896), BF16)] * 2, name="pack",
        )
        pair = join([keep, swap_core(send)], 3)
        line = join([pair] + [xor_with(pair, 8 * m, count) for m in range(1, nz)], 0, after=[unit])
        w_pieces = [line] + [xor_with(line, m, count) for m in (4, 2, 6)]
        block = jnp.concatenate([up_weight, down_weight.T, out_weight], axis=0)
        (block,) = call(
            hold_kernel, 0, [("a", block), ("d", line)],
            [("w", block.shape, BF16)], scratch=[pltpu.SemaphoreType.DMA((1,))], name="hold",
        )
        ff_line = join([block] + [xor_with(block, 8 * m, count) for m in range(1, nz)], 0, after=w_pieces)
        by_x, by_y = xor_with(ff_line, 4, count), xor_with(ff_line, 2, count)
    else:
        whole = [
            lax.all_gather(a, BOTH, axis=0, tiled=True) for a in (mix_weight, gate_weight, out_weight) + vectors
        ]
        p0, p1 = mix_pack(whole[0], whole[1], whole[3:])
        blocks = jnp.where(first, p0, p1).reshape(nz, 2, 2, 2, 16, 896)
        w_pieces = [blocks[:, mx, my] for my, mx in ((0, 0), (0, 1), (1, 0), (1, 1))]
        up_all = lax.all_gather(up_weight, BOTH, axis=0, tiled=False).reshape(dp, tensor, -1, hidden)
        dn_all = lax.all_gather(down_weight.T, BOTH, axis=0, tiled=False).reshape(dp, tensor, -1, hidden)
        up_all = jnp.moveaxis(up_all, 1, 0).reshape(2, 2, nz, 2, -1, hidden)
        dn_all = jnp.moveaxis(dn_all, 1, 0).reshape(2, 2, nz, 2, -1, hidden)
        out_all = whole[2].reshape(nz, 2, 2, 2, 16, width).transpose(2, 3, 0, 1, 4, 5)
        ff_all = jnp.concatenate([up_all, dn_all, out_all], axis=4)
        ff_all = jnp.where(first, ff_all, ff_all[:, ::-1])
        ff_own, ff_other = (
            jnp.concatenate([ff_all[my, mc, :, mx] for my in range(2) for mx in range(2)]) for mc in range(2)
        )

    maps = lax.dynamic_slice_in_dim(random_maps, core * 4, 4, 0)
    zero = jnp.zeros((head, head), BF16)
    maps_pair = jnp.stack(
        [
            jnp.concatenate(
                [jnp.concatenate([maps[2 * p], zero], 1), jnp.concatenate([zero, maps[2 * p + 1]], 1)], 0
            )
            for p in range(2)
        ]
    )
    flip = jnp.swapaxes(maps, 1, 2)
    maps_back = jnp.stack(
        [
            jnp.concatenate(
                [
                    jnp.concatenate([flip[2 * p], zero], 1),
                    jnp.concatenate([-flip[2 * p], zero], 1),
                    jnp.concatenate([zero, flip[2 * p + 1]], 1),
                    jnp.concatenate([zero, -flip[2 * p + 1]], 1),
                ],
                0,
            )
            for p in range(2)
        ]
    )
    bias = jnp.pad(lax.dynamic_slice_in_dim(gate_bias, core * 4, 4, 0), (0, 124))[None]

    tokens = seqs * long
    feats = (seqs, 4, long, 128)
    npack = 2 * seqs + 1
    attend, fq, fk, fql, fkl, va, ccol, ucol, crow, smid, pack, wmix, vec, vbar = call(
        project_kernel, seqs,
        [("m", pos), ("s", unit)] + [("a", w) for w in w_pieces] + [("w", bias), ("w", maps_pair)],
        [
            ("s", (seqs, long, width), BF16), ("s", feats, BF16), ("s", feats, BF16), ("s", feats, BF16), ("s", feats, BF16), ("s", feats, BF16),
            ("s", (seqs, long, 128), F32), ("s", (seqs, long, 128), F32),
            ("s", (seqs, 2, 8, chunk), F32),
            ("s", (seqs, 4, 128, 128), F32),
            ("w", (npack, 128, 128), BF16), ("w", (width, 896), BF16), ("w", (8, width), F32),
            ("w", (8, width // 2), F32),
        ],
        scratch=[pltpu.VMEM((nz, 2, 2, 2, 16, 896), BF16), pltpu.SemaphoreType.DMA((4,))], us=12, name="project",
    )
    if direct:
        half_z = nz // 2
        near_shape, far_shape = (3 * nz, *ff_line.shape[1:]), (half_z, *ff_line.shape[1:])
        ff_near, x_half, y_half = call(
            near_kernel, 0, [("a", ff_line), ("a", by_x), ("a", by_y), ("d", pack)],
            [("w", near_shape, BF16), ("w", far_shape, BF16), ("w", far_shape, BF16)],
            scratch=[pltpu.SemaphoreType.DMA((5,))], name="near",
        )
    ahead = [(i, i + 2) for i in range(count) if (i % tensor) < 2]
    arrived = lax.ppermute(pack, BOTH, ahead)
    (o_loc,) = call(
        local_kernel, seqs,
        [("s", fq), ("s", fk), ("s", fql), ("s", fkl), ("s", va), ("s", ccol), ("s", crow)],
        [("s", feats, F32)], us=0.3, name="local",
    )
    (inv_root, turn, st, att_keep, att_send) = call(
        finish_kernel, seqs,
        [("m", pos), ("s", o_loc), ("s", fq), ("s", ccol), ("w", arrived), ("s", smid), ("w", vbar)],
        [
            ("s", feats, F32), ("s", feats, F32), ("s", (seqs, 4, 2, 128, 128), BF16),
            ("s", (seqs, chunk, width // 2), BF16), ("s", (seqs, chunk, width // 2), BF16),
        ],
        us=0.3, name="finish",
    )
    att_recv = swap_core(att_send)
    if direct:
        near_other = swap_core(ff_near)
        far_parts = [xor_with(x_half, 2, count), xor_with(y_half, 4, count)]
        (ff_far,) = call(
            gather_kernel, 0, [("a", a) for a in far_parts] + [("d", att_keep)],
            [("w", ff_line.shape, BF16)], scratch=[pltpu.SemaphoreType.DMA((2,))], name="gather",
        )
        far_other = swap_core(ff_far)
    else:
        ff_near, ff_far, near_other, far_other = ff_own[: 3 * nz], ff_own[3 * nz :], ff_other[: 3 * nz], ff_other[3 * nz :]

    own = seqs * chunk
    nrows = ff_near.shape[1]
    payload, out_payload = (2, 2, nz, nrows - 16, hidden), (2, 2, nz, 16, hidden)
    rows_low, rows_full = ("w", (own, width), BF16), ("w", (own, width), F32)
    work = [
        pltpu.VMEM((width, 2 * hidden), BF16), pltpu.VMEM((width, 2 * hidden), BF16),
        pltpu.VMEM((own, 2 * hidden), BF16), pltpu.VMEM((own, 2 * hidden), BF16),
    ]
    big = pltpu.VMEM((width, 2 * hidden), BF16)
    g_send, *fed = call(
        feed_first_kernel, 0,
        [("m", pos)] + [
            ("w", a) for a in (
                att_keep, att_recv, inputs, cotangent, cot_t, vec, ff_near, ff_far, near_other, far_other
            )
        ],
        [
            ("w", payload, BF16), rows_full, rows_full, rows_full, rows_low, ("w", (width, own), BF16), rows_low,
            ("w", (width, width), BF16),
        ],
        scratch=[*work, big], us=10, name="feed_first", limit=24,
    )
    g_recv = swap_core(g_send)
    output, grad_middle, ga_keep, ga_send, g_keep, o_keep, o_send, grad_vec = call(
        feed_second_kernel, 0,
        [("m", pos)] + [("w", a) for a in (cotangent, cot_t, vec, ff_near, ff_far, *fed)],
        [
            ("w", (seqs, chunk, width), BF16), ("w", (seqs, chunk, width), F32),
            ("w", (seqs, chunk, width // 2), BF16), ("w", (seqs, chunk, width // 2), BF16),
            ("w", payload, BF16), ("w", out_payload, BF16), ("w", out_payload, BF16), ("w", (8, width), F32),
        ],
        scratch=[
            *work, pltpu.VMEM((own, width), BF16), big,
        ],
        us=10, name="feed_second", limit=24,
    )
    ga_recv = swap_core(ga_send)

    if direct:
        o_recv = swap_core(o_send)
        half_z = nz // 2
        two, one = (2, half_z, nrows, hidden), (half_z, nrows, hidden)
        x_keep, x_send, y_keep, y_send = call(
            pair_sum_kernel, 0, [("w", g_keep), ("w", g_recv), ("w", o_keep), ("w", o_recv)], [("w", two, BF16)] * 4,
            us=0.6, name="pair_sum",
        )
        x_recv, y_recv = xor_with(x_send, 4, count), xor_with(y_send, 2, count)
        before_adjoint = [x_keep]
    else:
        before_adjoint = []
        g_keep, g_send = (jnp.concatenate(parts, axis=3) for parts in ((g_keep, o_keep), (g_send, o_send)))
        by_core = jnp.where(first, jnp.stack([g_keep, g_send]), jnp.stack([g_send, g_keep]))
        by_rows = by_core.transpose(3, 2, 1, 0, 4, 5)
        rows_up = (nrows - 16) // 2
        ups = by_rows[..., :rows_up, :].reshape(nz * 2, 4, rows_up, hidden).transpose(1, 0, 2, 3)
        dns = by_rows[..., rows_up : 2 * rows_up, :].reshape(nz * 2, 4, rows_up, hidden).transpose(1, 0, 2, 3)
        ups = ups.reshape(4, dp, -1, hidden).transpose(1, 0, 2, 3)
        dns = dns.reshape(4, dp, -1, hidden).transpose(1, 0, 2, 3)
        outs = by_rows[..., 2 * rows_up :, :].reshape(width, width)

        def reduced(a):
            return lax.psum_scatter(a.astype(F32).reshape(count, -1, a.shape[-1]), BOTH, scatter_dimension=0)

        up_grad, down_grad, out_grad = reduced(ups), reduced(dns).T, reduced(outs)

    g, scaled, l1, pack_b = call(
        adjoint_kernel, seqs,
        [("m", pos), ("s", ga_keep), ("s", ga_recv), ("s", inv_root), ("s", turn), ("s", fq), ("s", ccol)]
        + [("d", a) for a in before_adjoint],
        [
            ("s", feats, BF16), ("s", feats, BF16), ("s", (seqs, 4, 128, 128), F32), ("w", (npack, 128, 128), BF16),
        ],
        us=0.3, name="adjoint",
    )
    behind = [(i, i - 2) for i in range(count) if (i % tensor) >= 2]
    arrived_b = lax.ppermute(pack_b, BOTH, behind)
    dfq, dfk, dva = call(
        local_back_kernel, seqs,
        [("s", fq), ("s", fk), ("s", va), ("s", g), ("s", scaled), ("s", st), ("s", ccol), ("s", crow)],
        [("s", feats, F32), ("s", feats, F32), ("s", feats, F32)],
        us=0.3, name="local_back",
    )
    before_close = []
    if direct:
        x_own, x_far, y_own, y_far = call(
            half_sum_kernel, 0, [("w", a) for a in (x_keep, x_recv, y_keep, y_recv)] + [("d", dfq)],
            [("w", one, BF16)] * 4, us=0.4, name="half_sum",
        )
        x_recv, y_recv = xor_with(x_far, 2, count), xor_with(y_far, 4, count)
        before_close = [x_own]
    *m_pieces, gn_keep, gn_send = call(
        functools.partial(close_kernel, seqs_total=seqs), seqs,
        [("m", pos), ("s", unit), ("w", attend), ("s", fq), ("s", fk), ("s", va), ("s", dfq),
         ("s", dfk), ("s", dva), ("s", ccol), ("s", ucol), ("w", arrived_b), ("s", l1), ("s", st),
         ("w", wmix), ("w", grad_vec), ("w", maps_back)] + [("d", a) for a in before_close],
        [*[("w", (nz, 32, 896), BF16)] * 4, ("s", (seqs, chunk, width), F32), ("s", (seqs, chunk, width), BF16)],
        scratch=[
            pltpu.VMEM((width, 896), F32), pltpu.VMEM((tokens, 896), BF16), pltpu.VMEM((8, 128), F32),
            pltpu.VMEM((8, width), F32), pltpu.VMEM((width, 896), BF16),
        ],
        us=14.7, name="close",
    )
    if direct:
        g_line = call(
            line_sum_kernel, 0, [("w", a) for a in (x_own, x_recv, y_own, y_recv)] + [("d", gn_keep)],
            [("w", (nrows, hidden), BF16)] * nz, us=0.4, name="line_sum",
        )
        m_parts = from_plane(m_pieces)
    gn_recv = swap_core(gn_send)
    def finish_input(after):
        return call(
            input_kernel, seqs,
            [("s", inputs), ("s", grad_middle), ("s", gn_keep), ("s", gn_recv), ("w", vec)] + [("d", a) for a in after],
            [("s", (seqs, chunk, width), F32)], us=0.3, name="input_grad",
        )

    if direct:
        m_plane = call(
            mix_sum_kernel, 0, [("w", a) for a in m_parts] + [("d", pause([g_line[0]], 40))],
            [("w", (32, 896), BF16)] * nz, us=0.4, name="mix_sum",
        )
        (input_grad,) = finish_input([m_plane[0]])
        g_parts = [g_line[0]] + [xor_with(g_line[m], 8 * m, count) for m in range(1, nz)]
        up_grad, down_grad, out_grad = call(
            feed_last_kernel, 0, [("w", a) for a in g_parts],
            [("w", a.shape, F32) for a in (up_weight, down_weight, out_weight)], us=0.3, name="feed_last",
        )
        mix_parts = [m_plane[0]] + [xor_with(m_plane[m], 8 * m, count) for m in range(1, nz)]
        m_keep, m_send = call(
            mix_last_kernel, 0, [("m", pos)] + [("w", a) for a in mix_parts] + [("d", out_grad), ("d", input_grad)],
            [("w", (mix_weight.shape[0], 896), F32)] * 2, name="mix_last",
        )
        m_recv = swap_core(m_send)
    else:
        (input_grad,) = finish_input([])
        m_all = jnp.stack(m_pieces).astype(F32).reshape(2, 2, nz, 32, 896)
        mine_rows = m_all.transpose(2, 1, 0, 3, 4).reshape(count, -1, 896)
        keep_part = lax.psum_scatter(mine_rows * jnp.where(first, 1.0, 0.0), BOTH, scatter_dimension=0)
        far_part = lax.psum_scatter(mine_rows * jnp.where(first, 0.0, 1.0), BOTH, scatter_dimension=0)
        m_keep = jnp.where(first, keep_part, far_part)
        m_recv = jnp.where(first, far_part, keep_part)
    if direct:
        mix_grad, gate_grad, bias_grad, *per_row = call(
            final_kernel, 0, [("m", pos), ("w", m_keep), ("w", m_recv)],
            [("w", mix_weight.shape, F32), ("w", gate_weight.shape, F32), ("w", (heads,), F32)]
            + [("w", gain_first.shape, F32)] * 4,
            us=1.2, name="final",
        )
    else:
        m_low = jnp.where(first, m_keep, m_recv)
        m_high = jnp.where(first, m_recv, m_keep)
        mix_grad = jnp.concatenate(
            [part[:, 256 * i : 256 * i + 256] for i in range(3) for part in (m_low, m_high)], axis=1
        )
        gate_grad = jnp.concatenate([m_low[:, 768:772], m_high[:, 768:772]], axis=1)
        bias_grad = jnp.concatenate([m[0, 776:780] + m[0, 780:784] for m in (m_low, m_high)])
        per_row = [m_keep[:, 772 + i] + m_recv[:, 772 + i] for i in range(4)]
    return (
        output, input_grad, mix_grad, gate_grad, bias_grad, out_grad,
        *per_row, up_grad, down_grad,
    )


def solution(mesh):
    rows, spread = P(("dp", "tensor"), None), P(("dp", "tensor"))
    tokens = P("dp", "tensor", None)
    in_specs = (
        tokens, tokens, rows, rows, P(), rows, spread, spread, spread, spread, P("dp", "tensor"), P("tensor", "dp"), P(),
    )
    out_specs = (
        tokens, tokens, rows, rows, P(), rows, spread, spread, spread, spread, P("dp", "tensor"), P("tensor", "dp"),
    )
    return jax.shard_map(body, mesh=mesh, in_specs=in_specs, out_specs=out_specs, check_vma=False)
```

time: 188 us -> 161 us (0.86)
  Pallas kernels: 89.3 us -> 73.6 us
  local copies, waits for them, and re-layouts: 15.5 us -> 5.84 us
    pallas_call x17 -> x25, Pallas kernels: 89.3 us -> 73.6 us  [call(): pl.pallas_call(run, in_specs=[spec(kind) for kind in kinds], out_specs=[s...]
    ppermute x1, waiting for transfers between devices: 0.01 us -> 4.59 us  [body(): arrived = lax.ppermute(pack, BOTH, ahead)]
    ppermute x35 -> x36, waiting for transfers between devices: 35.2 us -> 31.5 us  [xor_with(): return lax.ppermute(a, BOTH, [(i, i ^ mask) for i in range(count)])]
    broadcast_in_dim x4 -> x0, local copies, waits for them, and re-layouts: 2.98 us -> none  [half(): parts += [placed(v[:, None], 772 + i) for i, v in enumerate(vectors)]]
    unnamed x51 -> x48, local copies, waits for them, and re-layouts: 8.57 us -> 5.61 us
    ppermute x1, waiting for transfers between devices: 4.5 us -> 1.9 us  [body(): arrived_b = lax.ppermute(pack_b, BOTH, behind)]
    ppermute x35 -> x36, starting transfers between devices: 35.6 us -> 36.1 us  [xor_with(): return lax.ppermute(a, BOTH, [(i, i ^ mask) for i in range(count)])]
  transfers between devices with their start and end apart: 37 -> 38, of which waited for: 14 -> 17; matrix products, arithmetic and copies ran while one was open for 2% -> 2% of each run, Pallas kernels for 26% -> 38%
where the time goes in v2:
time: 161 us; the launch traced here: 160 us
  Pallas kernels  73.6 us (46%)
  starting transfers between devices  40.8 us (25%)
  waiting for transfers between devices  38 us (24%)
  local copies, waits for them, and re-layouts  5.84 us (4%)
    pallas_call x25, Pallas kernels, call(): pl.pallas_call(run, in_specs=[spec(kind) for kind in kinds], out_specs=[s...  73.6 us
    ppermute x36, starting transfers between devices, xor_with(): return lax.ppermute(a, BOTH, [(i, i ^ mask) for i in range(count)])  36.1 us
    ppermute x36, waiting for transfers between devices, xor_with(): return lax.ppermute(a, BOTH, [(i, i ^ mask) for i in range(count)])  31.5 us
    unnamed x48, local copies, waits for them, and re-layouts  5.61 us
    ppermute x1, waiting for transfers between devices, body(): arrived = lax.ppermute(pack, BOTH, ahead)  4.59 us
    ppermute x1, starting transfers between devices, body(): arrived = lax.ppermute(pack, BOTH, ahead)  3.43 us
  transfers between devices with their start and end apart: 38, of which 17 were waited for; matrix products, arithmetic and copies ran while one was open for 2% of the time, Pallas kernels for 38%

profile of v2, /device:TPU:0, one launch (start us, length us, event | category | flops | bytes accessed | tf_op | source)
XLA Modules:
  0.0 160.4 jit_solution(3829654676927573204)
XLA Ops:
  6.1 2.8 %collective-permute-start.2 = (bf16[2,16,896]{2,1,0:T(8,128)(2,1)S(1)}, bf16[2,16,896]{2,1,0:T(8,128)(2,1)S(1)}, u32[]{:S(2)}, u32[]{:S(2)}) collective-permute-start(bf16[2,16,896]{2,1,0:T(8,128)(2,1)S(1)} %join.3.refs_1_), channel_id=1, source_target_pairs={{0,8},{1,9},{2,10},{3,11},{4,12},{5,13},{6,14},{7,15},{8,0},{9,1},... | collective-permute-start | bytes 172040 | tf_op jit(solution)/shard_map/ppermute | solution.py:746
  8.9 2.6 %collective-permute-start.3 = (bf16[2,16,896]{2,1,0:T(8,128)(2,1)S(1)}, bf16[2,16,896]{2,1,0:T(8,128)(2,1)S(1)}, u32[]{:S(2)}, u32[]{:S(2)}) collective-permute-start(bf16[2,16,896]{2,1,0:T(8,128)(2,1)S(1)} %join.3.refs_1_), channel_id=1, source_target_pairs={{0,16},{1,17},{2,18},{3,19},{4,20},{5,21},{6,22},{7,23},{8,24},{9,... | collective-permute-start | bytes 172040 | tf_op jit(solution)/shard_map/ppermute | solution.py:746
  15.4 2.0 %collective-permute-done.4.refs_4_ = bf16[2,16,896]{2,1,0:T(8,128)(2,1)S(1)} collective-permute-done((bf16[2,16,896]{2,1,0:T(8,128)(2,1)S(1)}, bf16[2,16,896]{2,1,0:T(8,128)(2,1)S(1)}, u32[]{:S(2)}, u32[]{:S(2)}) %collective-permute-start.4) | collective-permute-done | bytes 57376 | tf_op jit(solution)/shard_map/ppermute | solution.py:746
  24.4 2.2 %collective-permute-done.10.refs_4_ = bf16[144,512]{1,0:T(8,128)(2,1)S(1)} collective-permute-done((bf16[144,512]{1,0:T(8,128)(2,1)S(1)}, bf16[144,512]{1,0:T(8,128)(2,1)S(1)}, u32[]{:S(2)}, u32[]{:S(2)}) %collective-permute-start.10) | collective-permute-done | bytes 147488 | tf_op jit(solution)/shard_map/ppermute | solution.py:746
  28.7 2.2 %collective-permute-done.8.refs_2_ = bf16[144,512]{1,0:T(8,128)(2,1)S(1)} collective-permute-done((bf16[144,512]{1,0:T(8,128)(2,1)S(1)}, bf16[144,512]{1,0:T(8,128)(2,1)S(1)}, u32[]{:S(2)}, u32[]{:S(2)}) %collective-permute-start.8) | collective-permute-done | bytes 147488 | tf_op jit(solution)/shard_map/ppermute | solution.py:746
  30.9 3.3 %collective-permute-done.9.refs_3_ = bf16[144,512]{1,0:T(8,128)(2,1)S(1)} collective-permute-done((bf16[144,512]{1,0:T(8,128)(2,1)S(1)}, bf16[144,512]{1,0:T(8,128)(2,1)S(1)}, u32[]{:S(2)}, u32[]{:S(2)}) %collective-permute-start.9) | collective-permute-done | bytes 147488 | tf_op jit(solution)/shard_map/ppermute | solution.py:746
  38.7 10.8 %project.1 = (bf16[3,512,512]{2,1,0:T(8,128)(2,1)S(1)}, bf16[3,4,512,128]{3,2,1,0:T(8,128)(2,1)S(1)}, bf16[3,4,512,128]{3,2,1,0:T(8,128)(2,1)S(1)}, bf16[3,4,512...) custom-call(s32[4]{0:T(128)S(1)} %pad_add_fusion.refs_0_, ...), custom_call_target="tpu_custom_call" | custom-call | flops 13799999488 | tf_op jit(solution)/shard_map/project/pallas_call | solution.py:733
  52.0 3.4 %collective-permute-start.15 = (bf16[7,128,128]{2,1,0:T(8,128)(2,1)S(1)}, bf16[7,128,128]{2,1,0:T(8,128)(2,1)S(1)}, u32[]{:S(2)}, u32[]{:S(2)}) collective-permute-start(bf16[7,128,128]{2,1,0:T(8,128)(2,1)S(1)} %get-tuple-element.100.refs_3_), channel_id=1, source_target_pairs={{0,2},{1,3},{4,6},{5,7},{8,10},{9,11},{12,14},{13,15},{16,18},{17,... | collective-permute-start | bytes 688136 | tf_op jit(solution)/shard_map/ppermute | solution.py:894
  55.4 3.3 %local.1.refs_1_ = f32[3,4,512,128]{3,2,1,0:T(8,128)S(1)} custom-call(bf16[3,4,512,128]{3,2,1,0:T(8,128)(2,1)S(1)} %get-tuple-element.104.refs_0_.refs_2_.refs_5_.refs_3_, bf16[3,4,512,128]{3,2,1,0:T(8,128)(2,1)S(1)} %get-tuple-element.105.refs_1_.refs_4_, bf16[3,4,512,128]{3,2,1,0:T(8,128)(2,1)S(1)} %get-tuple-element.106.refs_2_, ...), custom_call_target="tpu_custom_call" | custom-call | flops 345000000 | tf_op jit(solution)/shard_map/local/pallas_call | solution.py:733
  58.7 4.6 %collective-permute-done.15.refs_4_ = bf16[7,128,128]{2,1,0:T(8,128)(2,1)S(1)} collective-permute-done((bf16[7,128,128]{2,1,0:T(8,128)(2,1)S(1)}, bf16[7,128,128]{2,1,0:T(8,128)(2,1)S(1)}, u32[]{:S(2)}, u32[]{:S(2)}) %collective-permute-start.15) | collective-permute-done | bytes 229408 | tf_op jit(solution)/shard_map/ppermute | solution.py:894
  63.3 4.1 %finish.1 = (f32[3,4,512,128]{3,2,1,0:T(8,128)S(1)}, f32[3,4,512,128]{3,2,1,0:T(8,128)S(1)}, bf16[3,4,2,128,128]{4,3,2,1,0:T(8,128)(2,1)S(1)}, bf16[3,256,256]{2,1,0:T(8,128)(2,1)S(1)}, bf16[3,256,256]{2,1,0:T(8,128)(2,1)S(1)}) custom-call(s32[4]{0:T(128)S(1)} %pad_add_fusion.refs_0_, f32[3,4,512,128]{3,2,1,0:T(8,128)S(1)} %local.1.refs_1_, ...), custom_call_target="tpu_custom_call" | custom-call | flops 345000000 | tf_op jit(solution)/shard_map/finish/pallas_call | solution.py:733
  68.3 2.1 %collective-permute-done.16.refs_2_ = bf16[3,256,256]{2,1,0:T(8,128)(2,1)S(1)} collective-permute-done((bf16[3,256,256]{2,1,0:T(8,128)(2,1)S(1)}, bf16[3,256,256]{2,1,0:T(8,128)(2,1)S(1)}, u32[]{:S(2)}, u32[]{:S(2)}) %collective-permute-start.16) | collective-permute-done | bytes 393248 | tf_op jit(solution)/shard_map/ppermute | solution.py:746
  70.4 8.4 %feed_first.1 = (bf16[2,2,4,128,512]{4,3,2,1,0:T(8,128)(2,1)S(1)}, f32[768,512]{1,0:T(8,128)S(1)}, f32[768,512]{1,0:T(8,128)S(1)}, f32[768,512]{1,0:T(8,128)S(1)...) custom-call(s32[4]{0:T(128)S(1)} %pad_add_fusion.refs_0_, ...), custom_call_target="tpu_custom_call" | custom-call | flops 11500000256 | tf_op jit(solution)/shard_map/feed_first/pallas_call | solution.py:733
  79.1 10.0 %feed_second.1 = (bf16[3,256,512]{2,1,0:T(8,128)(2,1)}, f32[3,256,512]{2,1,0:T(8,128)S(1)}, bf16[3,256,256]{2,1,0:T(8,128)(2,1)S(1)}, bf16[3,256,256]{2,1,0:T(8,...) custom-call(s32[4]{0:T(128)S(1)} %pad_add_fusion.refs_0_, ...), custom_call_target="tpu_custom_call" | custom-call | flops 11500000256 | tf_op jit(solution)/shard_map/feed_second/pallas_call | solution.py:733
  91.8 2.5 %collective-permute-start.24 = (bf16[2,2,144,512]{3,2,1,0:T(8,128)(2,1)S(1)}, bf16[2,2,144,512]{3,2,1,0:T(8,128)(2,1)S(1)}, u32[]{:S(2)}, u32[]{:S(2)}) collective-permute-start(bf16[2,2,144,512]{3,2,1,0:T(8,128)(2,1)S(1)} %get-tuple-element.147), channel_id=1, source_target_pairs={{0,2},{1,3},{2,0},{3,1},{4,6},{5,7},{6,4},{7,5},{8,10},{9,11},{10,... | collective-permute-start | bytes 1769480 | tf_op jit(solution)/shard_map/ppermute | solution.py:746
  94.3 5.2 %adjoint.1 = (bf16[3,4,512,128]{3,2,1,0:T(8,128)(2,1)S(1)}, bf16[3,4,512,128]{3,2,1,0:T(8,128)(2,1)S(1)}, f32[3,4,128,128]{3,2,1,0:T(8,128)S(1)}, bf16[7,128,128]{2,1,0:T(8,128)(2,1)S(1)}) custom-call(s32[4]{0:T(128)S(1)} %pad_add_fusion.refs_0_, bf16[3,256,256]{2,1,0:T(8,128)(2,1)S(1)} %get-tuple-element.125.refs_1_, ...), custom_call_target="tpu_custom_call" | custom-call | flops 345000000 | tf_op jit(solution)/shard_map/adjoint/pallas_call | solution.py:733
  100.9 5.4 %local_back.1 = (f32[3,4,512,128]{3,2,1,0:T(8,128)S(1)}, f32[3,4,512,128]{3,2,1,0:T(8,128)S(1)}, f32[3,4,512,128]{3,2,1,0:T(8,128)S(1)}) custom-call(bf16[3,4,512,128]{3,2,1,0:T(8,128)(2,1)S(1)} %get-tuple-element.104.refs_0_.refs_2_.refs_5_.refs_3_, bf16[3,4,512,128]{3,2,1,0:T(8,128)(2,1)S(1)} %get-tuple-element.105.refs_1_.refs_4_, ...), custom_call_target="tpu_custom_call" | custom-call | flops 345000000 | tf_op jit(solution)/shard_map/local_back/pallas_call | solution.py:733
  113.3 13.8 %close.1 = (bf16[4,32,896]{2,1,0:T(8,128)(2,1)S(1)}, bf16[4,32,896]{2,1,0:T(8,128)(2,1)S(1)}, bf16[4,32,896]{2,1,0:T(8,128)(2,1)S(1)}, bf16[4,32,896]{2,1,0:T(8,...) custom-call(s32[4]{0:T(128)S(1)} %pad_add_fusion.refs_0_, f32[3,512,512]{2,1,0:T(8,128)S(1)} %copy-done.9, ...), custom_call_target="tpu_custom_call" | custom-call | flops 16904999936 | tf_op jit(solution)/shard_map/close/pallas_call | solution.py:733
  130.9 4.8 %collective-permute-done.26.refs_1_ = bf16[4,32,896]{2,1,0:T(8,128)(2,1)S(1)} collective-permute-done((bf16[4,32,896]{2,1,0:T(8,128)(2,1)S(1)}, bf16[4,32,896]{2,1,0:T(8,128)(2,1)S(1)}, u32[]{:S(2)}, u32[]{:S(2)}) %collective-permute-start.26) | collective-permute-done | bytes 229408 | tf_op jit(solution)/shard_map/ppermute | solution.py:746
  136.4 3.4 %collective-permute-done.27.refs_2_ = bf16[4,32,896]{2,1,0:T(8,128)(2,1)S(1)} collective-permute-done((bf16[4,32,896]{2,1,0:T(8,128)(2,1)S(1)}, bf16[4,32,896]{2,1,0:T(8,128)(2,1)S(1)}, u32[]{:S(2)}, u32[]{:S(2)}) %collective-permute-start.27) | collective-permute-done | bytes 229408 | tf_op jit(solution)/shard_map/ppermute | solution.py:746
  142.0 2.4 %collective-permute-start.32 = (bf16[32,896]{1,0:T(8,128)(2,1)S(1)}, bf16[32,896]{1,0:T(8,128)(2,1)S(1)}, u32[]{:S(2)}, u32[]{:S(2)}) collective-permute-start(bf16[32,896]{1,0:T(8,128)(2,1)S(1)} %get-tuple-element.161), channel_id=1, source_target_pairs={{0,16},{1,17},{2,18},{3,19},{4,20},{5,21},{6,22},{7,23},{8,24},{9,... | collective-permute-start | bytes 172040 | tf_op jit(solution)/shard_map/ppermute | solution.py:746
  144.4 4.7 %collective-permute-done.35.refs_2_ = bf16[144,512]{1,0:T(8,128)(2,1)S(1)} collective-permute-done((bf16[144,512]{1,0:T(8,128)(2,1)S(1)}, bf16[144,512]{1,0:T(8,128)(2,1)S(1)}, u32[]{:S(2)}, u32[]{:S(2)}) %collective-permute-start.35) | collective-permute-done | bytes 147488 | tf_op jit(solution)/shard_map/ppermute | solution.py:746
  149.2 2.4 %collective-permute-start.33 = (bf16[32,896]{1,0:T(8,128)(2,1)S(1)}, bf16[32,896]{1,0:T(8,128)(2,1)S(1)}, u32[]{:S(2)}, u32[]{:S(2)}) collective-permute-start(bf16[32,896]{1,0:T(8,128)(2,1)S(1)} %get-tuple-element.162), channel_id=1, source_target_pairs={{0,24},{1,25},{2,26},{3,27},{4,28},{5,29},{6,30},{7,31},{8,16},{9,... | collective-permute-start | bytes 172040 | tf_op jit(solution)/shard_map/ppermute | solution.py:746
  152.3 2.3 %input_grad.1.refs_6_ = f32[3,256,512]{2,1,0:T(8,128)} custom-call(bf16[3,256,512]{2,1,0:T(8,128)(2,1)S(1)} %copy-done.3, f32[3,256,512]{2,1,0:T(8,128)S(1)} %get-tuple-element.123.refs_1_, f32[3,256,512]{2,1,0:T(8,128)S(1)} %get-tuple-element.149.refs_4_.refs_2_, bf16[3,256,512]{2,1,0:T(8,128)(2,1)S(1)} %collective-permute-done.25.refs_3_, ...), custom_call_target="tpu_custom_call" | custom-call | flops 345000000 | tf_op jit(solution)/shard_map/input_grad/pallas_call | solution.py:733
  (141 shorter events, 50.5 us)
Async XLA Ops:
  0.7 10.8 %collective-permute-start = (bf16[3,256,512]{2,1,0:T(8,128)(2,1)}, bf16[3,256,512]{2,1,0:T(8,128)(2,1)S(1)}, u32[]{:S(2)}, u32[]{:S(2)}) collective-permute-start(bf16[3,256,512]{2,1,0:T(8,128)(2,1)} %refs_0_.1), channel_id=1, source_target_pairs={{0,1},{1,0},{2,3},{3,2},{4,5},{5,4},{6,7},{7,6},{8,9},{9,8},{10,11... | collective-permute-start | bytes 2359304 | tf_op jit(solution)/shard_map/ppermute | solution.py:746
  20.4 13.8 %collective-permute-start.5 = (bf16[4,2,16,896]{3,2,1,0:T(8,128)(2,1)S(1)}, bf16[4,2,16,896]{3,2,1,0:T(8,128)(2,1)S(1)}, u32[]{:S(2)}, u32[]{:S(2)}) collective-permute-start(bf16[4,2,16,896]{3,2,1,0:T(8,128)(2,1)S(1)} %join.4.refs_2_.refs_1_.refs_5_), channel_id=1, source_target_pairs={{0,4},{1,5},{2,6},{3,7},{4,0},{5,1},{6,2},{7,3},{8,12},{9,13},{10,... | collective-permute-start | bytes 688136 | tf_op jit(solution)/shard_map/ppermute | solution.py:746
  22.0 12.2 %collective-permute-start.6 = (bf16[4,2,16,896]{3,2,1,0:T(8,128)(2,1)S(1)}, bf16[4,2,16,896]{3,2,1,0:T(8,128)(2,1)S(1)}, u32[]{:S(2)}, u32[]{:S(2)}) collective-permute-start(bf16[4,2,16,896]{3,2,1,0:T(8,128)(2,1)S(1)} %join.4.refs_2_.refs_1_.refs_5_), channel_id=1, source_target_pairs={{0,2},{1,3},{2,0},{3,1},{4,6},{5,7},{6,4},{7,5},{8,10},{9,11},{10,... | collective-permute-start | bytes 688136 | tf_op jit(solution)/shard_map/ppermute | solution.py:746
  23.5 10.7 %collective-permute-start.7 = (bf16[4,2,16,896]{3,2,1,0:T(8,128)(2,1)S(1)}, bf16[4,2,16,896]{3,2,1,0:T(8,128)(2,1)S(1)}, u32[]{:S(2)}, u32[]{:S(2)}) collective-permute-start(bf16[4,2,16,896]{3,2,1,0:T(8,128)(2,1)S(1)} %join.4.refs_2_.refs_1_.refs_5_), channel_id=1, source_target_pairs={{0,6},{1,7},{2,4},{3,5},{4,2},{5,3},{6,0},{7,1},{8,14},{9,15},{10,... | collective-permute-start | bytes 688136 | tf_op jit(solution)/shard_map/ppermute | solution.py:746
  35.6 13.9 %collective-permute-start.11 = (bf16[4,144,512]{2,1,0:T(8,128)(2,1)S(1)}, bf16[4,144,512]{2,1,0:T(8,128)(2,1)S(1)}, u32[]{:S(2)}, u32[]{:S(2)}) collective-permute-start(bf16[4,144,512]{2,1,0:T(8,128)(2,1)S(1)} %join.5.refs_0_), channel_id=1, source_target_pairs={{0,4},{1,5},{2,6},{3,7},{4,0},{5,1},{6,2},{7,3},{8,12},{9,13},{10,... | collective-permute-start | bytes 1769480 | tf_op jit(solution)/shard_map/ppermute | solution.py:746
  37.1 12.4 %collective-permute-start.12 = (bf16[4,144,512]{2,1,0:T(8,128)(2,1)S(1)}, bf16[4,144,512]{2,1,0:T(8,128)(2,1)S(1)}, u32[]{:S(2)}, u32[]{:S(2)}) collective-permute-start(bf16[4,144,512]{2,1,0:T(8,128)(2,1)S(1)} %join.5.refs_0_), channel_id=1, source_target_pairs={{0,2},{1,3},{2,0},{3,1},{4,6},{5,7},{6,4},{7,5},{8,10},{9,11},{10,... | collective-permute-start | bytes 1769480 | tf_op jit(solution)/shard_map/ppermute | solution.py:746
  50.9 19.5 %collective-permute-start.17 = (bf16[12,144,512]{2,1,0:T(8,128)(2,1)S(1)}, bf16[12,144,512]{2,1,0:T(8,128)(2,1)S(1)}, u32[]{:S(2)}, u32[]{:S(2)}) collective-permute-start(bf16[12,144,512]{2,1,0:T(8,128)(2,1)S(1)} %get-tuple-element.101.refs_7_.refs_4_), channel_id=1, source_target_pairs={{0,1},{1,0},{2,3},{3,2},{4,5},{5,4},{6,7},{7,6},{8,9},{9,8},{10,11... | collective-permute-start | bytes 5308424 | tf_op jit(solution)/shard_map/ppermute | solution.py:746
  50.9 16.5 %collective-permute-start.13 = (bf16[2,144,512]{2,1,0:T(8,128)(2,1)S(1)}, bf16[2,144,512]{2,1,0:T(8,128)(2,1)S(1)}, u32[]{:S(2)}, u32[]{:S(2)}) collective-permute-start(bf16[2,144,512]{2,1,0:T(8,128)(2,1)S(1)} %get-tuple-element.102), channel_id=1, source_target_pairs={{0,2},{1,3},{2,0},{3,1},{4,6},{5,7},{6,4},{7,5},{8,10},{9,11},{10,... | collective-permute-start | bytes 884744 | tf_op jit(solution)/shard_map/ppermute | solution.py:746
  51.4 16.0 %collective-permute-start.14 = (bf16[2,144,512]{2,1,0:T(8,128)(2,1)S(1)}, bf16[2,144,512]{2,1,0:T(8,128)(2,1)S(1)}, u32[]{:S(2)}, u32[]{:S(2)}) collective-permute-start(bf16[2,144,512]{2,1,0:T(8,128)(2,1)S(1)} %get-tuple-element.103), channel_id=1, source_target_pairs={{0,4},{1,5},{2,6},{3,7},{4,0},{5,1},{6,2},{7,3},{8,12},{9,13},{10,... | collective-permute-start | bytes 884744 | tf_op jit(solution)/shard_map/ppermute | solution.py:746
  52.0 11.3 %collective-permute-start.15 = (bf16[7,128,128]{2,1,0:T(8,128)(2,1)S(1)}, bf16[7,128,128]{2,1,0:T(8,128)(2,1)S(1)}, u32[]{:S(2)}, u32[]{:S(2)}) collective-permute-start(bf16[7,128,128]{2,1,0:T(8,128)(2,1)S(1)} %get-tuple-element.100.refs_3_), channel_id=1, source_target_pairs={{0,2},{1,3},{4,6},{5,7},{8,10},{9,11},{12,14},{13,15},{16,18},{17,... | collective-permute-start | bytes 688136 | tf_op jit(solution)/shard_map/ppermute | solution.py:894
  78.9 11.8 %collective-permute-start.20 = (bf16[2,2,4,128,512]{4,3,2,1,0:T(8,128)(2,1)S(1)}, bf16[2,2,4,128,512]{4,3,2,1,0:T(8,128)(2,1)S(1)}, u32[]{:S(2)}, u32[]{:S(2)}) collective-permute-start(bf16[2,2,4,128,512]{4,3,2,1,0:T(8,128)(2,1)S(1)} %get-tuple-element.130), channel_id=1, source_target_pairs={{0,1},{1,0},{2,3},{3,2},{4,5},{5,4},{6,7},{7,6},{8,9},{9,8},{10,11... | collective-permute-start | bytes 6291464 | tf_op jit(solution)/shard_map/ppermute | solution.py:746
  91.2 15.7 %collective-permute-start.23 = (bf16[2,2,144,512]{3,2,1,0:T(8,128)(2,1)S(1)}, bf16[2,2,144,512]{3,2,1,0:T(8,128)(2,1)S(1)}, u32[]{:S(2)}, u32[]{:S(2)}) collective-permute-start(bf16[2,2,144,512]{3,2,1,0:T(8,128)(2,1)S(1)} %get-tuple-element.145), channel_id=1, source_target_pairs={{0,4},{1,5},{2,6},{3,7},{4,0},{5,1},{6,2},{7,3},{8,12},{9,13},{10,... | collective-permute-start | bytes 1769480 | tf_op jit(solution)/shard_map/ppermute | solution.py:746
  91.8 16.6 %collective-permute-start.24 = (bf16[2,2,144,512]{3,2,1,0:T(8,128)(2,1)S(1)}, bf16[2,2,144,512]{3,2,1,0:T(8,128)(2,1)S(1)}, u32[]{:S(2)}, u32[]{:S(2)}) collective-permute-start(bf16[2,2,144,512]{3,2,1,0:T(8,128)(2,1)S(1)} %get-tuple-element.147), channel_id=1, source_target_pairs={{0,2},{1,3},{2,0},{3,1},{4,6},{5,7},{6,4},{7,5},{8,10},{9,11},{10,... | collective-permute-start | bytes 1769480 | tf_op jit(solution)/shard_map/ppermute | solution.py:746
  99.5 13.8 %collective-permute-start.22 = (bf16[7,128,128]{2,1,0:T(8,128)(2,1)S(1)}, bf16[7,128,128]{2,1,0:T(8,128)(2,1)S(1)}, u32[]{:S(2)}, u32[]{:S(2)}) collective-permute-start(bf16[7,128,128]{2,1,0:T(8,128)(2,1)S(1)} %get-tuple-element.141), channel_id=1, source_target_pairs={{2,0},{3,1},{6,4},{7,5},{10,8},{11,9},{14,12},{15,13},{18,16},{19,... | collective-permute-start | bytes 688136 | tf_op jit(solution)/shard_map/ppermute | solution.py:996
  108.7 22.0 %collective-permute-start.29 = (bf16[2,144,512]{2,1,0:T(8,128)(2,1)S(1)}, bf16[2,144,512]{2,1,0:T(8,128)(2,1)S(1)}, u32[]{:S(2)}, u32[]{:S(2)}) collective-permute-start(bf16[2,144,512]{2,1,0:T(8,128)(2,1)S(1)} %get-tuple-element.155), channel_id=1, source_target_pairs={{0,2},{1,3},{2,0},{3,1},{4,6},{5,7},{6,4},{7,5},{8,10},{9,11},{10,... | collective-permute-start | bytes 884744 | tf_op jit(solution)/shard_map/ppermute | solution.py:746
  109.9 20.8 %collective-permute-start.30 = (bf16[2,144,512]{2,1,0:T(8,128)(2,1)S(1)}, bf16[2,144,512]{2,1,0:T(8,128)(2,1)S(1)}, u32[]{:S(2)}, u32[]{:S(2)}) collective-permute-start(bf16[2,144,512]{2,1,0:T(8,128)(2,1)S(1)} %get-tuple-element.157), channel_id=1, source_target_pairs={{0,4},{1,5},{2,6},{3,7},{4,0},{5,1},{6,2},{7,3},{8,12},{9,13},{10,... | collective-permute-start | bytes 884744 | tf_op jit(solution)/shard_map/ppermute | solution.py:746
  128.7 11.1 %collective-permute-start.27 = (bf16[4,32,896]{2,1,0:T(8,128)(2,1)S(1)}, bf16[4,32,896]{2,1,0:T(8,128)(2,1)S(1)}, u32[]{:S(2)}, u32[]{:S(2)}) collective-permute-start(bf16[4,32,896]{2,1,0:T(8,128)(2,1)S(1)} %get-tuple-element.153), channel_id=1, source_target_pairs={{0,2},{1,3},{2,0},{3,1},{4,6},{5,7},{6,4},{7,5},{8,10},{9,11},{10,... | collective-permute-start | bytes 688136 | tf_op jit(solution)/shard_map/ppermute | solution.py:746
  128.7 13.1 %collective-permute-start.28 = (bf16[4,32,896]{2,1,0:T(8,128)(2,1)S(1)}, bf16[4,32,896]{2,1,0:T(8,128)(2,1)S(1)}, u32[]{:S(2)}, u32[]{:S(2)}) collective-permute-start(bf16[4,32,896]{2,1,0:T(8,128)(2,1)S(1)} %get-tuple-element.154), channel_id=1, source_target_pairs={{0,6},{1,7},{2,4},{3,5},{4,2},{5,3},{6,0},{7,1},{8,14},{9,15},{10,... | collective-permute-start | bytes 688136 | tf_op jit(solution)/shard_map/ppermute | solution.py:746
  130.7 21.6 %collective-permute-start.25 = (bf16[3,256,512]{2,1,0:T(8,128)(2,1)S(1)}, bf16[3,256,512]{2,1,0:T(8,128)(2,1)S(1)}, u32[]{:S(2)}, u32[]{:S(2)}) collective-permute-start(bf16[3,256,512]{2,1,0:T(8,128)(2,1)S(1)} %get-tuple-element.150), channel_id=1, source_target_pairs={{0,1},{1,0},{2,3},{3,2},{4,5},{5,4},{6,7},{7,6},{8,9},{9,8},{10,11... | collective-permute-start | bytes 2359304 | tf_op jit(solution)/shard_map/ppermute | solution.py:746
  130.8 11.1 %collective-permute-start.34 = (bf16[144,512]{1,0:T(8,128)(2,1)S(1)}, bf16[144,512]{1,0:T(8,128)(2,1)S(1)}, u32[]{:S(2)}, u32[]{:S(2)}) collective-permute-start(bf16[144,512]{1,0:T(8,128)(2,1)S(1)} %get-tuple-element.163), channel_id=1, source_target_pairs={{0,8},{1,9},{2,10},{3,11},{4,12},{5,13},{6,14},{7,15},{8,0},{9,1},... | collective-permute-start | bytes 442376 | tf_op jit(solution)/shard_map/ppermute | solution.py:746
  135.7 13.4 %collective-permute-start.35 = (bf16[144,512]{1,0:T(8,128)(2,1)S(1)}, bf16[144,512]{1,0:T(8,128)(2,1)S(1)}, u32[]{:S(2)}, u32[]{:S(2)}) collective-permute-start(bf16[144,512]{1,0:T(8,128)(2,1)S(1)} %get-tuple-element.164), channel_id=1, source_target_pairs={{0,16},{1,17},{2,18},{3,19},{4,20},{5,21},{6,22},{7,23},{8,24},{9,... | collective-permute-start | bytes 442376 | tf_op jit(solution)/shard_map/ppermute | solution.py:746
  139.8 11.7 %collective-permute-start.36 = (bf16[144,512]{1,0:T(8,128)(2,1)S(1)}, bf16[144,512]{1,0:T(8,128)(2,1)S(1)}, u32[]{:S(2)}, u32[]{:S(2)}) collective-permute-start(bf16[144,512]{1,0:T(8,128)(2,1)S(1)} %get-tuple-element.165), channel_id=1, source_target_pairs={{0,24},{1,25},{2,26},{3,27},{4,28},{5,29},{6,30},{7,31},{8,16},{9,... | collective-permute-start | bytes 442376 | tf_op jit(solution)/shard_map/ppermute | solution.py:746
  141.9 12.7 %collective-permute-start.31 = (bf16[32,896]{1,0:T(8,128)(2,1)S(1)}, bf16[32,896]{1,0:T(8,128)(2,1)S(1)}, u32[]{:S(2)}, u32[]{:S(2)}) collective-permute-start(bf16[32,896]{1,0:T(8,128)(2,1)S(1)} %get-tuple-element.160), channel_id=1, source_target_pairs={{0,8},{1,9},{2,10},{3,11},{4,12},{5,13},{6,14},{7,15},{8,0},{9,1},... | collective-permute-start | bytes 172040 | tf_op jit(solution)/shard_map/ppermute | solution.py:746
  142.0 12.6 %collective-permute-start.32 = (bf16[32,896]{1,0:T(8,128)(2,1)S(1)}, bf16[32,896]{1,0:T(8,128)(2,1)S(1)}, u32[]{:S(2)}, u32[]{:S(2)}) collective-permute-start(bf16[32,896]{1,0:T(8,128)(2,1)S(1)} %get-tuple-element.161), channel_id=1, source_target_pairs={{0,16},{1,17},{2,18},{3,19},{4,20},{5,21},{6,22},{7,23},{8,24},{9,... | collective-permute-start | bytes 172040 | tf_op jit(solution)/shard_map/ppermute | solution.py:746
  (36 other events, 173.7 us)

commit v3 on v2

--- a/solution.py
+++ b/solution.py
@@ -119,10 +119,14 @@
     pack_o[last] = zcols.astype(BF16)
 
 
-def pack_kernel(pos, mix, side, keep_o, send_o):
+def pack_kernel(pos, mix, columns, keep_o, send_o):
     width = mix.shape[1] // 6
-    lane = lanes_of(side.shape)
-    sides = side[...].astype(F32)
+    rows = mix.shape[0]
+    table = jnp.concatenate(
+        [columns[...].astype(F32), jnp.zeros((128 - columns.shape[0], rows), F32)], axis=0
+    )
+    sides = jnp.concatenate([table, jnp.zeros((128, 128 - rows), F32)], axis=1).T[0:rows]
+    lane = lanes_of(sides.shape)
     moved = pltpu.roll(sides, 124, 1)
     halves = []
     for s, block in ((0, jnp.where(lane < 4, sides, moved)), (1, moved)):
@@ -143,9 +147,30 @@
     cott_o[0] = low(cot[0].astype(F32).T)
 
 
+def feature_parts(angles, lane):
+    s, c = sincos(angles)
+    out = []
+    for f in (jnp.where(lane < 64, s, swap_halves(c)), jnp.where(lane < 64, swap_halves(s), c)):
+        high = low(f)
+        out.append((high, low(f - high.astype(F32))))
+    return out
+
+
+def query_kernel(b, a, wmix, maps, fq_o, fql_o):
+    chunk = a.shape[1] // 2
+    lane = lanes_of((chunk, 128))
+    spans = [slice(j * chunk, (j + 1) * chunk) for j in range(2)]
+    mixed = [low(mm(a[0, rows], wmix[:, 0:256])) for rows in spans]
+    angles = [[mm(m[:, 128 * p : 128 * p + 128], maps[p]) for p in range(2)] for m in mixed]
+    for j, rows in enumerate(spans):
+        for p in range(2):
+            for i, (high, rest) in enumerate(feature_parts(angles[j][p], lane)):
+                fq_o[0, 2 * p + i, rows], fql_o[0, 2 * p + i, rows] = high, rest
+
+
 def project_kernel(
     b, pos, units, w0, w1, w2, w3, bias, maps,
-    a_o, fq_o, fk_o, fql_o, fkl_o, va_o, ccol_o, ucol_o, crow_o, smid_o, pack_o, wmix_o, vec_o, vbar_o,
+    a_o, fk_o, fkl_o, va_o, ccol_o, ucol_o, crow_o, smid_o, pack_o, wmix_o, vec_o, vbar_o,
     w_s, sems,
 ):
     chunk = units.shape[1] // 2
@@ -172,14 +197,12 @@
     attends = [low(units[0, rows] * gain + shift) for rows in spans]
     for a, rows in zip(attends, spans):
         a_o[0, rows] = a
-    wide = [mm(a, wmix_o[...]) for a in attends]
-    mixed = [low(m[:, 0:768]) for m in wide]
-    angles = [
-        [mm(m[:, base : base + 128], maps[p]) for base, p in ((0, 0), (128, 1), (256, 0), (384, 1))] for m in mixed
-    ]
+    wide = [mm(a, wmix_o[:, 256:896]) for a in attends]
+    mixed = [low(m[:, 0:512]) for m in wide]
+    angles = [[mm(m[:, 128 * p : 128 * p + 128], maps[p]) for p in range(2)] for m in mixed]
     douts, ends = [], []
     for j, rows in enumerate(spans):
-        logits = wide[j][:, 768:896] + bias[...]
+        logits = wide[j][:, 512:640] + bias[...]
         e = jnp.exp(-jnp.abs(logits))
         w = 1.0 + e
         log1 = jnp.where(w == 1.0, e, jnp.log(w) * (e / jnp.where(w == 1.0, 1.0, w - 1.0)))
@@ -195,25 +218,18 @@
     shares = [[None] * 4, [None] * 4]
     for j, rows in enumerate(spans):
         for p in range(2):
-            v = mixed[j][:, 512 + 128 * p : 640 + 128 * p].astype(F32) - vbar_o[0:1, 128 * p : 128 * p + 128]
+            v = mixed[j][:, 256 + 128 * p : 384 + 128 * p].astype(F32) - vbar_o[0:1, 128 * p : 128 * p + 128]
             for h, vh in ((2 * p, v), (2 * p + 1, swap_halves(v))):
                 aug = jnp.where(lane < 64, vh, one)
                 va_o[0, h, rows] = low(aug)
                 shares[j][h] = low(aug * douts[j][:, h : h + 1])
     locals_ = [[None] * 4, [None] * 4]
-    for base, target, rest in ((2, fk_o, fkl_o), (0, fq_o, fql_o)):
-        for j, rows in enumerate(spans):
-            for p in range(2):
-                s, c = sincos(angles[j][base + p])
-                for h, f in (
-                    (2 * p, jnp.where(lane < 64, s, swap_halves(c))),
-                    (2 * p + 1, jnp.where(lane < 64, swap_halves(s), c)),
-                ):
-                    high = low(f)
-                    target[0, h, rows] = high
-                    rest[0, h, rows] = low(f - high.astype(F32))
-                    if base == 2:
-                        locals_[j][h] = mm(high, shares[j][h], TN)
+    for j, rows in enumerate(spans):
+        for p in range(2):
+            parts = feature_parts(angles[j][p], lane)
+            for h in (2 * p, 2 * p + 1):
+                fk_o[0, h, rows], fkl_o[0, h, rows] = parts[h - 2 * p]
+                locals_[j][h] = mm(parts[h - 2 * p][0], shares[j][h], TN)
     states = []
     for h in range(4):
         smid_o[0, h] = locals_[0][h]
@@ -320,12 +336,12 @@
 
     spans = [slice(r * chunk, (r + 1) * chunk) for r in range(seqs)]
     outs, grads = [], []
+    pres = [mm(feed[rows], up_s[...]) for rows in spans]
+    ghs = [mm(cot[r], dn_s[...]) for r in range(seqs)]
     for r, rows in enumerate(spans):
-        pre = mm(feed[rows], up_s[...])
-        gh = mm(cot[r], dn_s[...])
-        cdf, pdf = normal_parts(pre)
-        hid_s[rows] = low(pre * cdf)
-        gp_s[rows] = low(gh * (cdf + pre * pdf))
+        cdf, pdf = normal_parts(pres[r])
+        hid_s[rows] = low(pres[r] * cdf)
+        gp_s[rows] = low(ghs[r] * (cdf + pres[r] * pdf))
     for rows in spans:
         outs.append(mm(hid_s[rows], dn_s[...], NT))
         grads.append(mm(gp_s[rows], up_s[...], NT))
@@ -506,14 +522,13 @@
         d = douts[j][:, h : h + 1]
         keys, queries = fk[0, h, rows].astype(F32), fq[0, h, rows].astype(F32)
         dk_far = d * dk_fars[i]
-        kd_far = jnp.sum(keys * dk_far, axis=1, keepdims=True)
         dk = dk_far + dfk[0, h, rows]
         dq = dfq[0, h, rows]
         kds.append(jnp.sum(keys * dk, axis=1, keepdims=True))
         qds.append(jnp.sum(queries * dq, axis=1, keepdims=True))
         passed = st[0, h, j].astype(F32) * nears[i].astype(F32)
         passed = jnp.sum(jnp.sum(passed, axis=0, keepdims=True), axis=1, keepdims=True)
-        total = jnp.sum(kd_far, axis=0, keepdims=True)
+        total = jnp.sum(jnp.sum(keys * dk_far, axis=0, keepdims=True), axis=1, keepdims=True)
         levels.append(total + jnp.exp(cums[j][chunk - 1 : chunk, h : h + 1]) * passed)
         dvs.append(dva[0, h, rows] + d * dv_fars[i])
         pks.append(low(dk * swap_halves(keys)))
@@ -578,8 +593,9 @@
             mix_o[:, (2 * i + s) * width : (2 * i + s + 1) * width] = halves[s][:, i * width : (i + 1) * width]
     sides = [half[:, 3 * width :] for half in halves]
     lane = lanes_of(sides[0].shape)
-    gate_o[...] = jnp.where(lane < 4, sides[0], pltpu.roll(sides[1], 4, 1))[:, 0 : gate_o.shape[1]]
-    both = jnp.concatenate([sides[0] + sides[1], jnp.zeros((112, 128), F32)], axis=0).T
+    both = jnp.concatenate([sides[0] + sides[1], sides[0], sides[1], jnp.zeros((80, 128), F32)], axis=0).T
+    gate_o[0:4] = both[0:4, 16:32]
+    gate_o[4:8] = both[0:4, 32:48]
     for i, out in enumerate(vec_o):
         out[...] = both[4 + i, 0:16]
     sums = [side[0:8] + pltpu.roll(side[0:8], 124, 1) for side in sides]
@@ -587,7 +603,8 @@
     bias_o[...] = row[0, 0:8]
 
 
-def input_kernel(b, x, gm, keep, recv, vec, o):
+def input_kernel(b, x, gm, keep, recv, vec, o, done_o):
+    done_o[...] = jnp.zeros_like(done_o)
     unit, inv = norm_of(x[0].astype(F32))
     grad = keep[0] + recv[0].astype(F32)
     o[0] = gm[0] + norm_back(grad * vec[4:5], unit, inv)
@@ -605,20 +622,11 @@
         copy.wait()
 
 
-def near_kernel(line, by_x, by_y, near, x_half, y_half, sems):
-    nz = line.shape[0]
-    half = nz // 2
+def halves_kernel(by_x, by_y, x_half, y_half, sems):
+    half = x_half.shape[0]
     copies = [
-        pltpu.make_async_copy(source, target, sems.at[i])
-        for i, (source, target) in enumerate(
-            (
-                (line, near.at[pl.ds(0, nz)]),
-                (by_x, near.at[pl.ds(nz, nz)]),
-                (by_y, near.at[pl.ds(2 * nz, nz)]),
-                (by_x.at[pl.ds(0, half)], x_half),
-                (by_y.at[pl.ds(half, half)], y_half),
-            )
-        )
+        pltpu.make_async_copy(by_x.at[pl.ds(0, half)], x_half, sems.at[0]),
+        pltpu.make_async_copy(by_y.at[pl.ds(half, half)], y_half, sems.at[1]),
     ]
     for copy in copies:
         copy.start()
@@ -692,11 +700,12 @@
         out[:, 768:896] = low(moved[i])
 
 
-def feed_last_kernel(a, b, c, d, up_o, down_o, out_o):
+def feed_last_kernel(a, b, c, d, up_o, down_o, out_o, done_o):
+    done_o[...] = jnp.zeros_like(done_o)
     total = sum_of_four((a, b, c, d))
     rows = up_o.shape[0]
     up_o[...] = total[0:rows]
-    down_o[...] = total[rows : 2 * rows].T
+    down_o[...] = total[rows : 2 * rows]
     out_o[...] = total[2 * rows :]
 
 
@@ -708,7 +717,7 @@
     send_o[...] = jnp.where(first, total[rows:], total[:rows])
 
 
-def call(kernel, steps, ins, outs, scratch=(), us=1.0, name=None, limit=14):
+def call(kernel, steps, ins, outs, scratch=(), us=1.0, name=None, limit=12):
     def spec(kind):
         if kind in "da":
             return pl.BlockSpec(memory_space=pl.ANY)
@@ -803,13 +812,13 @@
         [("s", (seqs, long, width), F32), ("s", (seqs, width, chunk), BF16)], us=2.5, name="prepare",
     )
     if direct:
-        side_lane = lanes_of((mix_weight.shape[0], 128))
-        side = jnp.pad(gate_weight, ((0, 0), (0, 128 - heads)))
+        rows = mix_weight.shape[0]
+        columns = jnp.pad(gate_weight.T, ((0, 16 - heads), (0, 0)))
+        place = lax.broadcasted_iota(jnp.int32, columns.shape, 0)
         for i, v in enumerate(vectors):
-            side = jnp.where(side_lane == heads + i, lax.broadcast_in_dim(v, side_lane.shape, (0,)), side)
-        rows = mix_weight.shape[0]
+            columns = jnp.where(place == heads + i, lax.broadcast_in_dim(v, columns.shape, (1,)), columns)
         keep, send = call(
-            pack_kernel, 0, [("m", pos), ("w", mix_weight), ("w", side)], [("w", (rows, 896), BF16)] * 2, name="pack",
+            pack_kernel, 0, [("m", pos), ("w", mix_weight), ("w", columns)], [("w", (rows, 896), BF16)] * 2, name="pack",
         )
         pair = join([keep, swap_core(send)], 3)
         line = join([pair] + [xor_with(pair, 8 * m, count) for m in range(1, nz)], 0, after=[unit])
@@ -869,11 +878,11 @@
     tokens = seqs * long
     feats = (seqs, 4, long, 128)
     npack = 2 * seqs + 1
-    attend, fq, fk, fql, fkl, va, ccol, ucol, crow, smid, pack, wmix, vec, vbar = call(
+    attend, fk, fkl, va, ccol, ucol, crow, smid, pack, wmix, vec, vbar = call(
         project_kernel, seqs,
         [("m", pos), ("s", unit)] + [("a", w) for w in w_pieces] + [("w", bias), ("w", maps_pair)],
         [
-            ("s", (seqs, long, width), BF16), ("s", feats, BF16), ("s", feats, BF16), ("s", feats, BF16), ("s", feats, BF16), ("s", feats, BF16),
+            ("s", (seqs, long, width), BF16), ("s", feats, BF16), ("s", feats, BF16), ("s", feats, BF16),
             ("s", (seqs, long, 128), F32), ("s", (seqs, long, 128), F32),
             ("s", (seqs, 2, 8, chunk), F32),
             ("s", (seqs, 4, 128, 128), F32),
@@ -882,24 +891,35 @@
         ],
         scratch=[pltpu.VMEM((nz, 2, 2, 2, 16, 896), BF16), pltpu.SemaphoreType.DMA((4,))], us=12, name="project",
     )
-    if direct:
-        half_z = nz // 2
-        near_shape, far_shape = (3 * nz, *ff_line.shape[1:]), (half_z, *ff_line.shape[1:])
-        ff_near, x_half, y_half = call(
-            near_kernel, 0, [("a", ff_line), ("a", by_x), ("a", by_y), ("d", pack)],
-            [("w", near_shape, BF16), ("w", far_shape, BF16), ("w", far_shape, BF16)],
-            scratch=[pltpu.SemaphoreType.DMA((5,))], name="near",
-        )
     ahead = [(i, i + 2) for i in range(count) if (i % tensor) < 2]
     arrived = lax.ppermute(pack, BOTH, ahead)
+    fq, fql = call(
+        query_kernel, seqs, [("s", attend), ("w", wmix), ("w", maps_pair)], [("s", feats, BF16)] * 2, us=0.3, name="query",
+    )
     (o_loc,) = call(
         local_kernel, seqs,
         [("s", fq), ("s", fk), ("s", fql), ("s", fkl), ("s", va), ("s", ccol), ("s", crow)],
         [("s", feats, F32)], us=0.3, name="local",
     )
+    if direct:
+        half_z = nz // 2
+        far_shape = (half_z, *ff_line.shape[1:])
+        x_half, y_half = call(
+            halves_kernel, 0, [("a", by_x), ("a", by_y), ("d", arrived), ("d", o_loc)], [("w", far_shape, BF16)] * 2,
+            scratch=[pltpu.SemaphoreType.DMA((2,))], us=0.3, name="halves",
+        )
+        near_parts = [ff_line, by_x, by_y]
+        (ff_near,) = call(
+            gather_kernel, 0, [("a", a) for a in near_parts] + [("d", x_half)],
+            [("w", (3 * nz, *ff_line.shape[1:]), BF16)], scratch=[pltpu.SemaphoreType.DMA((3,))], us=0.5, name="near",
+        )
+        before_finish = [x_half]
+    else:
+        before_finish = []
     (inv_root, turn, st, att_keep, att_send) = call(
         finish_kernel, seqs,
-        [("m", pos), ("s", o_loc), ("s", fq), ("s", ccol), ("w", arrived), ("s", smid), ("w", vbar)],
+        [("m", pos), ("s", o_loc), ("s", fq), ("s", ccol), ("w", arrived), ("s", smid), ("w", vbar)]
+        + [("d", a) for a in before_finish],
         [
             ("s", feats, F32), ("s", feats, F32), ("s", (seqs, 4, 2, 128, 128), BF16),
             ("s", (seqs, chunk, width // 2), BF16), ("s", (seqs, chunk, width // 2), BF16),
@@ -938,7 +958,7 @@
             ("w", payload, BF16), rows_full, rows_full, rows_full, rows_low, ("w", (width, own), BF16), rows_low,
             ("w", (width, width), BF16),
         ],
-        scratch=[*work, big], us=10, name="feed_first", limit=24,
+        scratch=[*work, big], us=10, name="feed_first", limit=18,
     )
     g_recv = swap_core(g_send)
     output, grad_middle, ga_keep, ga_send, g_keep, o_keep, o_send, grad_vec = call(
@@ -952,7 +972,7 @@
         scratch=[
             *work, pltpu.VMEM((own, width), BF16), big,
         ],
-        us=10, name="feed_second", limit=24,
+        us=10, name="feed_second", limit=18,
     )
     ga_recv = swap_core(ga_send)
 
@@ -1031,28 +1051,30 @@
         return call(
             input_kernel, seqs,
             [("s", inputs), ("s", grad_middle), ("s", gn_keep), ("s", gn_recv), ("w", vec)] + [("d", a) for a in after],
-            [("s", (seqs, chunk, width), F32)], us=0.3, name="input_grad",
+            [("s", (seqs, chunk, width), F32), ("w", (8, 128), F32)], us=0.3, name="input_grad",
         )
 
     if direct:
         m_plane = call(
-            mix_sum_kernel, 0, [("w", a) for a in m_parts] + [("d", pause([g_line[0]], 40))],
+            mix_sum_kernel, 0, [("w", a) for a in m_parts] + [("d", pause([g_line[0]], 40)), ("d", gn_recv)],
             [("w", (32, 896), BF16)] * nz, us=0.4, name="mix_sum",
         )
-        (input_grad,) = finish_input([m_plane[0]])
+        input_grad, input_done = finish_input([m_plane[0]])
         g_parts = [g_line[0]] + [xor_with(g_line[m], 8 * m, count) for m in range(1, nz)]
-        up_grad, down_grad, out_grad = call(
+        up_grad, down_back, out_grad, feed_done = call(
             feed_last_kernel, 0, [("w", a) for a in g_parts],
-            [("w", a.shape, F32) for a in (up_weight, down_weight, out_weight)], us=0.3, name="feed_last",
-        )
+            [("w", shape, F32) for shape in (up_weight.shape, down_weight.shape[::-1], out_weight.shape, (8, 128))],
+            us=0.3, name="feed_last",
+        )
+        down_grad = down_back.T
         mix_parts = [m_plane[0]] + [xor_with(m_plane[m], 8 * m, count) for m in range(1, nz)]
         m_keep, m_send = call(
-            mix_last_kernel, 0, [("m", pos)] + [("w", a) for a in mix_parts] + [("d", out_grad), ("d", input_grad)],
+            mix_last_kernel, 0, [("m", pos)] + [("w", a) for a in mix_parts] + [("d", feed_done), ("d", input_done)],
             [("w", (mix_weight.shape[0], 896), F32)] * 2, name="mix_last",
         )
         m_recv = swap_core(m_send)
     else:
-        (input_grad,) = finish_input([])
+        input_grad, input_done = finish_input([])
         m_all = jnp.stack(m_pieces).astype(F32).reshape(2, 2, nz, 32, 896)
         mine_rows = m_all.transpose(2, 1, 0, 3, 4).reshape(count, -1, 896)
         keep_part = lax.psum_scatter(mine_rows * jnp.where(first, 1.0, 0.0), BOTH, scatter_dimension=0)
@@ -1060,12 +1082,13 @@
         m_keep = jnp.where(first, keep_part, far_part)
         m_recv = jnp.where(first, far_part, keep_part)
     if direct:
-        mix_grad, gate_grad, bias_grad, *per_row = call(
+        mix_grad, gate_back, bias_grad, *per_row = call(
             final_kernel, 0, [("m", pos), ("w", m_keep), ("w", m_recv)],
-            [("w", mix_weight.shape, F32), ("w", gate_weight.shape, F32), ("w", (heads,), F32)]
+            [("w", mix_weight.shape, F32), ("w", gate_weight.shape[::-1], F32), ("w", (heads,), F32)]
             + [("w", gain_first.shape, F32)] * 4,
             us=1.2, name="final",
         )
+        gate_grad = gate_back.T
     else:
         m_low = jnp.where(first, m_keep, m_recv)
         m_high = jnp.where(first, m_recv, m_keep)

time: 161 us -> 152 us (0.944)
  local copies, waits for them, and re-layouts: 5.84 us -> 1.28 us
  starting transfers between devices: 40.8 us -> 37.4 us
    ppermute x1, waiting for transfers between devices: 4.59 us -> 0.01 us  [body(): arrived = lax.ppermute(pack, BOTH, ahead)]
    unnamed x48 -> x31, local copies, waits for them, and re-layouts: 5.61 us -> 1.06 us
    ppermute x36, waiting for transfers between devices: 31.5 us -> 35.1 us  [xor_with(): return lax.ppermute(a, BOTH, [(i, i ^ mask) for i in range(count)])]
    ppermute x36, starting transfers between devices: 36.1 us -> 33.7 us  [xor_with(): return lax.ppermute(a, BOTH, [(i, i ^ mask) for i in range(count)])]
    pallas_call x25 -> x27, Pallas kernels: 73.6 us -> 73.5 us  [call(): pl.pallas_call(run, in_specs=[spec(kind) for kind in kinds], out_specs=[s...]
  transfers between devices with their start and end apart: 38 -> 38, of which waited for: 17 -> 17; matrix products, arithmetic and copies ran while one was open for 2% -> 1% of each run, Pallas kernels for 38% -> 40%
where the time goes in v3:
time: 152 us
  Pallas kernels  73.5 us (48%)
  starting transfers between devices  37.4 us (25%)
  waiting for transfers between devices  37.3 us (25%)
    pallas_call x27, Pallas kernels, call(): pl.pallas_call(run, in_specs=[spec(kind) for kind in kinds], out_specs=[s...  73.5 us
    ppermute x36, waiting for transfers between devices, xor_with(): return lax.ppermute(a, BOTH, [(i, i ^ mask) for i in range(count)])  35.1 us
    ppermute x36, starting transfers between devices, xor_with(): return lax.ppermute(a, BOTH, [(i, i ^ mask) for i in range(count)])  33.7 us
  transfers between devices with their start and end apart: 38, of which 17 were waited for; matrix products, arithmetic and copies ran while one was open for 1% of the time, Pallas kernels for 40%

profile of v3, /device:TPU:0, one launch (start us, length us, event | category | flops | bytes accessed | tf_op | source)
XLA Modules:
  0.0 151.8 jit_solution(5656604081141345987)
XLA Ops:
  5.4 2.8 %collective-permute-start.2 = (bf16[2,16,896]{2,1,0:T(8,128)(2,1)S(1)}, bf16[2,16,896]{2,1,0:T(8,128)(2,1)S(1)}, u32[]{:S(2)}, u32[]{:S(2)}) collective-permute-start(bf16[2,16,896]{2,1,0:T(8,128)(2,1)S(1)} %join.3.refs_1_), channel_id=1, source_target_pairs={{0,8},{1,9},{2,10},{3,11},{4,12},{5,13},{6,14},{7,15},{8,0},{9,1},... | collective-permute-start | bytes 172040 | tf_op jit(solution)/shard_map/ppermute | solution.py:755
  8.2 2.6 %collective-permute-start.3 = (bf16[2,16,896]{2,1,0:T(8,128)(2,1)S(1)}, bf16[2,16,896]{2,1,0:T(8,128)(2,1)S(1)}, u32[]{:S(2)}, u32[]{:S(2)}) collective-permute-start(bf16[2,16,896]{2,1,0:T(8,128)(2,1)S(1)} %join.3.refs_1_), channel_id=1, source_target_pairs={{0,16},{1,17},{2,18},{3,19},{4,20},{5,21},{6,22},{7,23},{8,24},{9,... | collective-permute-start | bytes 172040 | tf_op jit(solution)/shard_map/ppermute | solution.py:755
  14.7 2.0 %collective-permute-done.4.refs_4_ = bf16[2,16,896]{2,1,0:T(8,128)(2,1)S(1)} collective-permute-done((bf16[2,16,896]{2,1,0:T(8,128)(2,1)S(1)}, bf16[2,16,896]{2,1,0:T(8,128)(2,1)S(1)}, u32[]{:S(2)}, u32[]{:S(2)}) %collective-permute-start.4) | collective-permute-done | bytes 57376 | tf_op jit(solution)/shard_map/ppermute | solution.py:755
  23.7 2.3 %collective-permute-done.10.refs_4_ = bf16[144,512]{1,0:T(8,128)(2,1)S(1)} collective-permute-done((bf16[144,512]{1,0:T(8,128)(2,1)S(1)}, bf16[144,512]{1,0:T(8,128)(2,1)S(1)}, u32[]{:S(2)}, u32[]{:S(2)}) %collective-permute-start.10) | collective-permute-done | bytes 147488 | tf_op jit(solution)/shard_map/ppermute | solution.py:755
  28.0 2.1 %collective-permute-done.8.refs_2_ = bf16[144,512]{1,0:T(8,128)(2,1)S(1)} collective-permute-done((bf16[144,512]{1,0:T(8,128)(2,1)S(1)}, bf16[144,512]{1,0:T(8,128)(2,1)S(1)}, u32[]{:S(2)}, u32[]{:S(2)}) %collective-permute-start.8) | collective-permute-done | bytes 147488 | tf_op jit(solution)/shard_map/ppermute | solution.py:755
  30.1 3.4 %collective-permute-done.9.refs_3_ = bf16[144,512]{1,0:T(8,128)(2,1)S(1)} collective-permute-done((bf16[144,512]{1,0:T(8,128)(2,1)S(1)}, bf16[144,512]{1,0:T(8,128)(2,1)S(1)}, u32[]{:S(2)}, u32[]{:S(2)}) %collective-permute-start.9) | collective-permute-done | bytes 147488 | tf_op jit(solution)/shard_map/ppermute | solution.py:755
  38.0 8.6 %project.1 = (bf16[3,512,512]{2,1,0:T(8,128)(2,1)S(1)}, bf16[3,4,512,128]{3,2,1,0:T(8,128)(2,1)S(1)}, bf16[3,4,512,128]{3,2,1,0:T(8,128)(2,1)S(1)}, bf16[3,4,512...) custom-call(s32[4]{0:T(128)S(1)} %pad_add_fusion.refs_0_, ...), custom_call_target="tpu_custom_call" | custom-call | flops 13799999488 | tf_op jit(solution)/shard_map/project/pallas_call | solution.py:742
  46.7 2.4 %collective-permute-start.13 = (bf16[7,128,128]{2,1,0:T(8,128)(2,1)S(1)}, bf16[7,128,128]{2,1,0:T(8,128)(2,1)S(1)}, u32[]{:S(2)}, u32[]{:S(2)}) collective-permute-start(bf16[7,128,128]{2,1,0:T(8,128)(2,1)S(1)} %get-tuple-element.102), channel_id=1, source_target_pairs={{0,2},{1,3},{4,6},{5,7},{8,10},{9,11},{12,14},{13,15},{16,18},{17,... | collective-permute-start | bytes 688136 | tf_op jit(solution)/shard_map/ppermute | solution.py:895
  49.1 3.5 %query.1 = (bf16[3,4,512,128]{3,2,1,0:T(8,128)(2,1)S(1)}, bf16[3,4,512,128]{3,2,1,0:T(8,128)(2,1)S(1)}) custom-call(bf16[3,512,512]{2,1,0:T(8,128)(2,1)S(1)} %get-tuple-element.103.refs_0_.refs_2_, bf16[512,896]{1,0:T(8,128)(2,1)S(1)} %get-tuple-element.104.refs_1_.refs_14_, bf16[2,128,128]{2,1,0:T(8,128)(2,1)S(1)} %copy.26.refs_7_.refs_2_), custom_call_target="tpu_custom_call" | custom-call | flops 345000000 | tf_op jit(solution)/shard_map/query/pallas_call | solution.py:742
  52.6 3.3 %local.1.refs_3_.refs_1_ = f32[3,4,512,128]{3,2,1,0:T(8,128)S(1)} custom-call(bf16[3,4,512,128]{3,2,1,0:T(8,128)(2,1)S(1)} %get-tuple-element.105.refs_0_.refs_2_.refs_5_.refs_3_, bf16[3,4,512,128]{3,2,1,0:T(8,128)(2,1)S(1)} %get-tuple-element.106.refs_1_.refs_4_, bf16[3,4,512,128]{3,2,1,0:T(8,128)(2,1)S(1)} %get-tuple-element.107.refs_2_, ...), custom_call_target="tpu_custom_call" | custom-call | flops 345000000 | tf_op jit(solution)/shard_map/local/pallas_call | solution.py:742
  57.3 4.1 %finish.1 = (f32[3,4,512,128]{3,2,1,0:T(8,128)S(1)}, f32[3,4,512,128]{3,2,1,0:T(8,128)S(1)}, bf16[3,4,2,128,128]{4,3,2,1,0:T(8,128)(2,1)S(1)}, bf16[3,256,256]{2,1,0:T(8,128)(2,1)S(1)}, bf16[3,256,256]{2,1,0:T(8,128)(2,1)S(1)}) custom-call(s32[4]{0:T(128)S(1)} %pad_add_fusion.refs_0_, f32[3,4,512,128]{3,2,1,0:T(8,128)S(1)} %local.1.refs_3_.refs_1_, ...), custom_call_target="tpu_custom_call" | custom-call | flops 345000000 | tf_op jit(solution)/shard_map/finish/pallas_call | solution.py:742
  61.4 4.6 %collective-permute-done.14.refs_0_ = bf16[2,144,512]{2,1,0:T(8,128)(2,1)S(1)} collective-permute-done((bf16[2,144,512]{2,1,0:T(8,128)(2,1)S(1)}, bf16[2,144,512]{2,1,0:T(8,128)(2,1)S(1)}, u32[]{:S(2)}, u32[]{:S(2)}) %collective-permute-start.14) | collective-permute-done | bytes 294944 | tf_op jit(solution)/shard_map/ppermute | solution.py:755
  66.9 2.1 %collective-permute-done.16.refs_2_ = bf16[3,256,256]{2,1,0:T(8,128)(2,1)S(1)} collective-permute-done((bf16[3,256,256]{2,1,0:T(8,128)(2,1)S(1)}, bf16[3,256,256]{2,1,0:T(8,128)(2,1)S(1)}, u32[]{:S(2)}, u32[]{:S(2)}) %collective-permute-start.16) | collective-permute-done | bytes 393248 | tf_op jit(solution)/shard_map/ppermute | solution.py:755
  69.0 7.9 %feed_first.1 = (bf16[2,2,4,128,512]{4,3,2,1,0:T(8,128)(2,1)S(1)}, f32[768,512]{1,0:T(8,128)S(1)}, f32[768,512]{1,0:T(8,128)S(1)}, f32[768,512]{1,0:T(8,128)S(1)...) custom-call(s32[4]{0:T(128)S(1)} %pad_add_fusion.refs_0_, ...), custom_call_target="tpu_custom_call" | custom-call | flops 11500000256 | tf_op jit(solution)/shard_map/feed_first/pallas_call | solution.py:742
  77.1 9.5 %feed_second.1 = (bf16[3,256,512]{2,1,0:T(8,128)(2,1)}, f32[3,256,512]{2,1,0:T(8,128)S(1)}, bf16[3,256,256]{2,1,0:T(8,128)(2,1)S(1)}, bf16[3,256,256]{2,1,0:T(8,...) custom-call(s32[4]{0:T(128)S(1)} %pad_add_fusion.refs_0_, ...), custom_call_target="tpu_custom_call" | custom-call | flops 11500000256 | tf_op jit(solution)/shard_map/feed_second/pallas_call | solution.py:742
  91.1 5.2 %adjoint.1 = (bf16[3,4,512,128]{3,2,1,0:T(8,128)(2,1)S(1)}, bf16[3,4,512,128]{3,2,1,0:T(8,128)(2,1)S(1)}, f32[3,4,128,128]{3,2,1,0:T(8,128)S(1)}, bf16[7,128,128]{2,1,0:T(8,128)(2,1)S(1)}) custom-call(s32[4]{0:T(128)S(1)} %pad_add_fusion.refs_0_, bf16[3,256,256]{2,1,0:T(8,128)(2,1)S(1)} %get-tuple-element.127.refs_1_, ...), custom_call_target="tpu_custom_call" | custom-call | flops 345000000 | tf_op jit(solution)/shard_map/adjoint/pallas_call | solution.py:742
  97.7 5.3 %local_back.1 = (f32[3,4,512,128]{3,2,1,0:T(8,128)S(1)}, f32[3,4,512,128]{3,2,1,0:T(8,128)S(1)}, f32[3,4,512,128]{3,2,1,0:T(8,128)S(1)}) custom-call(bf16[3,4,512,128]{3,2,1,0:T(8,128)(2,1)S(1)} %get-tuple-element.105.refs_0_.refs_2_.refs_5_.refs_3_, bf16[3,4,512,128]{3,2,1,0:T(8,128)(2,1)S(1)} %get-tuple-element.106.refs_1_.refs_4_, ...), custom_call_target="tpu_custom_call" | custom-call | flops 345000000 | tf_op jit(solution)/shard_map/local_back/pallas_call | solution.py:742
  108.2 2.2 %collective-permute-done.22.refs_11_ = bf16[7,128,128]{2,1,0:T(8,128)(2,1)S(1)} collective-permute-done((bf16[7,128,128]{2,1,0:T(8,128)(2,1)S(1)}, bf16[7,128,128]{2,1,0:T(8,128)(2,1)S(1)}, u32[]{:S(2)}, u32[]{:S(2)}) %collective-permute-start.22) | collective-permute-done | bytes 229408 | tf_op jit(solution)/shard_map/ppermute | solution.py:1016
  110.4 13.5 %close.1 = (bf16[4,32,896]{2,1,0:T(8,128)(2,1)S(1)}, bf16[4,32,896]{2,1,0:T(8,128)(2,1)S(1)}, bf16[4,32,896]{2,1,0:T(8,128)(2,1)S(1)}, bf16[4,32,896]{2,1,0:T(8,...) custom-call(s32[4]{0:T(128)S(1)} %pad_add_fusion.refs_0_, f32[3,512,512]{2,1,0:T(8,128)S(1)} %copy-done.6, ...), custom_call_target="tpu_custom_call" | custom-call | flops 16904999936 | tf_op jit(solution)/shard_map/close/pallas_call | solution.py:742
  127.7 2.3 %collective-permute-done.26.refs_1_ = bf16[4,32,896]{2,1,0:T(8,128)(2,1)S(1)} collective-permute-done((bf16[4,32,896]{2,1,0:T(8,128)(2,1)S(1)}, bf16[4,32,896]{2,1,0:T(8,128)(2,1)S(1)}, u32[]{:S(2)}, u32[]{:S(2)}) %collective-permute-start.26) | collective-permute-done | bytes 229408 | tf_op jit(solution)/shard_map/ppermute | solution.py:755
  130.4 6.0 %collective-permute-done.27.refs_2_ = bf16[4,32,896]{2,1,0:T(8,128)(2,1)S(1)} collective-permute-done((bf16[4,32,896]{2,1,0:T(8,128)(2,1)S(1)}, bf16[4,32,896]{2,1,0:T(8,128)(2,1)S(1)}, u32[]{:S(2)}, u32[]{:S(2)}) %collective-permute-start.27) | collective-permute-done | bytes 229408 | tf_op jit(solution)/shard_map/ppermute | solution.py:755
  138.5 2.6 %collective-permute-start.32 = (bf16[32,896]{1,0:T(8,128)(2,1)S(1)}, bf16[32,896]{1,0:T(8,128)(2,1)S(1)}, u32[]{:S(2)}, u32[]{:S(2)}) collective-permute-start(bf16[32,896]{1,0:T(8,128)(2,1)S(1)} %get-tuple-element.163), channel_id=1, source_target_pairs={{0,16},{1,17},{2,18},{3,19},{4,20},{5,21},{6,22},{7,23},{8,24},{9,... | collective-permute-start | bytes 172040 | tf_op jit(solution)/shard_map/ppermute | solution.py:755
  142.9 2.4 %collective-permute-done.35.refs_2_ = bf16[144,512]{1,0:T(8,128)(2,1)S(1)} collective-permute-done((bf16[144,512]{1,0:T(8,128)(2,1)S(1)}, bf16[144,512]{1,0:T(8,128)(2,1)S(1)}, u32[]{:S(2)}, u32[]{:S(2)}) %collective-permute-start.35) | collective-permute-done | bytes 147488 | tf_op jit(solution)/shard_map/ppermute | solution.py:755
  146.1 2.3 %input_grad.1 = (f32[3,256,512]{2,1,0:T(8,128)}, f32[8,128]{1,0:T(8,128)S(1)}) custom-call(bf16[3,256,512]{2,1,0:T(8,128)(2,1)S(1)} %copy-done.2, f32[3,256,512]{2,1,0:T(8,128)S(1)} %get-tuple-element.126.refs_1_, f32[3,256,512]{2,1,0:T(8,128)S(1)} %get-tuple-element.150.refs_4_.refs_2_, bf16[3,256,512]{2,1,0:T(8,128)(2,1)S(1)} %collective-permute-done.25.refs_5_.refs_3_, ...), custom_call_target="tpu_custom_call" | custom-call | flops 345000000 | tf_op jit(solution)/shard_map/input_grad/pallas_call | solution.py:742
  (126 shorter events, 47.5 us)
Async XLA Ops:
  0.7 10.2 %collective-permute-start = (bf16[3,256,512]{2,1,0:T(8,128)(2,1)}, bf16[3,256,512]{2,1,0:T(8,128)(2,1)S(1)}, u32[]{:S(2)}, u32[]{:S(2)}) collective-permute-start(bf16[3,256,512]{2,1,0:T(8,128)(2,1)} %refs_0_.1), channel_id=1, source_target_pairs={{0,1},{1,0},{2,3},{3,2},{4,5},{5,4},{6,7},{7,6},{8,9},{9,8},{10,11... | collective-permute-start | bytes 2359304 | tf_op jit(solution)/shard_map/ppermute | solution.py:755
  19.8 13.8 %collective-permute-start.5 = (bf16[4,2,16,896]{3,2,1,0:T(8,128)(2,1)S(1)}, bf16[4,2,16,896]{3,2,1,0:T(8,128)(2,1)S(1)}, u32[]{:S(2)}, u32[]{:S(2)}) collective-permute-start(bf16[4,2,16,896]{3,2,1,0:T(8,128)(2,1)S(1)} %join.4.refs_2_.refs_1_.refs_5_), channel_id=1, source_target_pairs={{0,4},{1,5},{2,6},{3,7},{4,0},{5,1},{6,2},{7,3},{8,12},{9,13},{10,... | collective-permute-start | bytes 688136 | tf_op jit(solution)/shard_map/ppermute | solution.py:755
  21.3 12.3 %collective-permute-start.6 = (bf16[4,2,16,896]{3,2,1,0:T(8,128)(2,1)S(1)}, bf16[4,2,16,896]{3,2,1,0:T(8,128)(2,1)S(1)}, u32[]{:S(2)}, u32[]{:S(2)}) collective-permute-start(bf16[4,2,16,896]{3,2,1,0:T(8,128)(2,1)S(1)} %join.4.refs_2_.refs_1_.refs_5_), channel_id=1, source_target_pairs={{0,2},{1,3},{2,0},{3,1},{4,6},{5,7},{6,4},{7,5},{8,10},{9,11},{10,... | collective-permute-start | bytes 688136 | tf_op jit(solution)/shard_map/ppermute | solution.py:755
  22.8 10.8 %collective-permute-start.7 = (bf16[4,2,16,896]{3,2,1,0:T(8,128)(2,1)S(1)}, bf16[4,2,16,896]{3,2,1,0:T(8,128)(2,1)S(1)}, u32[]{:S(2)}, u32[]{:S(2)}) collective-permute-start(bf16[4,2,16,896]{3,2,1,0:T(8,128)(2,1)S(1)} %join.4.refs_2_.refs_1_.refs_5_), channel_id=1, source_target_pairs={{0,6},{1,7},{2,4},{3,5},{4,2},{5,3},{6,0},{7,1},{8,14},{9,15},{10,... | collective-permute-start | bytes 688136 | tf_op jit(solution)/shard_map/ppermute | solution.py:755
  34.9 21.0 %collective-permute-start.11 = (bf16[4,144,512]{2,1,0:T(8,128)(2,1)S(1)}, bf16[4,144,512]{2,1,0:T(8,128)(2,1)S(1)}, u32[]{:S(2)}, u32[]{:S(2)}) collective-permute-start(bf16[4,144,512]{2,1,0:T(8,128)(2,1)S(1)} %join.5.refs_0_), channel_id=1, source_target_pairs={{0,4},{1,5},{2,6},{3,7},{4,0},{5,1},{6,2},{7,3},{8,12},{9,13},{10,... | collective-permute-start | bytes 1769480 | tf_op jit(solution)/shard_map/ppermute | solution.py:755
  36.5 19.4 %collective-permute-start.12 = (bf16[4,144,512]{2,1,0:T(8,128)(2,1)S(1)}, bf16[4,144,512]{2,1,0:T(8,128)(2,1)S(1)}, u32[]{:S(2)}, u32[]{:S(2)}) collective-permute-start(bf16[4,144,512]{2,1,0:T(8,128)(2,1)S(1)} %join.5.refs_0_), channel_id=1, source_target_pairs={{0,2},{1,3},{2,0},{3,1},{4,6},{5,7},{6,4},{7,5},{8,10},{9,11},{10,... | collective-permute-start | bytes 1769480 | tf_op jit(solution)/shard_map/ppermute | solution.py:755
  46.7 9.2 %collective-permute-start.13 = (bf16[7,128,128]{2,1,0:T(8,128)(2,1)S(1)}, bf16[7,128,128]{2,1,0:T(8,128)(2,1)S(1)}, u32[]{:S(2)}, u32[]{:S(2)}) collective-permute-start(bf16[7,128,128]{2,1,0:T(8,128)(2,1)S(1)} %get-tuple-element.102), channel_id=1, source_target_pairs={{0,2},{1,3},{4,6},{5,7},{8,10},{9,11},{12,14},{13,15},{16,18},{17,... | collective-permute-start | bytes 688136 | tf_op jit(solution)/shard_map/ppermute | solution.py:895
  56.5 12.5 %collective-permute-start.17 = (bf16[12,144,512]{2,1,0:T(8,128)(2,1)S(1)}, bf16[12,144,512]{2,1,0:T(8,128)(2,1)S(1)}, u32[]{:S(2)}, u32[]{:S(2)}) collective-permute-start(bf16[12,144,512]{2,1,0:T(8,128)(2,1)S(1)} %near.1.refs_7_.refs_4_), channel_id=1, source_target_pairs={{0,1},{1,0},{2,3},{3,2},{4,5},{5,4},{6,7},{7,6},{8,9},{9,8},{10,11... | collective-permute-start | bytes 5308424 | tf_op jit(solution)/shard_map/ppermute | solution.py:755
  56.6 9.4 %collective-permute-start.14 = (bf16[2,144,512]{2,1,0:T(8,128)(2,1)S(1)}, bf16[2,144,512]{2,1,0:T(8,128)(2,1)S(1)}, u32[]{:S(2)}, u32[]{:S(2)}) collective-permute-start(bf16[2,144,512]{2,1,0:T(8,128)(2,1)S(1)} %get-tuple-element.112.refs_3_.refs_7_), channel_id=1, source_target_pairs={{0,2},{1,3},{2,0},{3,1},{4,6},{5,7},{6,4},{7,5},{8,10},{9,11},{10,... | collective-permute-start | bytes 884744 | tf_op jit(solution)/shard_map/ppermute | solution.py:755
  56.7 9.3 %collective-permute-start.15 = (bf16[2,144,512]{2,1,0:T(8,128)(2,1)S(1)}, bf16[2,144,512]{2,1,0:T(8,128)(2,1)S(1)}, u32[]{:S(2)}, u32[]{:S(2)}) collective-permute-start(bf16[2,144,512]{2,1,0:T(8,128)(2,1)S(1)} %get-tuple-element.113), channel_id=1, source_target_pairs={{0,4},{1,5},{2,6},{3,7},{4,0},{5,1},{6,2},{7,3},{8,12},{9,13},{10,... | collective-permute-start | bytes 884744 | tf_op jit(solution)/shard_map/ppermute | solution.py:755
  76.9 11.3 %collective-permute-start.20 = (bf16[2,2,4,128,512]{4,3,2,1,0:T(8,128)(2,1)S(1)}, bf16[2,2,4,128,512]{4,3,2,1,0:T(8,128)(2,1)S(1)}, u32[]{:S(2)}, u32[]{:S(2)}) collective-permute-start(bf16[2,2,4,128,512]{4,3,2,1,0:T(8,128)(2,1)S(1)} %get-tuple-element.132), channel_id=1, source_target_pairs={{0,1},{1,0},{2,3},{3,2},{4,5},{5,4},{6,7},{7,6},{8,9},{9,8},{10,11... | collective-permute-start | bytes 6291464 | tf_op jit(solution)/shard_map/ppermute | solution.py:755
  88.7 15.7 %collective-permute-start.23 = (bf16[2,2,144,512]{3,2,1,0:T(8,128)(2,1)S(1)}, bf16[2,2,144,512]{3,2,1,0:T(8,128)(2,1)S(1)}, u32[]{:S(2)}, u32[]{:S(2)}) collective-permute-start(bf16[2,2,144,512]{3,2,1,0:T(8,128)(2,1)S(1)} %get-tuple-element.146), channel_id=1, source_target_pairs={{0,4},{1,5},{2,6},{3,7},{4,0},{5,1},{6,2},{7,3},{8,12},{9,13},{10,... | collective-permute-start | bytes 1769480 | tf_op jit(solution)/shard_map/ppermute | solution.py:755
  89.3 16.2 %collective-permute-start.24 = (bf16[2,2,144,512]{3,2,1,0:T(8,128)(2,1)S(1)}, bf16[2,2,144,512]{3,2,1,0:T(8,128)(2,1)S(1)}, u32[]{:S(2)}, u32[]{:S(2)}) collective-permute-start(bf16[2,2,144,512]{3,2,1,0:T(8,128)(2,1)S(1)} %get-tuple-element.148), channel_id=1, source_target_pairs={{0,2},{1,3},{2,0},{3,1},{4,6},{5,7},{6,4},{7,5},{8,10},{9,11},{10,... | collective-permute-start | bytes 1769480 | tf_op jit(solution)/shard_map/ppermute | solution.py:755
  96.3 14.1 %collective-permute-start.22 = (bf16[7,128,128]{2,1,0:T(8,128)(2,1)S(1)}, bf16[7,128,128]{2,1,0:T(8,128)(2,1)S(1)}, u32[]{:S(2)}, u32[]{:S(2)}) collective-permute-start(bf16[7,128,128]{2,1,0:T(8,128)(2,1)S(1)} %get-tuple-element.143), channel_id=1, source_target_pairs={{2,0},{3,1},{6,4},{7,5},{10,8},{11,9},{14,12},{15,13},{18,16},{19,... | collective-permute-start | bytes 688136 | tf_op jit(solution)/shard_map/ppermute | solution.py:1016
  105.8 19.7 %collective-permute-start.29 = (bf16[2,144,512]{2,1,0:T(8,128)(2,1)S(1)}, bf16[2,144,512]{2,1,0:T(8,128)(2,1)S(1)}, u32[]{:S(2)}, u32[]{:S(2)}) collective-permute-start(bf16[2,144,512]{2,1,0:T(8,128)(2,1)S(1)} %get-tuple-element.156), channel_id=1, source_target_pairs={{0,2},{1,3},{2,0},{3,1},{4,6},{5,7},{6,4},{7,5},{8,10},{9,11},{10,... | collective-permute-start | bytes 884744 | tf_op jit(solution)/shard_map/ppermute | solution.py:755
  106.7 20.8 %collective-permute-start.30 = (bf16[2,144,512]{2,1,0:T(8,128)(2,1)S(1)}, bf16[2,144,512]{2,1,0:T(8,128)(2,1)S(1)}, u32[]{:S(2)}, u32[]{:S(2)}) collective-permute-start(bf16[2,144,512]{2,1,0:T(8,128)(2,1)S(1)} %get-tuple-element.158), channel_id=1, source_target_pairs={{0,4},{1,5},{2,6},{3,7},{4,0},{5,1},{6,2},{7,3},{8,12},{9,13},{10,... | collective-permute-start | bytes 884744 | tf_op jit(solution)/shard_map/ppermute | solution.py:755
  125.5 10.9 %collective-permute-start.27 = (bf16[4,32,896]{2,1,0:T(8,128)(2,1)S(1)}, bf16[4,32,896]{2,1,0:T(8,128)(2,1)S(1)}, u32[]{:S(2)}, u32[]{:S(2)}) collective-permute-start(bf16[4,32,896]{2,1,0:T(8,128)(2,1)S(1)} %get-tuple-element.154), channel_id=1, source_target_pairs={{0,2},{1,3},{2,0},{3,1},{4,6},{5,7},{6,4},{7,5},{8,10},{9,11},{10,... | collective-permute-start | bytes 688136 | tf_op jit(solution)/shard_map/ppermute | solution.py:755
  125.5 12.8 %collective-permute-start.25 = (bf16[3,256,512]{2,1,0:T(8,128)(2,1)S(1)}, bf16[3,256,512]{2,1,0:T(8,128)(2,1)S(1)}, u32[]{:S(2)}, u32[]{:S(2)}) collective-permute-start(bf16[3,256,512]{2,1,0:T(8,128)(2,1)S(1)} %get-tuple-element.151), channel_id=1, source_target_pairs={{0,1},{1,0},{2,3},{3,2},{4,5},{5,4},{6,7},{7,6},{8,9},{9,8},{10,11... | collective-permute-start | bytes 2359304 | tf_op jit(solution)/shard_map/ppermute | solution.py:755
  125.5 12.7 %collective-permute-start.28 = (bf16[4,32,896]{2,1,0:T(8,128)(2,1)S(1)}, bf16[4,32,896]{2,1,0:T(8,128)(2,1)S(1)}, u32[]{:S(2)}, u32[]{:S(2)}) collective-permute-start(bf16[4,32,896]{2,1,0:T(8,128)(2,1)S(1)} %get-tuple-element.155), channel_id=1, source_target_pairs={{0,6},{1,7},{2,4},{3,5},{4,2},{5,3},{6,0},{7,1},{8,14},{9,15},{10,... | collective-permute-start | bytes 688136 | tf_op jit(solution)/shard_map/ppermute | solution.py:755
  127.7 13.4 %collective-permute-start.34 = (bf16[144,512]{1,0:T(8,128)(2,1)S(1)}, bf16[144,512]{1,0:T(8,128)(2,1)S(1)}, u32[]{:S(2)}, u32[]{:S(2)}) collective-permute-start(bf16[144,512]{1,0:T(8,128)(2,1)S(1)} %get-tuple-element.165), channel_id=1, source_target_pairs={{0,8},{1,9},{2,10},{3,11},{4,12},{5,13},{6,14},{7,15},{8,0},{9,1},... | collective-permute-start | bytes 442376 | tf_op jit(solution)/shard_map/ppermute | solution.py:755
  130.0 15.3 %collective-permute-start.35 = (bf16[144,512]{1,0:T(8,128)(2,1)S(1)}, bf16[144,512]{1,0:T(8,128)(2,1)S(1)}, u32[]{:S(2)}, u32[]{:S(2)}) collective-permute-start(bf16[144,512]{1,0:T(8,128)(2,1)S(1)} %get-tuple-element.166), channel_id=1, source_target_pairs={{0,16},{1,17},{2,18},{3,19},{4,20},{5,21},{6,22},{7,23},{8,24},{9,... | collective-permute-start | bytes 442376 | tf_op jit(solution)/shard_map/ppermute | solution.py:755
  136.5 8.9 %collective-permute-start.36 = (bf16[144,512]{1,0:T(8,128)(2,1)S(1)}, bf16[144,512]{1,0:T(8,128)(2,1)S(1)}, u32[]{:S(2)}, u32[]{:S(2)}) collective-permute-start(bf16[144,512]{1,0:T(8,128)(2,1)S(1)} %get-tuple-element.167), channel_id=1, source_target_pairs={{0,24},{1,25},{2,26},{3,27},{4,28},{5,29},{6,30},{7,31},{8,16},{9,... | collective-permute-start | bytes 442376 | tf_op jit(solution)/shard_map/ppermute | solution.py:755
  138.4 9.9 %collective-permute-start.31 = (bf16[32,896]{1,0:T(8,128)(2,1)S(1)}, bf16[32,896]{1,0:T(8,128)(2,1)S(1)}, u32[]{:S(2)}, u32[]{:S(2)}) collective-permute-start(bf16[32,896]{1,0:T(8,128)(2,1)S(1)} %get-tuple-element.162), channel_id=1, source_target_pairs={{0,8},{1,9},{2,10},{3,11},{4,12},{5,13},{6,14},{7,15},{8,0},{9,1},... | collective-permute-start | bytes 172040 | tf_op jit(solution)/shard_map/ppermute | solution.py:755
  138.5 10.1 %collective-permute-start.32 = (bf16[32,896]{1,0:T(8,128)(2,1)S(1)}, bf16[32,896]{1,0:T(8,128)(2,1)S(1)}, u32[]{:S(2)}, u32[]{:S(2)}) collective-permute-start(bf16[32,896]{1,0:T(8,128)(2,1)S(1)} %get-tuple-element.163), channel_id=1, source_target_pairs={{0,16},{1,17},{2,18},{3,19},{4,20},{5,21},{6,22},{7,23},{8,24},{9,... | collective-permute-start | bytes 172040 | tf_op jit(solution)/shard_map/ppermute | solution.py:755
  (29 other events, 136.3 us)
